TPU v7x, 32 devices: a whole 2x2x4 slice. The times are simulated.
32 devices in a mesh: path: 4 (over y, x), dev: 8 (over z, core).
Axes of the slice: x: 2, y: 2, z: 4, core: 2. Of those that a mesh axis runs over, the one named last changes fastest.
Arguments:
- inputs: bfloat16 [32, 144, 1024], P(('path', 'dev')), may hold values from -6 to 6
- hires_maps: bfloat16 [32, 24, 24, 1536], P(('path', 'dev')), may hold values from -6 to 6
- target_path: int32 [4, 8], P('path', 'dev'), may hold values from 0 to 3, as said below
- cotangent: bfloat16 [32, 144, 1024], P(('path', 'dev')), may hold values from -6 to 6
- attn_gain: float32 [1024], replicated, may hold values from 0.5 to 1.5
- w_qkv: bfloat16 [1024, 3072], P('dev'), may hold values from -0.1875 to 0.1875
- w_out: bfloat16 [1024, 1024], P('dev'), may hold values from -0.5 to 0.5
- mlp_gain: float32 [1024], replicated, may hold values from 0.5 to 1.5
- w_fc1: bfloat16 [1024, 4096], P('dev'), may hold values from -0.1875 to 0.1875
- w_fc2: bfloat16 [4096, 1024], P('dev'), may hold values from -0.09375 to 0.09375
- w_adapter: bfloat16 [1536, 1024], P('dev'), may hold values from -0.15625 to 0.15625
- adapter_kernel: float32 [9, 1024], replicated, may hold values from -3 to 3
- merge_gate: float32 [1024], replicated, may hold values from 0.5 to 1.5
- section_kernel: float32 [49, 1536], replicated, may hold values from -1 to 1
- section_gain: float32 [1536], replicated, may hold values from 0.5 to 1.5
- w_expand: bfloat16 [1536, 6144], P('dev'), may hold values from -0.15625 to 0.15625
- w_reduce: bfloat16 [6144, 1536], P('dev'), may hold values from -0.078125 to 0.078125
- layer_scale: float32 [1536], replicated, may hold values from 0.5 to 1
Outputs:
- output: bfloat16 [32, 144, 1024], P(('path', 'dev'))
- grad_inputs: float32 [32, 144, 1024], P(('path', 'dev'))
- grad_hires_maps: float32 [32, 24, 24, 1536], P(('path', 'dev'))
- grad_attn_gain: float32 [1024], replicated
- grad_w_qkv: float32 [1024, 3072], P('dev')
- grad_w_out: float32 [1024, 1024], P('dev')
- grad_mlp_gain: float32 [1024], replicated
- grad_w_fc1: float32 [1024, 4096], P('dev')
- grad_w_fc2: float32 [4096, 1024], P('dev')
- grad_w_adapter: float32 [1536, 1024], P('dev')
- grad_adapter_kernel: float32 [9, 1024], replicated
- grad_merge_gate: float32 [1024], replicated
- grad_section_kernel: float32 [49, 1536], replicated
- grad_section_gain: float32 [1536], replicated
- grad_w_expand: float32 [1536, 6144], P('dev')
- grad_w_reduce: float32 [6144, 1536], P('dev')
- grad_layer_scale: float32 [1536], replicated
Inputs may be any that keep to these rules, and one draw needn't show every extreme that they name: For every d, the column target_path[:, d] is a permutation of 0 to 3.
All inputs are finite; a program needn't handle non-finite values.
Results may differ from a plain program's by a relative error of at most 0.02.
Values may be sent and summed in bfloat16 or wider, within the bound.
A program may use at most 512 MiB of HBM per device.

v0:
```python
import jax
import jax.numpy as jnp
from jax import lax
from jax.sharding import PartitionSpec as P

HEAD_DIM = 64


def layer_norm(values, gain_vec):
    centred = values - jnp.mean(values, axis=-1, keepdims=True)
    spread = jnp.mean(centred * centred, axis=-1, keepdims=True)
    return centred * lax.rsqrt(spread + 1e-06) * gain_vec


def depthwise(feature_map, taps_table, kernel_side):
    half_side = kernel_side // 2
    padded = jnp.pad(feature_map, ((0, 0), (half_side, half_side), (half_side, half_side), (0, 0)))
    map_side = feature_map.shape[1]
    accum_sum = jnp.zeros(feature_map.shape, feature_map.dtype)
    for offset_row in range(kernel_side):
        for offset_col in range(kernel_side):
            window = padded[
                :, offset_row : offset_row + map_side, offset_col : offset_col + map_side, :
            ]
            accum_sum = accum_sum + window * taps_table[offset_row * kernel_side + offset_col]
    return accum_sum


def section_depthwise(grid_field, grid_kernel):
    return depthwise(grid_field, grid_kernel, 7)


def adapter_depthwise(grid_field, grid_kernel):
    return depthwise(grid_field, grid_kernel, 3)


def local(
    inputs,
    hires_maps,
    target_path,
    cotangent,
    attn_gain,
    w_qkv,
    w_out,
    mlp_gain,
    w_fc1,
    w_fc2,
    w_adapter,
    adapter_kernel,
    merge_gate,
    section_kernel,
    section_gain,
    w_expand,
    w_reduce,
    layer_scale,
):
    gathered = (
        lax.all_gather(w_qkv, "dev", axis=0, tiled=True),
        lax.all_gather(w_out, "dev", axis=0, tiled=True),
        lax.all_gather(w_fc1, "dev", axis=0, tiled=True),
        lax.all_gather(w_fc2, "dev", axis=0, tiled=True),
        lax.all_gather(w_adapter, "dev", axis=0, tiled=True),
        lax.all_gather(w_expand, "dev", axis=0, tiled=True),
        lax.all_gather(w_reduce, "dev", axis=0, tiled=True),
    )
    full_qkv, full_out, full_fc1, full_fc2, full_adapter, full_expand, full_reduce = gathered
    path_count = lax.axis_size("path")
    maps_float = hires_maps.astype(jnp.float32)
    map_side = maps_float.shape[1]
    channels = maps_float.shape[3]
    grid_side = map_side // 2
    tokens = grid_side * grid_side
    quarter_rows = tokens // path_count
    model_width = inputs.shape[2]
    head_count = model_width // HEAD_DIM
    score_scale = HEAD_DIM ** (-0.5)
    section_mixed, section_back = jax.vjp(section_depthwise, maps_float, section_kernel)
    section_normed, section_norm_back = jax.vjp(layer_norm, section_mixed, section_gain)
    section_rows = section_normed.reshape(-1, channels).astype(jnp.bfloat16)
    expanded = jnp.dot(section_rows, full_expand, preferred_element_type=jnp.float32)
    activated, section_gelu_back = jax.vjp(jax.nn.gelu, expanded)
    activated_low = activated.astype(jnp.bfloat16)
    reduced = jnp.dot(activated_low, full_reduce, preferred_element_type=jnp.float32).reshape(
        maps_float.shape
    )
    section_out = maps_float + layer_scale * reduced
    pooled = jnp.mean(
        section_out.reshape(grid_side, 2, grid_side, 2, channels), axis=(1, 3)
    ).reshape(tokens, channels)
    pieces = pooled.astype(jnp.bfloat16).reshape(path_count, quarter_rows, channels)
    own_target = jnp.broadcast_to(target_path, (path_count, 1))
    spread_pieces, spread_targets = (
        lax.all_to_all(pieces, "path", split_axis=0, concat_axis=0, tiled=True),
        lax.all_to_all(own_target, "path", split_axis=0, concat_axis=0, tiled=True),
    )
    selector = (
        jnp.arange(path_count, dtype=jnp.int32)[:, None] == spread_targets.reshape(1, path_count)
    ).astype(jnp.float32)
    routed = jnp.einsum("pq,qtc->ptc", selector, spread_pieces.astype(jnp.float32)).astype(
        jnp.bfloat16
    )
    arrived = lax.all_to_all(routed, "path", split_axis=0, concat_axis=0, tiled=True)
    features = arrived.reshape(tokens, channels)
    adapted = jnp.dot(features, full_adapter, preferred_element_type=jnp.float32)
    spread_map, adapter_back = jax.vjp(
        adapter_depthwise, adapted.reshape(1, grid_side, grid_side, model_width), adapter_kernel
    )
    spread_rows = spread_map.reshape(tokens, model_width)
    gate_factor = jnp.tanh(merge_gate)
    hidden_in = inputs[0].astype(jnp.float32) + gate_factor * spread_rows
    normed_one, norm_one_back = jax.vjp(layer_norm, hidden_in, attn_gain)
    attn_rows = normed_one.astype(jnp.bfloat16)
    projected = jnp.dot(attn_rows, full_qkv, preferred_element_type=jnp.float32).astype(
        jnp.bfloat16
    )
    queries = projected[:, :model_width].reshape(tokens, head_count, HEAD_DIM)
    key_rows = projected[:, model_width : 2 * model_width].reshape(tokens, head_count, HEAD_DIM)
    values = projected[:, 2 * model_width :].reshape(tokens, head_count, HEAD_DIM)
    scores = (
        jnp.einsum("thd,shd->hts", queries, key_rows, preferred_element_type=jnp.float32)
        * score_scale
    )
    probs = jax.nn.softmax(scores, axis=-1)
    probs_low = probs.astype(jnp.bfloat16)
    attn_mixed = jnp.einsum("hts,shd->thd", probs_low, values, preferred_element_type=jnp.float32)
    attn_mixed = attn_mixed.astype(jnp.bfloat16).reshape(tokens, model_width)
    attended = jnp.dot(attn_mixed, full_out, preferred_element_type=jnp.float32)
    hidden_mid = hidden_in + attended
    normed_two, norm_two_back = jax.vjp(layer_norm, hidden_mid, mlp_gain)
    mlp_rows = normed_two.astype(jnp.bfloat16)
    raised = jnp.dot(mlp_rows, full_fc1, preferred_element_type=jnp.float32)
    lifted_value, gelu_back = jax.vjp(jax.nn.gelu, raised)
    lifted = lifted_value.astype(jnp.bfloat16)
    lowered = jnp.dot(lifted, full_fc2, preferred_element_type=jnp.float32)
    result = (hidden_mid + lowered)[None].astype(jnp.bfloat16)
    grad_out = cotangent[0].astype(jnp.float32)
    grad_out_low = grad_out.astype(jnp.bfloat16)
    grad_fc2_w = jnp.dot(lifted.T, grad_out_low, preferred_element_type=jnp.float32)
    grad_lifted = jnp.dot(grad_out_low, full_fc2.T, preferred_element_type=jnp.float32)
    grad_raised = gelu_back(grad_lifted)[0].astype(jnp.bfloat16)
    grad_fc1_w = jnp.dot(mlp_rows.T, grad_raised, preferred_element_type=jnp.float32)
    grad_normed_two = jnp.dot(grad_raised, full_fc1.T, preferred_element_type=jnp.float32)
    grad_mid_norm, grad_mlp_gain = norm_two_back(grad_normed_two)
    grad_mid = grad_out + grad_mid_norm
    grad_attended = grad_mid.astype(jnp.bfloat16)
    grad_out_w = jnp.dot(attn_mixed.T, grad_attended, preferred_element_type=jnp.float32)
    grad_mixed = jnp.dot(grad_attended, full_out.T, preferred_element_type=jnp.float32)
    grad_mixed = grad_mixed.astype(jnp.bfloat16).reshape(tokens, head_count, HEAD_DIM)
    grad_probs = jnp.einsum("thd,shd->hts", grad_mixed, values, preferred_element_type=jnp.float32)
    grad_values = jnp.einsum(
        "hts,thd->shd", probs_low, grad_mixed, preferred_element_type=jnp.float32
    )
    grad_scores = probs * (grad_probs - jnp.sum(grad_probs * probs, axis=-1, keepdims=True))
    grad_scores = grad_scores.astype(jnp.bfloat16)
    grad_queries = (
        jnp.einsum("hts,shd->thd", grad_scores, key_rows, preferred_element_type=jnp.float32)
        * score_scale
    )
    grad_keys = (
        jnp.einsum("hts,thd->shd", grad_scores, queries, preferred_element_type=jnp.float32)
        * score_scale
    )
    grad_projected = jnp.concatenate(
        [
            grad_queries.reshape(tokens, model_width),
            grad_keys.reshape(tokens, model_width),
            grad_values.reshape(tokens, model_width),
        ],
        axis=1,
    ).astype(jnp.bfloat16)
    grad_qkv_w = jnp.dot(attn_rows.T, grad_projected, preferred_element_type=jnp.float32)
    grad_normed_one = jnp.dot(grad_projected, full_qkv.T, preferred_element_type=jnp.float32)
    grad_in_norm, grad_attn_gain = norm_one_back(grad_normed_one)
    grad_in = grad_mid + grad_in_norm
    grad_merge = jnp.sum(grad_in * spread_rows, axis=0) * (1.0 - gate_factor * gate_factor)
    grad_spread = (grad_in * gate_factor).reshape(1, grid_side, grid_side, model_width)
    grad_adapted, grad_adapter_taps = adapter_back(grad_spread)
    grad_adapted_low = grad_adapted.reshape(tokens, model_width).astype(jnp.bfloat16)
    grad_adapter_w = jnp.dot(features.T, grad_adapted_low, preferred_element_type=jnp.float32)
    grad_features = jnp.dot(grad_adapted_low, full_adapter.T, preferred_element_type=jnp.float32)
    grad_pieces = grad_features.astype(jnp.bfloat16).reshape(path_count, quarter_rows, channels)
    grad_routed = lax.all_to_all(grad_pieces, "path", split_axis=0, concat_axis=0, tiled=True)
    grad_unrouted = jnp.einsum("pq,ptc->qtc", selector, grad_routed.astype(jnp.float32)).astype(
        jnp.bfloat16
    )
    grad_home = lax.all_to_all(grad_unrouted, "path", split_axis=0, concat_axis=0, tiled=True)
    grad_pooled = grad_home.astype(jnp.float32).reshape(tokens, channels)
    quarter = (grad_pooled * 0.25).reshape(1, grid_side, 1, grid_side, 1, channels)
    grad_section_out = jnp.broadcast_to(quarter, (1, grid_side, 2, grid_side, 2, channels)).reshape(
        maps_float.shape
    )
    grad_scale = jnp.sum((grad_section_out * reduced).reshape(-1, channels), axis=0)
    grad_reduced = (grad_section_out * layer_scale).reshape(-1, channels).astype(jnp.bfloat16)
    grad_reduce_w = jnp.dot(activated_low.T, grad_reduced, preferred_element_type=jnp.float32)
    grad_activated = jnp.dot(grad_reduced, full_reduce.T, preferred_element_type=jnp.float32)
    grad_expanded = section_gelu_back(grad_activated)[0].astype(jnp.bfloat16)
    grad_expand_w = jnp.dot(section_rows.T, grad_expanded, preferred_element_type=jnp.float32)
    grad_section_normed = jnp.dot(
        grad_expanded, full_expand.T, preferred_element_type=jnp.float32
    ).reshape(maps_float.shape)
    grad_section_mixed, grad_section_gain = section_norm_back(grad_section_normed)
    grad_maps_conv, grad_section_taps = section_back(grad_section_mixed)
    grad_maps = grad_section_out + grad_maps_conv
    shares = (
        lax.psum_scatter(grad_qkv_w, "dev", scatter_dimension=0, tiled=True),
        lax.psum_scatter(grad_out_w, "dev", scatter_dimension=0, tiled=True),
        lax.psum_scatter(grad_fc1_w, "dev", scatter_dimension=0, tiled=True),
        lax.psum_scatter(grad_fc2_w, "dev", scatter_dimension=0, tiled=True),
        lax.psum_scatter(grad_adapter_w, "dev", scatter_dimension=0, tiled=True),
        lax.psum_scatter(grad_expand_w, "dev", scatter_dimension=0, tiled=True),
        lax.psum_scatter(grad_reduce_w, "dev", scatter_dimension=0, tiled=True),
    )
    summed = (
        lax.psum(shares[0].astype(jnp.bfloat16), "path").astype(jnp.float32),
        lax.psum(shares[1].astype(jnp.bfloat16), "path").astype(jnp.float32),
        lax.psum(shares[2].astype(jnp.bfloat16), "path").astype(jnp.float32),
        lax.psum(shares[3].astype(jnp.bfloat16), "path").astype(jnp.float32),
        lax.psum(shares[4].astype(jnp.bfloat16), "path").astype(jnp.float32),
        lax.psum(shares[5].astype(jnp.bfloat16), "path").astype(jnp.float32),
        lax.psum(shares[6].astype(jnp.bfloat16), "path").astype(jnp.float32),
    )
    small_sums = lax.psum(
        (
            grad_attn_gain,
            grad_mlp_gain,
            grad_merge,
            grad_adapter_taps,
            grad_section_gain,
            grad_section_taps,
            grad_scale,
        ),
        ("path", "dev"),
    )
    return (
        result,
        grad_in[None],
        grad_maps,
        small_sums[0],
        summed[0],
        summed[1],
        small_sums[1],
        summed[2],
        summed[3],
        summed[4],
        small_sums[3],
        small_sums[2],
        small_sums[5],
        small_sums[4],
        summed[5],
        summed[6],
        small_sums[6],
    )


def solution(mesh):
    return jax.shard_map(
        local,
        mesh=mesh,
        in_specs=(
            P(("path", "dev"), None, None),
            P(("path", "dev"), None, None, None),
            P("path", "dev"),
            P(("path", "dev"), None, None),
            P(),
            P("dev", None),
            P("dev", None),
            P(),
            P("dev", None),
            P("dev", None),
            P("dev", None),
            P(),
            P(),
            P(),
            P(),
            P("dev", None),
            P("dev", None),
            P(),
        ),
        out_specs=(
            P(("path", "dev"), None, None),
            P(("path", "dev"), None, None),
            P(("path", "dev"), None, None, None),
            P(),
            P("dev", None),
            P("dev", None),
            P(),
            P("dev", None),
            P("dev", None),
            P("dev", None),
            P(),
            P(),
            P(),
            P(),
            P("dev", None),
            P("dev", None),
            P(),
        ),
        check_vma=False,
    )
```

profile of v0, /device:TPU:0, one launch (start us, length us, event | category | flops | bytes accessed | tf_op | source)
XLA Modules:
  0.0 2298.7 jit_solution(2663218305208189188)
XLA Ops:
  23.1 90.1 %fusion.60 = (f32[24,24]{1,0:T(8,128)}, f32[1,24,24,1536]{3,2,1,0:T(8,128)S(1)}) fusion(f32[1536]{0:T(1024)} %get-tuple-element.127, f32[1536]{0:T(1024)} %get-tuple-element.128, f32[1536]{0:T(1024)} %get-tuple-element.81, f32[1536]{0:T(1024)} %get-tuple-element.82, f32[1536]{0:T(1024)} %get-tuple-element.83, f32[1536]{0:T(1024)} %get-tuple-element.84, ...), kind=kLoop, calls=%fused_computation.355 | loop fusion | flops 86703552 | bytes 7381248 | tf_op jit(solution)/shard_map/jvp()/reduce_sum | solution.py:10
  117.5 63.2 %all-gather.8.cloned.1.call-done = bf16[1536,6144]{1,0:T(8,128)(2,1)} async-done(((bf16[192,6144]{1,0:T(8,128)(2,1)}), bf16[1536,6144]{1,0:T(8,128)(2,1)}) %all-gather.8.cloned.1.call-update) | async-done | bytes 18874384 | tf_op jit(solution)/shard_map/all_gather | solution.py:63
  180.7 18.3 fusion.65
  199.0 149.8 %all-gather.10.cloned.1.call-done = bf16[6144,1536]{1,0:T(8,128)(2,1)} async-done(((bf16[768,1536]{1,0:T(8,128)(2,1)}), bf16[6144,1536]{1,0:T(8,128)(2,1)}) %all-gather.10.cloned.1.call-update) | async-done | bytes 18874384 | tf_op jit(solution)/shard_map/all_gather | solution.py:64
  348.9 20.6 fusion.56
  412.9 39.2 %all-gather.14.cloned.1.call-done = bf16[1024,3072]{1,0:T(8,128)(2,1)} async-done(((bf16[128,3072]{1,0:T(8,128)(2,1)}), bf16[1024,3072]{1,0:T(8,128)(2,1)}) %all-gather.14.cloned.1.call-update) | async-done | bytes 6291472 | tf_op jit(solution)/shard_map/all_gather | solution.py:58
  484.6 79.8 %all-gather.18.cloned.1.call-done = bf16[1024,4096]{1,0:T(8,128)(2,1)} async-done(((bf16[128,4096]{1,0:T(8,128)(2,1)}), bf16[1024,4096]{1,0:T(8,128)(2,1)}) %all-gather.18.cloned.1.call-update) | async-done | bytes 8388624 | tf_op jit(solution)/shard_map/all_gather | solution.py:60
  569.3 77.3 %all-gather.20.cloned.1.call-done = bf16[4096,1024]{1,0:T(8,128)(2,1)} async-done(((bf16[512,1024]{1,0:T(8,128)(2,1)}), bf16[4096,1024]{1,0:T(8,128)(2,1)}) %all-gather.20.cloned.1.call-update) | async-done | bytes 8388624 | tf_op jit(solution)/shard_map/all_gather | solution.py:61
  759.7 25.5 %fusion.25 = f32[6144,1536]{1,0:T(8,128)} fusion(f32[576,1536]{1,0:T(8,128)} %broadcast_in_dim.240, f32[1536]{0:T(1024)S(1)} %copy-done.145, f32[576,6144]{1,0:T(8,128)} %fusion.65), kind=kOutput, calls=%fused_computation.237 | convolution fusion | flops 10905255936 | bytes 55449600 | tf_op jit(solution)/shard_map/dot_general | solution.py:194
  787.2 25.5 %fusion.7 = bf16[576,6144]{1,0:T(8,128)(2,1)} fusion(f32[576,6144]{1,0:T(8,128)} %fusion.65, bf16[6144,1536]{1,0:T(8,128)(2,1)} %all-gather.10.cloned.1.call-done, f32[576,1536]{1,0:T(8,128)S(1)} %copy-done.14, f32[1536]{0:T(1024)S(1)} %copy-done.145), kind=kOutput, calls=%fused_computation.57 | convolution fusion | flops 10944184320 | bytes 43653120 | tf_op jit(solution)/shard_map/dot_general | solution.py:195
  812.6 22.3 fusion.70
  842.9 18.9 fusion.67
  867.1 24.6 %multiply_reduce_fusion.48 = (f32[1536]{0:T(1024)}, f32[1536]{0:T(1024)}, f32[1536]{0:T(1024)}, f32[1536]{0:T(1024)}, f32[1536]{0:T(1024)}, /*index=5*/f32[1536]...) fusion(f32[1,24,24,1536]{3,2,1,0:T(8,128)} %convert_element_typ, ...), kind=kLoop, calls=%fused_computation.117 | loop fusion | flops 30061056 | bytes 16020480 | tf_op jit(solution)/shard_map/transpose(jvp())/reduce_sum | solution.py:25
  893.5 29.3 %multiply_reduce_fusion.49 = (f32[1536]{0:T(1024)}, f32[1536]{0:T(1024)}, f32[1536]{0:T(1024)}, f32[1536]{0:T(1024)}, f32[1536]{0:T(1024)}, /*index=5*/f32[1536]...) fusion(f32[1,24,24,1536]{3,2,1,0:T(8,128)S(1)} %get-tuple-eleme, ...), kind=kLoop, calls=%fused_computation.118 | loop fusion | flops 31822848 | bytes 7188480 | tf_op jit(solution)/shard_map/transpose(jvp())/reduce_sum | solution.py:25
  928.9 151.5 %reduce-scatter.14.cloned.1.call-done = f32[512,1024]{1,0:T(8,128)} async-done(((f32[4096,1024]{1,0:T(8,128)}), f32[512,1024]{1,0:T(8,128)}) %reduce-scatter.14.cloned.1.call-update) | async-done | bytes 2097168 | tf_op jit(solution)/shard_map/reduce_scatter | solution.py:208
  1083.2 166.1 %reduce-scatter.12.cloned.1.call-done = f32[128,4096]{1,0:T(8,128)} async-done(((f32[1024,4096]{1,0:T(8,128)}), f32[128,4096]{1,0:T(8,128)}) %reduce-scatter.12.cloned.1.call-update) | async-done | bytes 2097168 | tf_op jit(solution)/shard_map/reduce_scatter | solution.py:207
  1252.0 363.0 %reduce-scatter.20.cloned.1.call-done = f32[768,1536]{1,0:T(8,128)} async-done(((f32[6144,1536]{1,0:T(8,128)}), f32[768,1536]{1,0:T(8,128)}) %reduce-scatter.20.cloned.1.call-update) | async-done | bytes 4718608 | tf_op jit(solution)/shard_map/reduce_scatter | solution.py:211
  1619.0 361.6 %reduce-scatter.18.cloned.1.call-done = f32[192,6144]{1,0:T(8,128)} async-done(((f32[1536,6144]{1,0:T(8,128)}), f32[192,6144]{1,0:T(8,128)}) %reduce-scatter.18.cloned.1.call-update) | async-done | bytes 4718608 | tf_op jit(solution)/shard_map/reduce_scatter | solution.py:210
  1986.7 27.3 %multiply_reduce_fusion.50 = (f32[1536]{0:T(1024)}, f32[1536]{0:T(1024)}, f32[1536]{0:T(1024)}, f32[1536]{0:T(1024)}, f32[1536]{0:T(1024)}, /*index=5*/f32[1536]...) fusion(f32[1,24,24,1536]{3,2,1,0:T(8,128)S(1)} %copy-done.3, ...), kind=kLoop, calls=%fused_computation.119 | loop fusion | flops 31822848 | bytes 7188480 | tf_op jit(solution)/shard_map/transpose(jvp())/reduce_sum | solution.py:25
  2071.9 21.7 broadcast_multiply_fusion.1
  2093.8 21.0 broadcast_multiply_fusion
  2114.9 53.7 %pad_add_fusion = f32[1,30,30,1536]{3,2,1,0:T(8,128)S(1)} fusion(f32[1,24,24,1536]{3,2,1,0:T(8,128)} %get-tuple-element.162, f32[1,24,24,1536]{3,2,1,0:T(8,128)} %get-tuple-element.163, f32[1,24,24,1536]{3,2,1,0:T(8,128)} %get-tuple-element.164, f32[1,24,24,1536]{3,2,1,0:T(8,128)} %get-tuple-element.165, f32[1,24,24,1536]{3,2,1,0:T(8,128)} %get-tuple-element.166, ...), kind=kLoop, calls=%fused_computation.59 | loop fusion | flops 58060800 | bytes 157704192 | tf_op jit(solution)/shard_map/transpose(jvp())/add_any | solution.py:22
  2178.2 39.2 %all-reduce.118 = (f32[1024]{0:T(1024)}, f32[1024]{0:T(1024)}, f32[9,1024]{1,0:T(8,128)}, f32[1024]{0:T(1024)}, f32[1536]{0:T(1024)}, /*index=5*/f32[1536]{0:T(1024)}) all-reduce(f32[1024]{0:T(1024)S(1)} %copy-done.146, f32[1024]{0:T(1024)S(1)} %copy-done.124, ...), channel_id=1, replica_groups=mesh['path'=4,'dev'=8] {'path','dev'}, use_global_device_ids=true, to_apply=%region_17.18 | all-reduce | flops 15360 | bytes 122880 | tf_op jit(solution)/shard_map/psum | solution.py:222
  2232.6 57.5 %all-reduce.123.cloned.1.call-done = f32[49,1536]{1,0:T(8,128)} async-done(((f32[49,1536]{1,0:T(8,128)}), f32[49,1536]{1,0:T(8,128)}) %all-reduce.123.cloned.1.call-update) | async-done | bytes 301072 | tf_op jit(solution)/shard_map/psum | solution.py:222
  (502 shorter events, 334.7 us)
Async XLA Ops:
  7.2 173.5 %all-gather.8.cloned.1.call-start = ((), (), s32[]{:S(2)}) async-start(), calls=%async_computation.12 | async-start | bytes 21233664 | tf_op jit(solution)/shard_map/all_gather | solution.py:63
  7.9 340.9 %all-gather.10.cloned.1.call-start = ((), (), s32[]{:S(2)}) async-start(), calls=%async_computation.13 | async-start | bytes 21233664 | tf_op jit(solution)/shard_map/all_gather | solution.py:64
  8.7 399.3 %all-gather.12.cloned.1.call-start = ((), (), s32[]{:S(2)}) async-start(), calls=%async_computation.14 | async-start | bytes 3538944 | tf_op jit(solution)/shard_map/all_gather | solution.py:62
  9.4 442.7 %all-gather.14.cloned.1.call-start = ((), (), s32[]{:S(2)}) async-start(), calls=%async_computation.15 | async-start | bytes 7077888 | tf_op jit(solution)/shard_map/all_gather | solution.py:58
  10.0 471.4 %all-gather.16.cloned.1.call-start = ((), (), s32[]{:S(2)}) async-start(), calls=%async_computation.16 | async-start | bytes 2359296 | tf_op jit(solution)/shard_map/all_gather | solution.py:59
  10.6 553.8 %all-gather.18.cloned.1.call-start = ((), (), s32[]{:S(2)}) async-start(), calls=%async_computation.17 | async-start | bytes 9437184 | tf_op jit(solution)/shard_map/all_gather | solution.py:60
  12.4 371.6 %all-to-all-start = ((s32[4,1,1]{2,1,0:T(1,128)}), s32[4,1,1]{2,1,0:T(1,128)}, u32[]{:S(2)}, u32[]{:S(2)}) async-start(s32[4,1,1]{2,1,0:T(1,128)} %broadcast_in_dim.232), calls=%async_computation | async-start | bytes 4096 | tf_op jit(solution)/shard_map/all_to_all | solution.py:94
  17.6 629.1 %all-gather.20.cloned.1.call-start = ((), (), s32[]{:S(2)}) async-start(), calls=%async_computation.18 | async-start | bytes 9437184 | tf_op jit(solution)/shard_map/all_gather | solution.py:61
  199.0 172.2 %copy-start.10 = (bf16[1,24,24,1536]{3,2,1,0:T(8,128)(2,1)S(1)}, bf16[1,24,24,1536]{3,2,1,0:T(8,128)(2,1)}, u32[]{:S(2)}) copy-start(bf16[1,24,24,1536]{3,2,1,0:T(8,128)(2,1)} %param.19) | copy-start | bytes 5308420
  199.0 172.2 %copy-start.144 = (f32[1536]{0:T(1024)S(1)}, f32[1536]{0:T(1024)}, u32[]{:S(2)}) copy-start(f32[1536]{0:T(1024)} %param.35) | copy-start | bytes 18436
  384.0 11.7 all-to-all-start.1
  397.2 10.7 all-to-all-start.2
  400.6 522.2 %reduce-scatter.10.cloned.1.call-start = ((), (), s32[]{:S(2)}) async-start(), calls=%async_computation.20 | async-start | bytes 4718592 | tf_op jit(solution)/shard_map/reduce_scatter | solution.py:206
  463.1 101.3 %copy-start.54 = (f32[1024]{0:T(1024)S(1)}, f32[1024]{0:T(1024)}, u32[]{:S(2)}) copy-start(f32[1024]{0:T(1024)} %param.25) | copy-start | bytes 12292
  483.8 230.1 %copy-start.7 = (f32[144,1024]{1,0:T(8,128)}, f32[144,1024]{1,0:T(8,128)S(1)}, u32[]{:S(2)}) copy-start(f32[144,1024]{1,0:T(8,128)S(1)} %get-tuple-element.228) | copy-start | bytes 1769476
  569.3 135.6 %copy-start.19 = (f32[144,4096]{1,0:T(8,128)}, f32[144,4096]{1,0:T(8,128)S(1)}, u32[]{:S(2)}) copy-start(f32[144,4096]{1,0:T(8,128)S(1)} %fusion.55) | copy-start | bytes 7077892
  662.7 261.9 %reduce-scatter.16.cloned.1.call-start = ((), (), s32[]{:S(2)}) async-start(), calls=%async_computation.23 | async-start | bytes 7077888 | tf_op jit(solution)/shard_map/reduce_scatter | solution.py:209
  696.6 230.0 %reduce-scatter.8.cloned.1.call-start = ((), (), s32[]{:S(2)}) async-start(), calls=%async_computation.19 | async-start | bytes 14155776 | tf_op jit(solution)/shard_map/reduce_scatter | solution.py:205
  704.6 375.8 %reduce-scatter.14.cloned.1.call-start = ((), (), s32[]{:S(2)}) async-start(), calls=%async_computation.22 | async-start | bytes 18874368 | tf_op jit(solution)/shard_map/reduce_scatter | solution.py:208
  713.9 535.4 %reduce-scatter.12.cloned.1.call-start = ((), (), s32[]{:S(2)}) async-start(), calls=%async_computation.21 | async-start | bytes 18874368 | tf_op jit(solution)/shard_map/reduce_scatter | solution.py:207
  723.5 891.4 %reduce-scatter.20.cloned.1.call-start = ((), (), s32[]{:S(2)}) async-start(), calls=%async_computation.26 | async-start | bytes 42467328 | tf_op jit(solution)/shard_map/reduce_scatter | solution.py:211
  785.2 1195.5 %reduce-scatter.18.cloned.1.call-start = ((), (), s32[]{:S(2)}) async-start(), calls=%async_computation.25 | async-start | bytes 42467328 | tf_op jit(solution)/shard_map/reduce_scatter | solution.py:210
  835.0 1382.4 %all-reduce.125.cloned.1.call-start = ((), (), s32[]{:S(2)}) async-start(), calls=%async_computation.27 | async-start | bytes 16515072 | tf_op jit(solution)/shard_map/psum | solution.py:214
  1984.7 305.3 %all-reduce.123.cloned.1.call-start = ((), (), s32[]{:S(2)}) async-start(), calls=%async_computation.24 | async-start | bytes 688128 | tf_op jit(solution)/shard_map/psum | solution.py:222
  (146 other events, 1712.8 us)
Sparse Core Ops, SparseCore 0:
  9.7 170.9 all-gather.7
  182.3 166.4 all-gather.9
  350.5 36.4 all-gather.11
  388.5 63.6 all-gather.13
  453.6 27.7 all-gather.15
  482.9 81.5 all-gather.17
  566.0 80.5 all-gather.19
  662.8 48.5 reduce-scatter.9
  713.7 67.9 reduce-scatter.15
  783.8 127.5 reduce-scatter.7
  913.8 166.6 reduce-scatter.13
  1082.6 166.5 reduce-scatter.11
  1251.6 363.2 reduce-scatter.19
  1617.3 363.2 reduce-scatter.17
  1986.4 171.0 all-reduce.124
  2164.2 125.7 all-reduce.122
where the time goes:
time: 2310 us; the launch traced here: 2300 us
  waiting for transfers between devices  1550 us (67%)
  other arithmetic  362 us (16%)
  matrix products  212 us (9%)
  local copies, waits for them, and re-layouts  86.5 us (4%)
  blocking collectives  61.7 us (3%)
    reduce_scatter x1, waiting for transfers between devices, local(): lax.psum_scatter(grad_reduce_w, 'dev', scatter_dimension=0, tiled=True)  363 us
    reduce_scatter x1, waiting for transfers between devices, local(): lax.psum_scatter(grad_expand_w, 'dev', scatter_dimension=0, tiled=True)  362 us
    reduce_scatter x1, waiting for transfers between devices, local(): lax.psum_scatter(grad_fc1_w, 'dev', scatter_dimension=0, tiled=True)  166 us
    reduce_scatter x1, waiting for transfers between devices, local(): lax.psum_scatter(grad_fc2_w, 'dev', scatter_dimension=0, tiled=True)  152 us
    all_gather x1, waiting for transfers between devices, local(): lax.all_gather(w_reduce, 'dev', axis=0, tiled=True)  150 us
    reduce_sum x4, other arithmetic, layer_norm(): centred = values - jnp.mean(values, axis=-1, keepdims=True)  90.9 us
    reduce_sum x5, other arithmetic, depthwise(): window * taps_table[offset_row * kernel_side + offset_col]  88 us
    all_gather x1, waiting for transfers between devices, local(): lax.all_gather(w_fc1, 'dev', axis=0, tiled=True)  79.8 us
  transfers between devices with their start and end apart: 19, of which 13 were waited for; matrix products, arithmetic and copies ran while one was open for 27% of the time, Pallas kernels for 0%

commit v1 on v0

--- a/solution.py
+++ b/solution.py
@@ -1,9 +1,110 @@
+import functools
+
 import jax
 import jax.numpy as jnp
 from jax import lax
+from jax.experimental import pallas as pl
+from jax.experimental.pallas import tpu as pltpu
 from jax.sharding import PartitionSpec as P
 
 HEAD_DIM = 64
+MESH = pl.DeviceIdType.MESH
+
+def gather_jobs(shapes):
+    jobs = []
+    for w, (r, n) in enumerate(shapes):
+        q = r // 4
+        size = q * n
+        parts = max(1, round(size / (16 * 6144)))
+        while parts > 1 and (n // 2) % (parts * 128): parts -= 1
+        for k in range(parts):
+            jobs.append((w, q, k * (n // parts), n // parts))
+    return jobs
+
+def gather_kernel(jobs, count, *refs):
+    shards = refs[:count]; fulls = refs[count:2*count]
+    zs, zr, ps, pr, cs, cr, ls = refs[2*count:]
+    p = lax.axis_index("path"); d = lax.axis_index("dev")
+    masks = [(0,1),(0,2),(0,4),(0,6),(1,0),(2,0)]
+    def at(m): return (p ^ m[0], d ^ m[1])
+    bar = pltpu.get_barrier_semaphore()
+    for m in masks: pl.semaphore_signal(bar, inc=1, device_id=at(m), device_id_type=MESH)
+    pl.semaphore_wait(bar, len(masks))
+    def rows(w, owner):
+        r = shards[w].shape[0]; return r, owner * r
+    def copy(src, dst, ss, rs, m):
+        return pltpu.make_async_remote_copy(src, dst, ss, rs, device_id=at(m), device_id_type=MESH)
+    def quarter(w, owner, q, nq, c0, nc):
+        r = shards[w].shape[0]
+        return fulls[w].at[pl.ds(pl.multiple_of(owner * r + q * nq, 16), nq), pl.ds(c0, nc)]
+    own = []
+    for w in range(count):
+        r = shards[w].shape[0]
+        place = fulls[w].at[pl.ds(pl.multiple_of(d * r, 16), r)]
+        a = pltpu.make_async_copy(shards[w], place, ls.at[w]); a.start()
+        b = copy(shards[w], place, cs.at[w, 0], cr.at[w, 0], (0,1)); b.start()
+        own.append((a, b))
+    J = len(jobs)
+    def Z(i, k):
+        w, nq, c0, nc = jobs[i]
+        return copy(shards[w].at[pl.ds(pl.multiple_of(p * nq, 16), nq), pl.ds(c0, nc)], quarter(w, d, p, nq, c0, nc), zs.at[i,k], zr.at[i,k], (0, 2*(k+1)))
+    def XY(i, k, axis):
+        w, nq, c0, nc = jobs[i]
+        ref = quarter(w, d ^ (2*(k+1)), p, nq, c0, nc)
+        return copy(ref, ref, ps.at[i,k,axis], pr.at[i,k,axis], (1+axis, 0))
+    def DG(i, k, axis):
+        w, nq, c0, nc = jobs[i]
+        h = nc // 2
+        ref = quarter(w, d ^ (2*(k+1)), p ^ (2 - axis), nq, c0 + axis * h, h)
+        return copy(ref, ref, ps.at[i,k,2+axis], pr.at[i,k,2+axis], (1+axis, 0))
+    def S(w, k):
+        r = shards[w].shape[0]
+        ref = fulls[w].at[pl.ds(pl.multiple_of((d ^ (2*(k+1))) * r, 16), r)]
+        return copy(ref, ref, cs.at[w,1+k], cr.at[w,1+k], (0,1))
+    last = {}
+    for i,(w,*_) in enumerate(jobs): last[w] = i
+    AHEAD = 2
+    for i in range(min(AHEAD, J)):
+        for k in range(3): Z(i,k).start()
+    sent = []
+    for i in range(J + 2):
+        if i < J:
+            for k in range(3):
+                Z(i,k).wait_recv()
+                XY(i,k,0).start(); XY(i,k,1).start()
+            if i + AHEAD < J:
+                for k in range(3): Z(i+AHEAD,k).start()
+        if 0 <= i-1 < J:
+            for k in range(3):
+                XY(i-1,k,0).wait_recv(); DG(i-1,k,1).start()
+                XY(i-1,k,1).wait_recv(); DG(i-1,k,0).start()
+        if 0 <= i-2 < J:
+            for k in range(3):
+                DG(i-2,k,0).wait_recv(); DG(i-2,k,1).wait_recv()
+            w = jobs[i-2][0]
+            if last[w] == i-2:
+                for k in range(3): S(w,k).start()
+    for w in range(count):
+        own[w][0].wait(); own[w][1].wait()
+        for k in range(3): S(w,k).wait()
+    for i in range(J):
+        for k in range(3):
+            Z(i,k).wait_send()
+            for a in range(2): XY(i,k,a).wait_send(); DG(i,k,a).wait_send()
+
+def gather_weights(shards, collective_id=0):
+    shapes = [s.shape for s in shards]
+    jobs = gather_jobs(shapes); n = len(shards); J = len(jobs)
+    anyspec = pl.BlockSpec(memory_space=pl.ANY)
+    return pl.pallas_call(
+        functools.partial(gather_kernel, jobs, n),
+        out_shape=[jax.ShapeDtypeStruct((8*r, c), jnp.bfloat16) for r, c in shapes],
+        in_specs=[anyspec]*n, out_specs=[anyspec]*n,
+        scratch_shapes=[pltpu.SemaphoreType.DMA((J,3)),pltpu.SemaphoreType.DMA((J,3)),
+            pltpu.SemaphoreType.DMA((J,3,4)),pltpu.SemaphoreType.DMA((J,3,4)),
+            pltpu.SemaphoreType.DMA((n,4)),pltpu.SemaphoreType.DMA((n,4)),pltpu.SemaphoreType.DMA((n,))],
+        compiler_params=pltpu.CompilerParams(collective_id=collective_id, has_side_effects=True),
+    )(*shards)
 
 
 def layer_norm(values, gain_vec):
@@ -32,6 +133,70 @@
 
 def adapter_depthwise(grid_field, grid_kernel):
     return depthwise(grid_field, grid_kernel, 3)
+
+
+def gather_all(shards, tuned):
+    if tuned:
+        return gather_weights(shards)
+    return [lax.all_gather(shard, "dev", axis=0, tiled=True) for shard in shards]
+
+
+def swap(value, axis, mask):
+    size = lax.axis_size(axis)
+    return lax.ppermute(value, axis, [(i, i ^ mask) for i in range(size)])
+
+
+def pick(value, index, axis):
+    return lax.dynamic_index_in_dim(value, index, axis, keepdims=False)
+
+
+def add_low(left, right):
+    return (left.astype(jnp.float32) + right.astype(jnp.float32)).astype(jnp.bfloat16)
+
+
+def pair_gradient(rows, grads):
+    side = lax.rem(lax.axis_index("dev"), 2)
+    tokens, depth = rows.shape
+    split = rows.reshape(tokens, 4, 2, depth // 8)
+    mine = pick(split, side, 2)
+    theirs = swap(pick(split, 1 - side, 2), "dev", 1)
+    both_rows = jnp.concatenate([mine.reshape(tokens, depth // 2), theirs.reshape(tokens, depth // 2)])
+    both_grads = jnp.concatenate([grads, swap(grads, "dev", 1)])
+    product = lax.dot_general(
+        both_rows, both_grads, (((0,), (0,)), ((), ())), preferred_element_type=jnp.float32
+    )
+    return product.astype(jnp.bfloat16).reshape(4, depth // 8, grads.shape[1])
+
+
+def plane_first(share):
+    path = lax.axis_index("path")
+    up, across = path // 2, lax.rem(path, 2)
+    height = lax.axis_index("dev") // 2
+    _, rows, columns = share.shape
+    view = share.reshape(4, 2, 2, rows // 4, columns)
+    left, right = view[..., : columns // 2], view[..., columns // 2 :]
+    left = add_low(pick(left, across, 2), swap(pick(left, 1 - across, 2), "path", 1))
+    right = add_low(pick(right, up, 1), swap(pick(right, 1 - up, 1), "path", 2))
+    left = add_low(pick(left, up, 1), swap(pick(left, 1 - up, 1), "path", 2))
+    right = add_low(pick(right, across, 1), swap(pick(right, 1 - across, 1), "path", 1))
+    quarter = jnp.concatenate([left, right], axis=-1)
+    total = pick(quarter, height, 0).astype(jnp.float32)
+    for mask in (1, 2, 3):
+        total = total + swap(pick(quarter, height ^ mask, 0), "dev", 2 * mask).astype(jnp.float32)
+    low = total.astype(jnp.bfloat16)
+    pieces = jnp.stack([low] + [swap(low, "path", mask) for mask in (1, 2, 3)])
+    order = jnp.arange(4, dtype=jnp.int32) ^ path
+    return jnp.concatenate([pick(pieces, order[i], 0) for i in range(4)]).astype(jnp.float32)
+
+
+def summed_gradient(rows, grads, tuned, plane):
+    if tuned and plane:
+        return plane_first(pair_gradient(rows, grads))
+    product = lax.dot_general(
+        rows, grads, (((0,), (0,)), ((), ())), preferred_element_type=jnp.float32
+    ).astype(jnp.bfloat16)
+    share = lax.psum_scatter(product, "dev", scatter_dimension=0, tiled=True)
+    return lax.psum(share, "path").astype(jnp.float32)
 
 
 def local(
@@ -54,16 +219,10 @@
     w_reduce,
     layer_scale,
 ):
-    gathered = (
-        lax.all_gather(w_qkv, "dev", axis=0, tiled=True),
-        lax.all_gather(w_out, "dev", axis=0, tiled=True),
-        lax.all_gather(w_fc1, "dev", axis=0, tiled=True),
-        lax.all_gather(w_fc2, "dev", axis=0, tiled=True),
-        lax.all_gather(w_adapter, "dev", axis=0, tiled=True),
-        lax.all_gather(w_expand, "dev", axis=0, tiled=True),
-        lax.all_gather(w_reduce, "dev", axis=0, tiled=True),
-    )
-    full_qkv, full_out, full_fc1, full_fc2, full_adapter, full_expand, full_reduce = gathered
+    tuned = lax.axis_size("path") == 4 and lax.axis_size("dev") == 8
+    full_expand, full_reduce, full_adapter, full_qkv, full_out, full_fc1, full_fc2 = gather_all(
+        (w_expand, w_reduce, w_adapter, w_qkv, w_out, w_fc1, w_fc2), tuned
+    )
     path_count = lax.axis_size("path")
     maps_float = hires_maps.astype(jnp.float32)
     map_side = maps_float.shape[1]
@@ -135,15 +294,15 @@
     result = (hidden_mid + lowered)[None].astype(jnp.bfloat16)
     grad_out = cotangent[0].astype(jnp.float32)
     grad_out_low = grad_out.astype(jnp.bfloat16)
-    grad_fc2_w = jnp.dot(lifted.T, grad_out_low, preferred_element_type=jnp.float32)
+    grad_fc2_w = summed_gradient(lifted, grad_out_low, tuned, False)
     grad_lifted = jnp.dot(grad_out_low, full_fc2.T, preferred_element_type=jnp.float32)
     grad_raised = gelu_back(grad_lifted)[0].astype(jnp.bfloat16)
-    grad_fc1_w = jnp.dot(mlp_rows.T, grad_raised, preferred_element_type=jnp.float32)
+    grad_fc1_w = summed_gradient(mlp_rows, grad_raised, tuned, False)
     grad_normed_two = jnp.dot(grad_raised, full_fc1.T, preferred_element_type=jnp.float32)
     grad_mid_norm, grad_mlp_gain = norm_two_back(grad_normed_two)
     grad_mid = grad_out + grad_mid_norm
     grad_attended = grad_mid.astype(jnp.bfloat16)
-    grad_out_w = jnp.dot(attn_mixed.T, grad_attended, preferred_element_type=jnp.float32)
+    grad_out_w = summed_gradient(attn_mixed, grad_attended, tuned, False)
     grad_mixed = jnp.dot(grad_attended, full_out.T, preferred_element_type=jnp.float32)
     grad_mixed = grad_mixed.astype(jnp.bfloat16).reshape(tokens, head_count, HEAD_DIM)
     grad_probs = jnp.einsum("thd,shd->hts", grad_mixed, values, preferred_element_type=jnp.float32)
@@ -168,7 +327,7 @@
         ],
         axis=1,
     ).astype(jnp.bfloat16)
-    grad_qkv_w = jnp.dot(attn_rows.T, grad_projected, preferred_element_type=jnp.float32)
+    grad_qkv_w = summed_gradient(attn_rows, grad_projected, tuned, False)
     grad_normed_one = jnp.dot(grad_projected, full_qkv.T, preferred_element_type=jnp.float32)
     grad_in_norm, grad_attn_gain = norm_one_back(grad_normed_one)
     grad_in = grad_mid + grad_in_norm
@@ -176,7 +335,7 @@
     grad_spread = (grad_in * gate_factor).reshape(1, grid_side, grid_side, model_width)
     grad_adapted, grad_adapter_taps = adapter_back(grad_spread)
     grad_adapted_low = grad_adapted.reshape(tokens, model_width).astype(jnp.bfloat16)
-    grad_adapter_w = jnp.dot(features.T, grad_adapted_low, preferred_element_type=jnp.float32)
+    grad_adapter_w = summed_gradient(features, grad_adapted_low, tuned, False)
     grad_features = jnp.dot(grad_adapted_low, full_adapter.T, preferred_element_type=jnp.float32)
     grad_pieces = grad_features.astype(jnp.bfloat16).reshape(path_count, quarter_rows, channels)
     grad_routed = lax.all_to_all(grad_pieces, "path", split_axis=0, concat_axis=0, tiled=True)
@@ -191,33 +350,24 @@
     )
     grad_scale = jnp.sum((grad_section_out * reduced).reshape(-1, channels), axis=0)
     grad_reduced = (grad_section_out * layer_scale).reshape(-1, channels).astype(jnp.bfloat16)
-    grad_reduce_w = jnp.dot(activated_low.T, grad_reduced, preferred_element_type=jnp.float32)
+    grad_reduce_w = summed_gradient(activated_low, grad_reduced, tuned, True)
     grad_activated = jnp.dot(grad_reduced, full_reduce.T, preferred_element_type=jnp.float32)
     grad_expanded = section_gelu_back(grad_activated)[0].astype(jnp.bfloat16)
-    grad_expand_w = jnp.dot(section_rows.T, grad_expanded, preferred_element_type=jnp.float32)
+    grad_expand_w = summed_gradient(section_rows, grad_expanded, tuned, True)
     grad_section_normed = jnp.dot(
         grad_expanded, full_expand.T, preferred_element_type=jnp.float32
     ).reshape(maps_float.shape)
     grad_section_mixed, grad_section_gain = section_norm_back(grad_section_normed)
     grad_maps_conv, grad_section_taps = section_back(grad_section_mixed)
     grad_maps = grad_section_out + grad_maps_conv
-    shares = (
-        lax.psum_scatter(grad_qkv_w, "dev", scatter_dimension=0, tiled=True),
-        lax.psum_scatter(grad_out_w, "dev", scatter_dimension=0, tiled=True),
-        lax.psum_scatter(grad_fc1_w, "dev", scatter_dimension=0, tiled=True),
-        lax.psum_scatter(grad_fc2_w, "dev", scatter_dimension=0, tiled=True),
-        lax.psum_scatter(grad_adapter_w, "dev", scatter_dimension=0, tiled=True),
-        lax.psum_scatter(grad_expand_w, "dev", scatter_dimension=0, tiled=True),
-        lax.psum_scatter(grad_reduce_w, "dev", scatter_dimension=0, tiled=True),
-    )
     summed = (
-        lax.psum(shares[0].astype(jnp.bfloat16), "path").astype(jnp.float32),
-        lax.psum(shares[1].astype(jnp.bfloat16), "path").astype(jnp.float32),
-        lax.psum(shares[2].astype(jnp.bfloat16), "path").astype(jnp.float32),
-        lax.psum(shares[3].astype(jnp.bfloat16), "path").astype(jnp.float32),
-        lax.psum(shares[4].astype(jnp.bfloat16), "path").astype(jnp.float32),
-        lax.psum(shares[5].astype(jnp.bfloat16), "path").astype(jnp.float32),
-        lax.psum(shares[6].astype(jnp.bfloat16), "path").astype(jnp.float32),
+        grad_qkv_w,
+        grad_out_w,
+        grad_fc1_w,
+        grad_fc2_w,
+        grad_adapter_w,
+        grad_expand_w,
+        grad_reduce_w,
     )
     small_sums = lax.psum(
         (

time: 2310 us -> 1260 us (0.55)
  waiting for transfers between devices: 1550 us -> 130 us
  Pallas kernels: 0 us -> 259 us
  local copies, waits for them, and re-layouts: 86.5 us -> 196 us
  starting transfers between devices: 13.9 us -> 56.7 us
  other arithmetic: 362 us -> 331 us
  matrix products: 212 us -> 184 us
    reduce_scatter x7 -> x5, waiting for transfers between devices: 1040 us -> 0.82 us  [summed_gradient(): share = lax.psum_scatter(product, 'dev', scatter_dimension=0, tiled=True)]
    all_gather x7 -> x0, waiting for transfers between devices: 428 us -> none  [the longest x1 150 us: local(): lax.all_gather(w_reduce, 'dev', axis=0, tiled=True)]
    pallas_call x0 -> x1, Pallas kernels: none -> 259 us  [gather_weights(): pl.pallas_call(functools.partial(gather_kernel, jobs, n), out_shape=[jax....]
    ppermute x0 -> x24, waiting for transfers between devices: none -> 109 us  [swap(): return lax.ppermute(value, axis, [(i, i ^ mask) for i in range(size)])]
    dynamic_slice x0 -> x6, local copies, waits for them, and re-layouts: none -> 88.5 us  [pick(): return lax.dynamic_index_in_dim(value, index, axis, keepdims=False)]
    psum x1, waiting for transfers between devices: 57.5 us -> 0.01 us  [local(): lax.psum((grad_attn_gain, grad_mlp_gain, grad_merge, grad_adapter_taps, g...]
    ppermute x0 -> x24, starting transfers between devices: none -> 34.9 us  [swap(): return lax.ppermute(value, axis, [(i, i ^ mask) for i in range(size)])]
    broadcast_in_dim x49, local copies, waits for them, and re-layouts: 34.4 us -> 0.31 us  [depthwise(): taps_table[offset_row * kernel_side + offset_col]]
  transfers between devices with their start and end apart: 19 -> 36, of which waited for: 13 -> 10; matrix products, arithmetic and copies ran while one was open for 27% -> 52% of each run, Pallas kernels for 0% -> 21%
where the time goes in v1:
time: 1260 us; the launch traced here: 1240 us
  other arithmetic  331 us (26%)
  Pallas kernels  259 us (21%)
  local copies, waits for them, and re-layouts  196 us (16%)
  matrix products  184 us (15%)
  waiting for transfers between devices  130 us (10%)
  blocking collectives  61.8 us (5%)
  starting transfers between devices  56.7 us (4%)
  between operations  25.4 us (2%)
    pallas_call x1, Pallas kernels, gather_weights(): pl.pallas_call(functools.partial(gather_kernel, jobs, n), out_shape=[jax....  259 us
    ppermute x24, waiting for transfers between devices, swap(): return lax.ppermute(value, axis, [(i, i ^ mask) for i in range(size)])  109 us
    dynamic_slice x6, local copies, waits for them, and re-layouts, pick(): return lax.dynamic_index_in_dim(value, index, axis, keepdims=False)  88.5 us
    reduce_sum x4, other arithmetic, layer_norm(): centred = values - jnp.mean(values, axis=-1, keepdims=True)  85.8 us
    reduce_sum x5, other arithmetic, depthwise(): window * taps_table[offset_row * kernel_side + offset_col]  62.5 us
    psum x1, blocking collectives, local(): lax.psum((grad_attn_gain, grad_mlp_gain, grad_merge, grad_adapter_taps, g...  61.8 us
    mul x3, other arithmetic, depthwise(): window * taps_table[offset_row * kernel_side + offset_col]  57 us
    add_any x2, other arithmetic, depthwise(): padded[:, offset_row:offset_row + map_side, offset_col:offset_col + map_s...  50.5 us
  transfers between devices with their start and end apart: 36, of which 10 were waited for; matrix products, arithmetic and copies ran while one was open for 52% of the time, Pallas kernels for 21%

profile of v1, /device:TPU:0, one launch (start us, length us, event | category | flops | bytes accessed | tf_op | source)
XLA Modules:
  0.0 1244.5 jit_solution(18166256931534319181)
XLA Ops:
  24.3 84.8 %fusion.99 = (f32[24,24]{1,0:T(8,128)}, f32[1,24,24,1536]{3,2,1,0:T(8,128)S(1)}) fusion(f32[1536]{0:T(1024)} %get-tuple-element.141, f32[1536]{0:T(1024)} %get-tuple-element.142, f32[1536]{0:T(1024)S(1)} %get-tuple-element.95, f32[1536]{0:T(1024)S(1)} %get-tuple-element.96, f32[1536]{0:T(1024)} %get-tuple-element.97, f32[1536]{0:T(1024)} %get-tuple-element.98, ...), kind=kLoop, calls=%fused_computation.459 | loop fusion | flops 86703552 | bytes 7381248 | tf_op jit(solution)/shard_map/jvp()/reduce_sum | solution.py:111
  113.2 258.7 %shard_map.305 = (bf16[1536,6144]{1,0:T(8,128)(2,1)}, bf16[6144,1536]{1,0:T(8,128)(2,1)}, bf16[1536,1024]{1,0:T(8,128)(2,1)}, bf16[1024,3072]{1,0:T(8,128)(2,1)}...) custom-call(bf16[192,6144]{1,0:T(8,128)(2,1)} %refs_0_.1, ...), custom_call_target="tpu_custom_call" | custom-call | tf_op jit(solution)/shard_map/pallas_call | solution.py:99
  371.9 21.4 %multiply_convert_fusion = (bf16[576,6144]{1,0:T(8,128)(2,1)S(1)}, f32[576,6144]{1,0:T(8,128)}) fusion(bf16[576,1536]{1,0:T(8,128)(2,1)} %bitcast.228, bf16[1536,6144]{1,0:T(8,128)(2,1)} %get-tuple-element.24), kind=kOutput, calls=%fused_computation.62 | convolution fusion | flops 10903486464 | bytes 41877504 | tf_op jit(solution)/shard_map/dot_general | solution.py:239
  393.4 17.0 %fusion.107 = f32[576,1536]{1,0:T(8,128)S(1)} fusion(bf16[576,6144]{1,0:T(8,128)(2,1)S(1)} %get-tuple-element.269, bf16[6144,1536]{1,0:T(8,128)(2,1)} %get-tuple-element.25), kind=kOutput, calls=%fused_computation.467 | convolution fusion | flops 10871635968 | bytes 29491200 | tf_op jit(solution)/shard_map/dot_general | solution.py:242
  542.5 11.8 reshape.995
  554.3 66.2 %dynamic-slice_reduce_fusion = (bf16[576,4,768]{2,1,0:T(4,128)(2,1)}, bf16[576,4,1,768]{3,2,1,0:T(2,128)(2,1)}) fusion(bf16[576,4,2,768]{3,2,1,0:T(2,128)(2,1)} %reshape.995, s32[]{:T(128)S(6)} %select_n.84, s32[]{:T(128)S(6)} %select_n.85), kind=kLoop, calls=%fused_computation.70 | loop fusion | bytes 14155784 | tf_op jit(solution)/shard_map/jit(dynamic_index_in_dim)/dynamic_slice | solution.py:150
  692.3 24.7 %fusion.7 = bf16[576,6144]{1,0:T(8,128)(2,1)} fusion(f32[576,6144]{1,0:T(8,128)} %get-tuple-element.270, bf16[576,1536]{1,0:T(8,128)(2,1)} %get-tuple-element.178, bf16[6144,1536]{1,0:T(8,128)(2,1)} %get-tuple-element.25), kind=kOutput, calls=%fused_computation.57 | convolution fusion | flops 10942414848 | bytes 41877504 | tf_op jit(solution)/shard_map/dot_general | solution.py:354
  717.6 18.9 %fusion.109 = f32[576,1536]{1,0:T(8,128)} fusion(bf16[576,6144]{1,0:T(8,128)(2,1)} %fusion.7, bf16[1536,6144]{1,0:T(8,128)(2,1)} %get-tuple-element.24), kind=kOutput, calls=%fused_computation.469 | convolution fusion | flops 10871635968 | bytes 29491200 | tf_op jit(solution)/shard_map/dot_general | solution.py:357
  741.9 23.4 %multiply_reduce_fusion.48 = (f32[1536]{0:T(1024)}, f32[1536]{0:T(1024)}, f32[1536]{0:T(1024)}, f32[1536]{0:T(1024)}, f32[1536]{0:T(1024)}, /*index=5*/f32[1536]...) fusion(f32[1,24,24,1536]{3,2,1,0:T(8,128)} %convert_element_typ, ...), kind=kLoop, calls=%fused_computation.144 | loop fusion | flops 30061056 | bytes 16020480 | tf_op jit(solution)/shard_map/transpose(jvp())/reduce_sum | solution.py:126
  765.7 20.2 %broadcast_multiply_fusion.1 = (f32[1,24,24,1536]{3,2,1,0:T(8,128)}, f32[1,24,24,1536]{3,2,1,0:T(8,128)}, f32[1,24,24,1536]{3,2,1,0:T(8,128)}, f32[1,24,24,1536]...) fusion(f32[1,24,24,1536]{3,2,1,0:T(8,128)S(1)} %get-tuple-eleme, ...), kind=kLoop, calls=%fused_computation.211 | loop fusion | flops 15925248 | bytes 67350528 | tf_op jit(solution)/shard_map/transpose(jvp())/mul | solution.py:126
  786.1 21.3 %broadcast_multiply_fusion = (f32[1,24,24,1536]{3,2,1,0:T(8,128)}, f32[1,24,24,1536]{3,2,1,0:T(8,128)}, f32[1,24,24,1536]{3,2,1,0:T(8,128)}, f32[1,24,24,1536]{3...) fusion(f32[1,24,24,1536]{3,2,1,0:T(8,128)S(1)} %get-tuple-eleme, ...), kind=kLoop, calls=%fused_computation.210 | loop fusion | flops 15925248 | bytes 67350528 | tf_op jit(solution)/shard_map/transpose(jvp())/mul | solution.py:126
  807.7 10.0 multiply_reduce_fusion.49
  820.1 26.3 %multiply_reduce_fusion.50 = (f32[1536]{0:T(1024)S(1)}, f32[1536]{0:T(1024)S(1)}, f32[1536]{0:T(1024)S(1)}, f32[1536]{0:T(1024)S(1)}, f32[1536]{0:T(1024)S(1)}, ...) fusion(f32[1,24,24,1536]{3,2,1,0:T(8,128)S(1)} %copy-done.3, ...), kind=kLoop, calls=%fused_computation.146 | loop fusion | flops 31822848 | bytes 7188480 | tf_op jit(solution)/shard_map/transpose(jvp())/reduce_sum | solution.py:126
  850.6 16.7 %convolution_convert_fusion = bf16[3072,1536]{1,0:T(8,128)(2,1)} fusion(bf16[576,3072]{1,0:T(8,128)(2,1)S(1)} %bitcast.232, bf16[576,3072]{1,0:T(8,128)(2,1)S(1)} %bitcast.231, bf16[576,1536]{1,0:T(8,128)(2,1)} %collective-permute-done.13, bf16[576,1536]{1,0:T(8,128)(2,1)} %get-tuple-element.178), kind=kOutput, calls=%fused_computation.63 | convolution fusion | flops 10897588224 | bytes 20054016 | tf_op jit(solution)/shard_map/dot_general | solution.py:165
  885.7 15.5 %broadcast_multiply_fusion.2 = (f32[1,24,24,1536]{3,2,1,0:T(8,128)}, f32[1,24,24,1536]{3,2,1,0:T(8,128)}, f32[1,24,24,1536]{3,2,1,0:T(8,128)}, f32[1,24,24,1536]...) fusion(f32[1,24,24,1536]{3,2,1,0:T(8,128)S(1)} %copy-done.3, ...), kind=kLoop, calls=%fused_computation.212 | loop fusion | flops 11501568 | bytes 49625088 | tf_op jit(solution)/shard_map/transpose(jvp())/mul | solution.py:126
  901.2 54.9 %collective-permute-done.16 = bf16[4,2,192,768]{3,2,1,0:T(8,128)(2,1)} collective-permute-done((bf16[4,2,192,768]{3,2,1,0:T(8,128)(2,1)}, bf16[4,2,192,768]{3,2,1,0:T(8,128)(2,1)}, u32[]{:S(2)}, u32[]{:S(2)}) %collective-permute-start.16) | collective-permute-done | bytes 2359328 | tf_op jit(solution)/shard_map/ppermute | solution.py:146
  966.4 18.6 %fusion.12 = bf16[768,6144]{1,0:T(8,128)(2,1)} fusion(bf16[576,6144]{1,0:T(8,128)(2,1)} %collective-permute-done.1, bf16[576,6144]{1,0:T(8,128)(2,1)} %fusion.7, bf16[576,768]{0,1:T(8,128)(2,1)} %bitcast.40, bf16[576,768]{0,1:T(8,128)(2,1)S(1)} %bitcast.242), kind=kOutput, calls=%fused_computation.64 | convolution fusion | flops 10908205056 | bytes 25362432 | tf_op jit(solution)/shard_map/dot_general | solution.py:165
  997.3 50.2 %pad_add_fusion = f32[1,30,30,1536]{3,2,1,0:T(8,128)} fusion(f32[1,24,24,1536]{3,2,1,0:T(8,128)} %get-tuple-element.186, f32[1,24,24,1536]{3,2,1,0:T(8,128)} %get-tuple-element.187, f32[1,24,24,1536]{3,2,1,0:T(8,128)} %get-tuple-element.188, f32[1,24,24,1536]{3,2,1,0:T(8,128)} %get-tuple-element.189, f32[1,24,24,1536]{3,2,1,0:T(8,128)} %get-tuple-element.190, ...), kind=kLoop, calls=%fused_computation.71 | loop fusion | flops 58060800 | bytes 157704192 | tf_op jit(solution)/shard_map/transpose(jvp())/add_any | solution.py:123
  1068.3 14.9 %collective-permute-done.18 = bf16[192,1536]{1,0:T(8,128)(2,1)S(1)} collective-permute-done((bf16[192,1536]{1,0:T(8,128)(2,1)S(1)}, bf16[192,1536]{1,0:T(8,128)(2,1)S(1)}, u32[]{:S(2)}, u32[]{:S(2)}) %collective-permute-start.18) | collective-permute-done | bytes 589856 | tf_op jit(solution)/shard_map/ppermute | solution.py:146
  1083.2 17.6 %collective-permute-done.19 = bf16[192,1536]{1,0:T(8,128)(2,1)S(1)} collective-permute-done((bf16[192,1536]{1,0:T(8,128)(2,1)S(1)}, bf16[192,1536]{1,0:T(8,128)(2,1)S(1)}, u32[]{:S(2)}, u32[]{:S(2)}) %collective-permute-start.19) | collective-permute-done | bytes 589856 | tf_op jit(solution)/shard_map/ppermute | solution.py:146
  1107.2 11.2 collective-permute-start.6
  1129.0 61.8 %all-reduce.118 = (f32[1024]{0:T(1024)}, f32[1024]{0:T(1024)}, f32[9,1024]{1,0:T(8,128)}, f32[1024]{0:T(1024)}, f32[1536]{0:T(1024)}, /*index=5*/f32[1536]{0:T(1024)}) all-reduce(f32[1024]{0:T(1024)} %get-tuple-element.92, f32[1024]{0:T(1024)S(1)} %copy-done.150, ...), channel_id=1, replica_groups=mesh['path'=4,'dev'=8] {'path','dev'}, use_global_device_ids=true, to_apply=%region_17.18 | all-reduce | flops 15360 | bytes 122880 | tf_op jit(solution)/shard_map/psum | solution.py:372
  1201.2 10.7 collective-permute-done.11
  1211.8 10.3 collective-permute-done.10
  (610 shorter events, 332.0 us)
Async XLA Ops:
  8.4 417.7 %all-to-all-start = ((s32[4,1,1]{2,1,0:T(1,128)}), s32[4,1,1]{2,1,0:T(1,128)}, u32[]{:S(2)}, u32[]{:S(2)}) async-start(s32[4,1,1]{2,1,0:T(1,128)} %broadcast_in_dim.232), calls=%async_computation | async-start | bytes 4096 | tf_op jit(solution)/shard_map/all_to_all | solution.py:253
  444.5 373.3 %reduce-scatter.8.cloned.1.call-start = ((), (), s32[]{:S(2)}) async-start(), calls=%async_computation.11 | async-start | bytes 2359296 | tf_op jit(solution)/shard_map/reduce_scatter | solution.py:198
  491.5 326.3 %reduce-scatter.14.cloned.1.call-start = ((), (), s32[]{:S(2)}) async-start(), calls=%async_computation.14 | async-start | bytes 3538944 | tf_op jit(solution)/shard_map/reduce_scatter | solution.py:198
  509.7 308.0 %reduce-scatter.6.cloned.1.call-start = ((), (), s32[]{:S(2)}) async-start(), calls=%async_computation.10 | async-start | bytes 7077888 | tf_op jit(solution)/shard_map/reduce_scatter | solution.py:198
  515.6 302.2 %reduce-scatter.12.cloned.1.call-start = ((), (), s32[]{:S(2)}) async-start(), calls=%async_computation.13 | async-start | bytes 9437184 | tf_op jit(solution)/shard_map/reduce_scatter | solution.py:198
  542.5 423.9 %collective-permute-start = (bf16[576,4,192]{0,2,1:T(8,128)(2,1)}, bf16[576,4,192]{0,2,1:T(8,128)(2,1)}, u32[]{:S(2)}, u32[]{:S(2)}) collective-permute-start(bf16[576,4,192]{0,2,1:T(8,128)(2,1)} %bitcast.39), channel_id=1, source_target_pairs={{0,1},{1,0},{2,3},{3,2},{4,5},{5,4},{6,7},{7,6},{8,9},{9,8},{10,11... | collective-permute-start | bytes 2654216 | tf_op jit(solution)/shard_map/ppermute | solution.py:146
  626.6 220.7 %collective-permute-start.12 = (bf16[576,4,768]{2,0,1:T(8,128)(2,1)}, bf16[576,4,768]{2,0,1:T(8,128)(2,1)}, u32[]{:S(2)}, u32[]{:S(2)}) collective-permute-start(bf16[576,4,768]{2,0,1:T(8,128)(2,1)} %bitcast.211), channel_id=1, source_target_pairs={{0,1},{1,0},{2,3},{3,2},{4,5},{5,4},{6,7},{7,6},{8,9},{9,8},{10,11... | collective-permute-start | bytes 10616840 | tf_op jit(solution)/shard_map/ppermute | solution.py:146
  652.2 166.3 %reduce-scatter.10.cloned.1.call-start = ((), (), s32[]{:S(2)}) async-start(), calls=%async_computation.12 | async-start | bytes 9437184 | tf_op jit(solution)/shard_map/reduce_scatter | solution.py:198
  670.7 555.5 %all-reduce.125.cloned.1.call-start = ((), (), s32[]{:S(2)}) async-start(), calls=%async_computation.16 | async-start | bytes 7077888 | tf_op jit(solution)/shard_map/psum | solution.py:199
  692.3 157.9 %collective-permute-start.13 = (bf16[576,1536]{1,0:T(8,128)(2,1)}, bf16[576,1536]{1,0:T(8,128)(2,1)}, u32[]{:S(2)}, u32[]{:S(2)}) collective-permute-start(bf16[576,1536]{1,0:T(8,128)(2,1)} %get-tuple-element.178), channel_id=1, source_target_pairs={{0,1},{1,0},{2,3},{3,2},{4,5},{5,4},{6,7},{7,6},{8,9},{9,8},{10,11... | collective-permute-start | bytes 5308424 | tf_op jit(solution)/shard_map/ppermute | solution.py:146
  717.0 249.4 %collective-permute-start.1 = (bf16[576,6144]{1,0:T(8,128)(2,1)}, bf16[576,6144]{1,0:T(8,128)(2,1)}, u32[]{:S(2)}, u32[]{:S(2)}) collective-permute-start(bf16[576,6144]{1,0:T(8,128)(2,1)} %fusion.7), channel_id=1, source_target_pairs={{0,1},{1,0},{2,3},{3,2},{4,5},{5,4},{6,7},{7,6},{8,9},{9,8},{10,11... | collective-permute-start | bytes 21233672 | tf_op jit(solution)/shard_map/ppermute | solution.py:146
  818.6 417.1 %all-reduce.123.cloned.1.call-start = ((), (), s32[]{:S(2)}) async-start(), calls=%async_computation.15 | async-start | bytes 688128 | tf_op jit(solution)/shard_map/psum | solution.py:372
  877.9 78.1 %collective-permute-start.16 = (bf16[4,2,192,768]{3,2,1,0:T(8,128)(2,1)}, bf16[4,2,192,768]{3,2,1,0:T(8,128)(2,1)}, u32[]{:S(2)}, u32[]{:S(2)}) collective-permute-start(bf16[4,2,192,768]{3,2,1,0:T(8,128)(2,1)} %dynamic-slice_bitcast_fusion), channel_id=1, source_target_pairs={{0,16},{8,24},{16,0},{24,8},{1,17},{9,25},{17,1},{25,9},{2,18},{10... | collective-permute-start | bytes 7077896 | tf_op jit(solution)/shard_map/ppermute | solution.py:146
  885.0 76.6 %collective-permute-start.14 = (bf16[4,2,192,768]{3,2,0,1:T(8,128)(2,1)}, bf16[4,2,192,768]{3,2,0,1:T(8,128)(2,1)}, u32[]{:S(2)}, u32[]{:S(2)}) collective-permute-start(bf16[4,2,192,768]{3,2,0,1:T(8,128)(2,1)} %bitcast.212), channel_id=1, source_target_pairs={{0,8},{8,0},{16,24},{24,16},{1,9},{9,1},{17,25},{25,17},{2,10},{10... | collective-permute-start | bytes 7077896 | tf_op jit(solution)/shard_map/ppermute | solution.py:146
  960.2 91.1 %collective-permute-start.17 = (bf16[4,192,768]{2,1,0:T(8,128)(2,1)}, bf16[4,192,768]{2,1,0:T(8,128)(2,1)}, u32[]{:S(2)}, u32[]{:S(2)}) collective-permute-start(bf16[4,192,768]{2,1,0:T(8,128)(2,1)} %dynamic-slice_bitcast_fusion.2), channel_id=1, source_target_pairs={{0,8},{8,0},{16,24},{24,16},{1,9},{9,1},{17,25},{25,17},{2,10},{10... | collective-permute-start | bytes 3538952 | tf_op jit(solution)/shard_map/ppermute | solution.py:146
  965.9 87.5 %collective-permute-start.15 = (bf16[4,192,768]{2,1,0:T(8,128)(2,1)}, bf16[4,192,768]{2,1,0:T(8,128)(2,1)}, u32[]{:S(2)}, u32[]{:S(2)}) collective-permute-start(bf16[4,192,768]{2,1,0:T(8,128)(2,1)} %dynamic-slice_bitcast_fusion.3), channel_id=1, source_target_pairs={{0,16},{8,24},{16,0},{24,8},{1,17},{9,25},{17,1},{25,9},{2,18},{10... | collective-permute-start | bytes 3538952 | tf_op jit(solution)/shard_map/ppermute | solution.py:146
  995.2 65.2 %collective-permute-start.4 = (bf16[4,2,48,3072]{3,2,1,0:T(8,128)(2,1)}, bf16[4,2,48,3072]{3,2,1,0:T(8,128)(2,1)}, u32[]{:S(2)}, u32[]{:S(2)}) collective-permute-start(bf16[4,2,48,3072]{3,2,1,0:T(8,128)(2,1)} %dynamic-slice_bitcast_fusion.1), channel_id=1, source_target_pairs={{0,16},{8,24},{16,0},{24,8},{1,17},{9,25},{17,1},{25,9},{2,18},{10... | collective-permute-start | bytes 7077896 | tf_op jit(solution)/shard_map/ppermute | solution.py:146
  996.7 68.1 %collective-permute-start.2 = (bf16[4,2,48,3072]{3,2,0,1:T(8,128)(2,1)}, bf16[4,2,48,3072]{3,2,0,1:T(8,128)(2,1)}, u32[]{:S(2)}, u32[]{:S(2)}) collective-permute-start(bf16[4,2,48,3072]{3,2,0,1:T(8,128)(2,1)} %bitcast.213), channel_id=1, source_target_pairs={{0,8},{8,0},{16,24},{24,16},{1,9},{9,1},{17,25},{25,17},{2,10},{10... | collective-permute-start | bytes 7077896 | tf_op jit(solution)/shard_map/ppermute | solution.py:146
  1057.4 43.4 %collective-permute-start.19 = (bf16[192,1536]{1,0:T(8,128)(2,1)S(1)}, bf16[192,1536]{1,0:T(8,128)(2,1)S(1)}, u32[]{:S(2)}, u32[]{:S(2)}) collective-permute-start(bf16[192,1536]{1,0:T(8,128)(2,1)S(1)} %get-tuple-element.233), channel_id=1, source_target_pairs={{0,4},{1,5},{2,6},{3,7},{4,0},{5,1},{6,2},{7,3},{8,12},{9,13},{10,... | collective-permute-start | bytes 1769480 | tf_op jit(solution)/shard_map/ppermute | solution.py:146
  1102.5 88.3 %collective-permute-start.22 = (bf16[192,1536]{1,0:T(8,128)(2,1)S(1)}, bf16[192,1536]{1,0:T(8,128)(2,1)}, u32[]{:S(2)}, u32[]{:S(2)}) collective-permute-start(bf16[192,1536]{1,0:T(8,128)(2,1)S(1)} %fusion.48), channel_id=1, source_target_pairs={{0,16},{8,24},{16,0},{24,8},{1,17},{9,25},{17,1},{25,9},{2,18},{10... | collective-permute-start | bytes 1769480 | tf_op jit(solution)/shard_map/ppermute | solution.py:146
  1104.0 86.8 %collective-permute-start.21 = (bf16[192,1536]{1,0:T(8,128)(2,1)S(1)}, bf16[192,1536]{1,0:T(8,128)(2,1)}, u32[]{:S(2)}, u32[]{:S(2)}) collective-permute-start(bf16[192,1536]{1,0:T(8,128)(2,1)S(1)} %fusion.48), channel_id=1, source_target_pairs={{0,8},{8,0},{16,24},{24,16},{1,9},{9,1},{17,25},{25,17},{2,10},{10... | collective-permute-start | bytes 1769480 | tf_op jit(solution)/shard_map/ppermute | solution.py:146
  1107.2 85.4 %collective-permute-start.6 = (bf16[48,6144]{1,0:T(8,128)(2,1)}, bf16[48,6144]{1,0:T(8,128)(2,1)}, u32[]{:S(2)}, u32[]{:S(2)}) collective-permute-start(bf16[48,6144]{1,0:T(8,128)(2,1)} %get-tuple-element.239), channel_id=1, source_target_pairs={{0,2},{1,3},{2,0},{3,1},{4,6},{5,7},{6,4},{7,5},{8,10},{9,11},{10,... | collective-permute-start | bytes 1769480 | tf_op jit(solution)/shard_map/ppermute | solution.py:146
  1118.4 74.2 %collective-permute-start.7 = (bf16[48,6144]{1,0:T(8,128)(2,1)}, bf16[48,6144]{1,0:T(8,128)(2,1)}, u32[]{:S(2)}, u32[]{:S(2)}) collective-permute-start(bf16[48,6144]{1,0:T(8,128)(2,1)} %get-tuple-element.240), channel_id=1, source_target_pairs={{0,4},{1,5},{2,6},{3,7},{4,0},{5,1},{6,2},{7,3},{8,12},{9,13},{10,... | collective-permute-start | bytes 1769480 | tf_op jit(solution)/shard_map/ppermute | solution.py:146
  1120.1 72.5 %collective-permute-start.8 = (bf16[48,6144]{1,0:T(8,128)(2,1)}, bf16[48,6144]{1,0:T(8,128)(2,1)}, u32[]{:S(2)}, u32[]{:S(2)}) collective-permute-start(bf16[48,6144]{1,0:T(8,128)(2,1)} %get-tuple-element.241), channel_id=1, source_target_pairs={{0,6},{1,7},{2,4},{3,5},{4,2},{5,3},{6,0},{7,1},{8,14},{9,15},{10,... | collective-permute-start | bytes 1769480 | tf_op jit(solution)/shard_map/ppermute | solution.py:146
  (187 other events, 3039.3 us)
Sparse Core Ops, SparseCore 0:
  491.6 33.8 reduce-scatter.7
  527.8 39.0 reduce-scatter.13
  569.2 69.0 reduce-scatter.5
  640.4 87.9 reduce-scatter.11
  730.5 87.9 reduce-scatter.9
  822.2 118.9 all-reduce.124
  947.1 136.5 all-reduce.122

commit v2 on v1

--- a/solution.py
+++ b/solution.py
@@ -9,6 +9,73 @@
 
 HEAD_DIM = 64
 MESH = pl.DeviceIdType.MESH
+VMEM = pltpu.VMEM
+SIDE, REACH, EDGE, GROUP, LANES = 7, 3, 8, 8, 128
+
+
+def conv_rows(src, taps, group, flip, side):
+    base = group * GROUP
+    sums = [None] * GROUP
+    for dc in range(SIDE):
+        col = [taps((SIDE - 1 - dr) * SIDE + SIDE - 1 - dc if flip else dr * SIDE + dc) for dr in range(SIDE)]
+        for j in range(GROUP + SIDE - 1):
+            row = src[base + j, EDGE - REACH + dc : EDGE - REACH + dc + side, :]
+            for r in range(GROUP):
+                if 0 <= j - r < SIDE:
+                    term = row * col[j - r]
+                    sums[r] = term if sums[r] is None else sums[r] + term
+    return sums
+
+
+def clear_edges(pad, side):
+    rows, columns, lanes = pad.shape[-3:]
+    pad[:, :EDGE, :] = jnp.zeros((rows, EDGE, lanes), jnp.float32)
+    pad[:, EDGE + side :, :] = jnp.zeros((rows, columns - EDGE - side, lanes), jnp.float32)
+    pad[:REACH] = jnp.zeros((REACH, columns, lanes), jnp.float32)
+    pad[REACH + side :] = jnp.zeros((rows - REACH - side, columns, lanes), jnp.float32)
+
+
+def lane_block(block):
+    return pl.ds(pl.multiple_of(block * LANES, LANES), LANES)
+
+
+def mix_block(block, maps, taps, mixed, pad):
+    side = maps.shape[0]
+    at = lane_block(block)
+    pad[REACH : REACH + side, EDGE : EDGE + side, :] = maps[:, :, at].astype(jnp.float32)
+
+    def rows(group, carry):
+        sums = conv_rows(pad, lambda t: taps[pl.ds(t, 1), at], group, False, side)
+        for r in range(GROUP):
+            mixed[group * GROUP + r, :, at] = sums[r]
+        return carry
+
+    lax.fori_loop(0, side // GROUP, rows, 0)
+
+
+def norm_rows(h, mixed, gain, rows):
+    v = mixed[h]
+    centred = v - jnp.mean(v, axis=-1, keepdims=True)
+    scale = lax.rsqrt(jnp.mean(centred * centred, axis=-1, keepdims=True) + 1e-06)
+    rows[h] = (centred * scale * gain[...]).astype(jnp.bfloat16)
+
+
+def section_forward_kernel(maps, taps, gain, mixed, rows, pad):
+    side, _, channels = maps.shape
+    clear_edges(pad, side)
+
+    def blocks(block, carry):
+        mix_block(block, maps, taps, mixed, pad)
+        return carry
+
+    lax.fori_loop(0, channels // LANES, blocks, 0)
+
+    def norm(h, carry):
+        norm_rows(h, mixed, gain, rows)
+        return carry
+
+    lax.fori_loop(0, side, norm, 0)
+
 
 def gather_jobs(shapes):
     jobs = []
@@ -22,8 +89,10 @@
     return jobs
 
 def gather_kernel(jobs, count, *refs):
-    shards = refs[:count]; fulls = refs[count:2*count]
-    zs, zr, ps, pr, cs, cr, ls = refs[2*count:]
+    shards = refs[:count]
+    maps, taps, gain = refs[count : count + 3]
+    fulls = refs[count + 3 : 2 * count + 3]
+    mixed, rows_out, pad, zs, zr, ps, pr, cs, cr, ls = refs[2 * count + 3 :]
     p = lax.axis_index("path"); d = lax.axis_index("dev")
     masks = [(0,1),(0,2),(0,4),(0,6),(1,0),(2,0)]
     def at(m): return (p ^ m[0], d ^ m[1])
@@ -63,9 +132,10 @@
         return copy(ref, ref, cs.at[w,1+k], cr.at[w,1+k], (0,1))
     last = {}
     for i,(w,*_) in enumerate(jobs): last[w] = i
-    AHEAD = 2
+    AHEAD = 3
     for i in range(min(AHEAD, J)):
         for k in range(3): Z(i,k).start()
+    section_forward_kernel(maps, taps, gain, mixed, rows_out, pad)
     sent = []
     for i in range(J + 2):
         if i < J:
@@ -92,19 +162,296 @@
             Z(i,k).wait_send()
             for a in range(2): XY(i,k,a).wait_send(); DG(i,k,a).wait_send()
 
-def gather_weights(shards, collective_id=0):
+def gather_weights(shards, maps, taps, gain):
     shapes = [s.shape for s in shards]
-    jobs = gather_jobs(shapes); n = len(shards); J = len(jobs)
-    anyspec = pl.BlockSpec(memory_space=pl.ANY)
-    return pl.pallas_call(
+    jobs = gather_jobs(shapes)
+    n, J = len(shards), len(jobs)
+    side, _, channels = maps.shape
+    anyspec, whole = pl.BlockSpec(memory_space=pl.ANY), pl.BlockSpec(memory_space=VMEM)
+    dma = pltpu.SemaphoreType.DMA
+    results = pl.pallas_call(
         functools.partial(gather_kernel, jobs, n),
-        out_shape=[jax.ShapeDtypeStruct((8*r, c), jnp.bfloat16) for r, c in shapes],
-        in_specs=[anyspec]*n, out_specs=[anyspec]*n,
-        scratch_shapes=[pltpu.SemaphoreType.DMA((J,3)),pltpu.SemaphoreType.DMA((J,3)),
-            pltpu.SemaphoreType.DMA((J,3,4)),pltpu.SemaphoreType.DMA((J,3,4)),
-            pltpu.SemaphoreType.DMA((n,4)),pltpu.SemaphoreType.DMA((n,4)),pltpu.SemaphoreType.DMA((n,))],
-        compiler_params=pltpu.CompilerParams(collective_id=collective_id, has_side_effects=True),
-    )(*shards)
+        out_shape=[jax.ShapeDtypeStruct((8 * r, c), jnp.bfloat16) for r, c in shapes]
+        + [jax.ShapeDtypeStruct(maps.shape, jnp.float32), jax.ShapeDtypeStruct(maps.shape, jnp.bfloat16)],
+        in_specs=[anyspec] * n + [whole] * 3,
+        out_specs=[anyspec] * n + [whole] * 2,
+        scratch_shapes=[VMEM((side + 2 * REACH, side + 2 * EDGE, LANES), jnp.float32)]
+        + [dma((J, 3)), dma((J, 3)), dma((J, 3, 4)), dma((J, 3, 4)), dma((n, 4)), dma((n, 4)), dma((n,))],
+        compiler_params=pltpu.CompilerParams(
+            collective_id=0, has_side_effects=True, vmem_limit_bytes=40 * 2**20
+        ),
+    )(*shards, maps, taps, gain.reshape(1, channels))
+    return results[:n], results[n], results[n + 1]
+
+
+def add_block(total, term):
+    return (total.astype(jnp.float32) + term.astype(jnp.float32)).astype(jnp.bfloat16)
+
+
+def scatter_kernel(
+    big0, big1, t0, t1, t2, t3, small_in, grad_normed, mixed, maps, taps, gain,
+    grad_maps, small_out, o0, o1, o2, o3, o4, o5, land0a, land0b, land1a, land1b,
+    acc0a, acc0b, acc1a, acc1b, two0a, two0b, two1a, two1b, tmp0, tmp1,
+    own0, own1, own2, own3, two0, two1, two2, two3,
+    zr0, zr1, zr2, zr3, zr4, zr5, low0, low1, low2, low3, low4, low5,
+    full0, full1, full2, full3, full4, full5,
+    small_at, small_from, pad, grad_pad, tap_sums, ssem, rsem, lsem,
+):
+    p, d = lax.axis_index("path"), lax.axis_index("dev")
+    up, across, height, side = p // 2, lax.rem(p, 2), d // 2, lax.rem(d, 2)
+    masks = [(0, 1), (0, 2), (0, 4), (0, 6), (1, 0), (2, 0), (3, 0)]
+    bar = pltpu.get_barrier_semaphore()
+    for m in masks:
+        pl.semaphore_signal(bar, inc=1, device_id=(p ^ m[0], d ^ m[1]), device_id_type=MESH)
+    pl.semaphore_wait(bar, len(masks))
+
+    copies = []
+
+    def send(src, dst, m):
+        n = len(copies)
+        copy = pltpu.make_async_remote_copy(
+            src, dst, ssem.at[n], rsem.at[n], device_id=(p ^ m[0], d ^ m[1]), device_id_type=MESH
+        )
+        copies.append(copy)
+        copy.start()
+        return copy
+
+    local = []
+
+    def fetch(src, dst):
+        copy = pltpu.make_async_copy(src, dst, lsem.at[len(local)])
+        local.append(copy)
+        copy.start()
+        return copy
+
+    thin = [(t0, own0, two0, True), (t1, own1, two1, False), (t2, own2, two2, True), (t3, own3, two3, False)]
+    wide = [
+        (big0, (acc0a, acc0b), (land0a, land0b), (two0a, two0b), tmp0),
+        (big1, (acc1a, acc1b), (land1a, land1b), (two1a, two1b), tmp1),
+    ]
+    outs = [o0, o1, o2, o3, o4, o5]
+    zrs, lows, wholes = [zr0, zr1, zr2, zr3, zr4, zr5], [low0, low1, low2, low3, low4, low5], [full0, full1, full2, full3, full4, full5]
+
+    def thin_two(i):
+        src, own, two, upward = thin[i]
+        index, mask = (up, (2, 0)) if upward else (across, (1, 0))
+        loaded = fetch(src.at[:, :, index], own)
+        return loaded, send(src.at[:, :, 1 - index], two, mask)
+
+    def wide_one(w):
+        src, acc, land, _, _ = wide[w]
+        half = src.shape[5] // 2
+        a, b = pl.ds(0, half), pl.ds(half, half)
+        return (
+            fetch(src.at[:, :, :, across, :, a], acc[0]),
+            fetch(src.at[:, :, up, :, :, b], acc[1]),
+            send(src.at[:, :, :, 1 - across, :, a], land[0], (1, 0)),
+            send(src.at[:, :, 1 - up, :, :, b], land[1], (2, 0)),
+        )
+
+    def wide_two(w, started):
+        src, acc, land, two, tmp = wide[w]
+        started[0].wait()
+        started[1].wait()
+        sent = []
+        for k in range(2):
+            started[2 + k].wait_recv()
+            loads = [fetch(land[k].at[0], tmp.at[0])]
+            for z in range(4):
+                if z < 3:
+                    loads.append(fetch(land[k].at[z + 1], tmp.at[(z + 1) % 2]))
+                loads[z].wait()
+                for c in range(2):
+                    for q in range(2):
+                        acc[k][z, c, q] = add_block(acc[k][z, c, q], tmp[z % 2, c, q])
+            index, mask = (up, (2, 0)) if k == 0 else (across, (1, 0))
+            sent.append(send(acc[k].at[:, :, 1 - index], two[k], mask))
+        return sent
+
+    def heights(n, parts):
+        zr = zrs[n]
+        half = zr.shape[3] // len(parts)
+        return [
+            send(part.at[height ^ m], zr.at[m - 1, :, :, pl.ds(k * half, half)], (0, 2 * m))
+            for m in (1, 2, 3)
+            for k, part in enumerate(parts)
+        ]
+
+    def thin_three(i, started):
+        _, own, two, _ = thin[i]
+        started[0].wait()
+        started[1].wait_recv()
+        for z in range(4):
+            for c in range(2):
+                two[z, c] = add_block(two[z, c], own[z, c])
+        return heights(i, [two])
+
+    def wide_three(w, sent):
+        _, acc, _, two, _ = wide[w]
+        for k in range(2):
+            index = up if k == 0 else across
+            sent[k].wait_recv()
+            for z in range(4):
+                for c in range(2):
+                    two[k][z, c] = add_block(two[k][z, c], acc[k][z, c, index])
+        return heights(4 + w, two)
+
+    def total(n, parts, sent):
+        for copy in sent:
+            copy.wait_recv()
+        zr, low, whole = zrs[n], lows[n], wholes[n]
+        half = zr.shape[3] // len(parts)
+        for k, part in enumerate(parts):
+            cols = slice(k * half, (k + 1) * half)
+            for c in range(2):
+                value = part[height, c].astype(jnp.float32)
+                for m in range(3):
+                    value = value + zr[m, c, :, cols].astype(jnp.float32)
+                low[c, :, cols] = value.astype(jnp.bfloat16)
+        whole[side] = low[side]
+        return send(low.at[1 - side], whole.at[side], (0, 1))
+
+    def spread(n, swapped):
+        swapped.wait_recv()
+        return [fetch(wholes[n], outs[n].at[p])] + [send(wholes[n], outs[n].at[p], (m, 0)) for m in (1, 2, 3)]
+
+    side_cells, _, channels = maps.shape
+    count = channels // LANES
+
+    def norm_back():
+        clear_edges(pad, side_cells)
+        clear_edges(grad_pad, side_cells)
+        small_at[0] = small_in[...]
+
+        def norm(h, carry):
+            v = mixed[h]
+            centred = v - jnp.mean(v, axis=-1, keepdims=True)
+            scale = lax.rsqrt(jnp.mean(centred * centred, axis=-1, keepdims=True) + 1e-06)
+            unit = centred * scale
+            grad = grad_normed[h]
+            small_at[0, SIDE * SIDE : SIDE * SIDE + 1, :] += jnp.sum(grad * unit, axis=0, keepdims=True)
+            grad = grad * gain[...]
+            grad_maps[h] = scale * (
+                grad - jnp.mean(grad, axis=-1, keepdims=True) - unit * jnp.mean(grad * unit, axis=-1, keepdims=True)
+            )
+            return carry
+
+        lax.fori_loop(0, side_cells, norm, 0)
+
+    def blocks(first, last):
+        def one(block, carry):
+            at = lane_block(block)
+            inside = (slice(REACH, REACH + side_cells), slice(EDGE, EDGE + side_cells), slice(None))
+            pad[inside] = maps[:, :, at].astype(jnp.float32)
+            grad_pad[inside] = grad_maps[:, :, at]
+            tap_sums[...] = jnp.zeros_like(tap_sums)
+
+            def rows(group, inner):
+                base = group * GROUP
+                sums = conv_rows(grad_pad, lambda t: taps[pl.ds(t, 1), at], group, True, side_cells)
+                for r in range(GROUP):
+                    grad_maps[base + r, :, at] = sums[r]
+                for dc in range(SIDE):
+                    grads = [grad_pad[base + REACH + r, EDGE : EDGE + side_cells, :] for r in range(GROUP)]
+                    acc = [None] * SIDE
+                    for j in range(GROUP + SIDE - 1):
+                        row = pad[base + j, EDGE - REACH + dc : EDGE - REACH + dc + side_cells, :]
+                        for r in range(GROUP):
+                            dr = j - r
+                            if 0 <= dr < SIDE:
+                                term = row * grads[r]
+                                acc[dr] = term if acc[dr] is None else acc[dr] + term
+                    for dr in range(SIDE):
+                        tap_sums[dr * SIDE + dc] += jnp.sum(acc[dr].reshape(side_cells // 8, 8, LANES), axis=0)
+                return inner
+
+            lax.fori_loop(0, side_cells // GROUP, rows, 0)
+            small_at[0, : SIDE * SIDE, at] = jnp.sum(tap_sums[...], axis=1)
+            return carry
+
+        lax.fori_loop(first, last, one, 0)
+
+    small_masks = [(0, 1), (1, 0), (2, 0), (0, 2), (0, 4)]
+
+    def small_send(s):
+        return send(small_at.at[s], small_from.at[s], small_masks[s])
+
+    def small_step(s, copy):
+        copy.wait_recv()
+        value = small_at[s] + small_from[s]
+        if s + 1 < len(small_masks):
+            small_at[s + 1] = value
+            return small_send(s + 1)
+        small_out[...] = value
+
+    thin_sent = [thin_two(i) for i in range(4)]
+    one_reduce = wide_one(0)
+    norm_back()
+    blocks(0, count // 2)
+    thin_high = [thin_three(0, thin_sent[0]), thin_three(1, thin_sent[1])]
+    one_expand = wide_one(1)
+    blocks(count // 2, 3 * count // 4)
+    thin_high += [thin_three(2, thin_sent[2]), thin_three(3, thin_sent[3])]
+    blocks(3 * count // 4, count)
+    small = small_send(0)
+    two_reduce = wide_two(0, one_reduce)
+    small = small_step(0, small)
+    swaps = [total(i, [thin[i][2]], thin_high[i]) for i in range(2)]
+    small = small_step(1, small)
+    high_reduce = wide_three(0, two_reduce)
+    two_expand = wide_two(1, one_expand)
+    small = small_step(2, small)
+    swaps += [total(i, [thin[i][2]], thin_high[i]) for i in (2, 3)]
+    last = [spread(i, swaps[i]) for i in range(4)]
+    high_expand = wide_three(1, two_expand)
+    small = small_step(3, small)
+    swap_reduce = total(4, wide[0][3], high_reduce)
+    last.append(spread(4, swap_reduce))
+    small = small_step(4, small)
+    swap_expand = total(5, wide[1][3], high_expand)
+    last.append(spread(5, swap_expand))
+    for group in last:
+        group[0].wait()
+        for copy in group[1:]:
+            copy.wait_recv()
+    for copy in copies:
+        copy.wait_send()
+
+
+def scatter_gradients(part_reduce, part_expand, thins, small, grad_normed, mixed, maps, taps, gain):
+    side, _, channels = maps.shape
+    low, full = jnp.bfloat16, jnp.float32
+    anyspec, whole = pl.BlockSpec(memory_space=pl.ANY), pl.BlockSpec(memory_space=VMEM)
+    dma = pltpu.SemaphoreType.DMA
+    finals = [(t.shape[3], t.shape[4]) for t in thins] + [w.shape[4:] for w in (part_reduce, part_expand)]
+    landing = []
+    scratch = []
+    for w in (part_reduce, part_expand):
+        shape = w.shape[:3] + (w.shape[4], w.shape[5] // 2)
+        landing += [jax.ShapeDtypeStruct(shape, low)] * 2
+        scratch += [VMEM(shape, low)] * 2
+    scratch += [VMEM(w.shape[:2] + (w.shape[4], w.shape[5] // 2), low) for w in (part_reduce, part_expand) for _ in range(2)]
+    scratch += [VMEM((2, 2, 2, w.shape[4], w.shape[5] // 2), low) for w in (part_reduce, part_expand)]
+    scratch += [VMEM(t.shape[:2] + t.shape[3:], low) for t in thins] * 2
+    scratch += [VMEM((3, 2) + f, low) for f in finals]
+    scratch += [VMEM((2,) + f, low) for f in finals] * 2
+    edge = (side + 2 * REACH, side + 2 * EDGE, LANES)
+    scratch += [VMEM((5,) + small.shape, full)] * 2
+    scratch += [VMEM(edge, full)] * 2 + [VMEM((SIDE * SIDE, 8, LANES), full)]
+    scratch += [dma((80,)), dma((80,)), dma((40,))]
+    results = pl.pallas_call(
+        scatter_kernel,
+        out_shape=[jax.ShapeDtypeStruct(maps.shape, full), jax.ShapeDtypeStruct(small.shape, full)]
+        + [jax.ShapeDtypeStruct((4, 2) + f, low) for f in finals]
+        + landing,
+        in_specs=[anyspec] * 6 + [whole] * 6,
+        out_specs=[whole] * 2 + [anyspec] * 10,
+        scratch_shapes=scratch,
+        compiler_params=pltpu.CompilerParams(
+            collective_id=1, has_side_effects=True, vmem_limit_bytes=60 * 2**20
+        ),
+    )(part_reduce, part_expand, *thins, small, grad_normed, mixed, maps, taps, gain.reshape(1, channels))
+    return results[0], results[1], results[2:8]
 
 
 def layer_norm(values, gain_vec):
@@ -135,12 +482,6 @@
     return depthwise(grid_field, grid_kernel, 3)
 
 
-def gather_all(shards, tuned):
-    if tuned:
-        return gather_weights(shards)
-    return [lax.all_gather(shard, "dev", axis=0, tiled=True) for shard in shards]
-
-
 def swap(value, axis, mask):
     size = lax.axis_size(axis)
     return lax.ppermute(value, axis, [(i, i ^ mask) for i in range(size)])
@@ -154,44 +495,47 @@
     return (left.astype(jnp.float32) + right.astype(jnp.float32)).astype(jnp.bfloat16)
 
 
+def place():
+    path, dev = lax.axis_index("path"), lax.axis_index("dev")
+    return path, path // 2, lax.rem(path, 2), dev // 2, lax.rem(dev, 2)
+
+
+def both_images(rows):
+    return jnp.concatenate([rows, swap(rows, "dev", 1)])
+
+
 def pair_gradient(rows, grads):
-    side = lax.rem(lax.axis_index("dev"), 2)
-    tokens, depth = rows.shape
-    split = rows.reshape(tokens, 4, 2, depth // 8)
-    mine = pick(split, side, 2)
-    theirs = swap(pick(split, 1 - side, 2), "dev", 1)
-    both_rows = jnp.concatenate([mine.reshape(tokens, depth // 2), theirs.reshape(tokens, depth // 2)])
-    both_grads = jnp.concatenate([grads, swap(grads, "dev", 1)])
+    side = place()[4]
+    half = grads.shape[1] // 2
+    low, high = grads[:, :half], grads[:, half:]
+    mine = jnp.where(side == 0, low, high)
+    theirs = swap(jnp.where(side == 0, high, low), "dev", 1)
     product = lax.dot_general(
-        both_rows, both_grads, (((0,), (0,)), ((), ())), preferred_element_type=jnp.float32
-    )
-    return product.astype(jnp.bfloat16).reshape(4, depth // 8, grads.shape[1])
-
-
-def plane_first(share):
-    path = lax.axis_index("path")
-    up, across = path // 2, lax.rem(path, 2)
-    height = lax.axis_index("dev") // 2
-    _, rows, columns = share.shape
-    view = share.reshape(4, 2, 2, rows // 4, columns)
-    left, right = view[..., : columns // 2], view[..., columns // 2 :]
-    left = add_low(pick(left, across, 2), swap(pick(left, 1 - across, 2), "path", 1))
-    right = add_low(pick(right, up, 1), swap(pick(right, 1 - up, 1), "path", 2))
-    left = add_low(pick(left, up, 1), swap(pick(left, 1 - up, 1), "path", 2))
-    right = add_low(pick(right, across, 1), swap(pick(right, 1 - across, 1), "path", 1))
-    quarter = jnp.concatenate([left, right], axis=-1)
-    total = pick(quarter, height, 0).astype(jnp.float32)
-    for mask in (1, 2, 3):
-        total = total + swap(pick(quarter, height ^ mask, 0), "dev", 2 * mask).astype(jnp.float32)
-    low = total.astype(jnp.bfloat16)
-    pieces = jnp.stack([low] + [swap(low, "path", mask) for mask in (1, 2, 3)])
-    order = jnp.arange(4, dtype=jnp.int32) ^ path
-    return jnp.concatenate([pick(pieces, order[i], 0) for i in range(4)]).astype(jnp.float32)
-
-
-def summed_gradient(rows, grads, tuned, plane):
-    if tuned and plane:
-        return plane_first(pair_gradient(rows, grads))
+        rows, jnp.concatenate([mine, theirs]), (((0,), (0,)), ((), ())), preferred_element_type=jnp.float32
+    )
+    return product.astype(jnp.bfloat16).reshape(4, 2, 2, 2, rows.shape[1] // 32, half)
+
+
+def across_sum(share, axis):
+    across = place()[2]
+    return add_low(pick(share, across, axis), swap(pick(share, 1 - across, axis), "path", 1))
+
+
+def up_sum(share, axis):
+    up = place()[1]
+    return add_low(pick(share, up, axis), swap(pick(share, 1 - up, axis), "path", 2))
+
+
+def tie(*values):
+    return lax.optimization_barrier(values)
+
+
+def finish(pieces):
+    parts, _, rows, half = pieces.shape
+    return jnp.moveaxis(pieces, 1, 2).reshape(parts * rows, 2 * half).astype(jnp.float32)
+
+
+def plain_sum(rows, grads):
     product = lax.dot_general(
         rows, grads, (((0,), (0,)), ((), ())), preferred_element_type=jnp.float32
     ).astype(jnp.bfloat16)
@@ -220,9 +564,14 @@
     layer_scale,
 ):
     tuned = lax.axis_size("path") == 4 and lax.axis_size("dev") == 8
-    full_expand, full_reduce, full_adapter, full_qkv, full_out, full_fc1, full_fc2 = gather_all(
-        (w_expand, w_reduce, w_adapter, w_qkv, w_out, w_fc1, w_fc2), tuned
-    )
+    weights = (w_expand, w_reduce, w_adapter, w_qkv, w_out, w_fc1, w_fc2)
+    if tuned:
+        fulls, section_mixed, section_normed = gather_weights(
+            weights, hires_maps[0], section_kernel, section_gain
+        )
+    else:
+        fulls = [lax.all_gather(shard, "dev", axis=0, tiled=True) for shard in weights]
+    full_expand, full_reduce, full_adapter, full_qkv, full_out, full_fc1, full_fc2 = fulls
     path_count = lax.axis_size("path")
     maps_float = hires_maps.astype(jnp.float32)
     map_side = maps_float.shape[1]
@@ -233,8 +582,9 @@
     model_width = inputs.shape[2]
     head_count = model_width // HEAD_DIM
     score_scale = HEAD_DIM ** (-0.5)
-    section_mixed, section_back = jax.vjp(section_depthwise, maps_float, section_kernel)
-    section_normed, section_norm_back = jax.vjp(layer_norm, section_mixed, section_gain)
+    if not tuned:
+        section_mixed, section_back = jax.vjp(section_depthwise, maps_float, section_kernel)
+        section_normed, section_norm_back = jax.vjp(layer_norm, section_mixed, section_gain)
     section_rows = section_normed.reshape(-1, channels).astype(jnp.bfloat16)
     expanded = jnp.dot(section_rows, full_expand, preferred_element_type=jnp.float32)
     activated, section_gelu_back = jax.vjp(jax.nn.gelu, expanded)
@@ -294,15 +644,24 @@
     result = (hidden_mid + lowered)[None].astype(jnp.bfloat16)
     grad_out = cotangent[0].astype(jnp.float32)
     grad_out_low = grad_out.astype(jnp.bfloat16)
-    grad_fc2_w = summed_gradient(lifted, grad_out_low, tuned, False)
+    if tuned:
+        part_fc2 = pair_gradient(both_images(lifted), grad_out_low)
+    else:
+        grad_fc2_w = plain_sum(lifted, grad_out_low)
     grad_lifted = jnp.dot(grad_out_low, full_fc2.T, preferred_element_type=jnp.float32)
     grad_raised = gelu_back(grad_lifted)[0].astype(jnp.bfloat16)
-    grad_fc1_w = summed_gradient(mlp_rows, grad_raised, tuned, False)
+    if tuned:
+        part_fc1 = pair_gradient(both_images(mlp_rows), grad_raised)
+    else:
+        grad_fc1_w = plain_sum(mlp_rows, grad_raised)
     grad_normed_two = jnp.dot(grad_raised, full_fc1.T, preferred_element_type=jnp.float32)
     grad_mid_norm, grad_mlp_gain = norm_two_back(grad_normed_two)
     grad_mid = grad_out + grad_mid_norm
     grad_attended = grad_mid.astype(jnp.bfloat16)
-    grad_out_w = summed_gradient(attn_mixed, grad_attended, tuned, False)
+    if tuned:
+        part_out = pair_gradient(both_images(attn_mixed), grad_attended)
+    else:
+        grad_out_w = plain_sum(attn_mixed, grad_attended)
     grad_mixed = jnp.dot(grad_attended, full_out.T, preferred_element_type=jnp.float32)
     grad_mixed = grad_mixed.astype(jnp.bfloat16).reshape(tokens, head_count, HEAD_DIM)
     grad_probs = jnp.einsum("thd,shd->hts", grad_mixed, values, preferred_element_type=jnp.float32)
@@ -327,7 +686,10 @@
         ],
         axis=1,
     ).astype(jnp.bfloat16)
-    grad_qkv_w = summed_gradient(attn_rows, grad_projected, tuned, False)
+    if tuned:
+        part_qkv = pair_gradient(both_images(attn_rows), grad_projected)
+    else:
+        grad_qkv_w = plain_sum(attn_rows, grad_projected)
     grad_normed_one = jnp.dot(grad_projected, full_qkv.T, preferred_element_type=jnp.float32)
     grad_in_norm, grad_attn_gain = norm_one_back(grad_normed_one)
     grad_in = grad_mid + grad_in_norm
@@ -335,7 +697,10 @@
     grad_spread = (grad_in * gate_factor).reshape(1, grid_side, grid_side, model_width)
     grad_adapted, grad_adapter_taps = adapter_back(grad_spread)
     grad_adapted_low = grad_adapted.reshape(tokens, model_width).astype(jnp.bfloat16)
-    grad_adapter_w = summed_gradient(features, grad_adapted_low, tuned, False)
+    if tuned:
+        part_adapter = pair_gradient(both_images(features), grad_adapted_low)
+    else:
+        grad_adapter_w = plain_sum(features, grad_adapted_low)
     grad_features = jnp.dot(grad_adapted_low, full_adapter.T, preferred_element_type=jnp.float32)
     grad_pieces = grad_features.astype(jnp.bfloat16).reshape(path_count, quarter_rows, channels)
     grad_routed = lax.all_to_all(grad_pieces, "path", split_axis=0, concat_axis=0, tiled=True)
@@ -343,6 +708,10 @@
         jnp.bfloat16
     )
     grad_home = lax.all_to_all(grad_unrouted, "path", split_axis=0, concat_axis=0, tiled=True)
+    if tuned:
+        step_fc2, step_fc1 = across_sum(part_fc2, 3), up_sum(part_fc1, 2)
+        step_qkv = across_sum(part_qkv, 3)
+        step_rest = up_sum(jnp.concatenate([part_out, part_adapter], axis=4), 2)
     grad_pooled = grad_home.astype(jnp.float32).reshape(tokens, channels)
     quarter = (grad_pooled * 0.25).reshape(1, grid_side, 1, grid_side, 1, channels)
     grad_section_out = jnp.broadcast_to(quarter, (1, grid_side, 2, grid_side, 2, channels)).reshape(
@@ -350,16 +719,51 @@
     )
     grad_scale = jnp.sum((grad_section_out * reduced).reshape(-1, channels), axis=0)
     grad_reduced = (grad_section_out * layer_scale).reshape(-1, channels).astype(jnp.bfloat16)
-    grad_reduce_w = summed_gradient(activated_low, grad_reduced, tuned, True)
+    if tuned:
+        part_reduce = pair_gradient(both_images(activated_low), grad_reduced)
+    else:
+        grad_reduce_w = plain_sum(activated_low, grad_reduced)
     grad_activated = jnp.dot(grad_reduced, full_reduce.T, preferred_element_type=jnp.float32)
     grad_expanded = section_gelu_back(grad_activated)[0].astype(jnp.bfloat16)
-    grad_expand_w = summed_gradient(section_rows, grad_expanded, tuned, True)
+    if tuned:
+        grad_expanded, part_reduce, step_fc2, step_fc1 = tie(grad_expanded, part_reduce, step_fc2, step_fc1)
+    if tuned:
+        part_expand = pair_gradient(both_images(section_rows), grad_expanded)
+    else:
+        grad_expand_w = plain_sum(section_rows, grad_expanded)
     grad_section_normed = jnp.dot(
         grad_expanded, full_expand.T, preferred_element_type=jnp.float32
     ).reshape(maps_float.shape)
-    grad_section_mixed, grad_section_gain = section_norm_back(grad_section_normed)
-    grad_maps_conv, grad_section_taps = section_back(grad_section_mixed)
-    grad_maps = grad_section_out + grad_maps_conv
+    if tuned:
+        small_rows = jnp.concatenate(
+            [
+                jnp.zeros((section_kernel.shape[0] + 1, channels), jnp.float32),
+                jnp.concatenate([grad_attn_gain, grad_mlp_gain, grad_merge, grad_adapter_taps.reshape(-1)]).reshape(-1, channels),
+                grad_scale[None],
+            ]
+        )
+        small_count = small_rows.shape[0]
+        small_rows = jnp.pad(small_rows, ((0, -small_count % 8), (0, 0)))
+        grad_maps, small_rows, pieces = scatter_gradients(
+            part_reduce,
+            part_expand,
+            [step_fc2, step_fc1, step_qkv, step_rest],
+            small_rows,
+            grad_section_normed[0],
+            section_mixed,
+            hires_maps[0],
+            section_kernel,
+            section_gain,
+        )
+        grad_maps = grad_maps[None] + grad_section_out
+        split = part_out.shape[4]
+        grad_fc2_w, grad_fc1_w, grad_qkv_w = [finish(piece) for piece in pieces[:3]]
+        grad_out_w, grad_adapter_w = finish(pieces[3][:, :, :split]), finish(pieces[3][:, :, split:])
+        grad_reduce_w, grad_expand_w = finish(pieces[4]), finish(pieces[5])
+    else:
+        grad_section_mixed, grad_section_gain = section_norm_back(grad_section_normed)
+        grad_maps_conv, grad_section_taps = section_back(grad_section_mixed)
+        grad_maps = grad_section_out + grad_maps_conv
     summed = (
         grad_qkv_w,
         grad_out_w,
@@ -369,18 +773,31 @@
         grad_expand_w,
         grad_reduce_w,
     )
-    small_sums = lax.psum(
-        (
-            grad_attn_gain,
-            grad_mlp_gain,
-            grad_merge,
-            grad_adapter_taps,
-            grad_section_gain,
-            grad_section_taps,
-            grad_scale,
-        ),
-        ("path", "dev"),
-    )
+    if tuned:
+        tap_count = section_kernel.shape[0]
+        flat = small_rows[tap_count + 1 : small_count - 1].reshape(-1)
+        small_sums = (
+            flat[:model_width],
+            flat[model_width : 2 * model_width],
+            flat[2 * model_width : 3 * model_width],
+            flat[3 * model_width :].reshape(adapter_kernel.shape),
+            small_rows[tap_count],
+            small_rows[:tap_count],
+            small_rows[small_count - 1],
+        )
+    else:
+        small_sums = lax.psum(
+            (
+                grad_attn_gain,
+                grad_mlp_gain,
+                grad_merge,
+                grad_adapter_taps,
+                grad_section_gain,
+                grad_section_taps,
+                grad_scale,
+            ),
+            ("path", "dev"),
+        )
     return (
         result,
         grad_in[None],

time: 1260 us -> 999 us (0.79)
  Pallas kernels: 259 us -> 578 us
  other arithmetic: 331 us -> 52.2 us
  local copies, waits for them, and re-layouts: 196 us -> 96 us
  waiting for transfers between devices: 130 us -> 52.2 us
  blocking collectives: 61.8 us -> 0 us
  starting transfers between devices: 56.7 us -> 26.8 us
  between operations: 25.4 us -> 3.11 us
    pallas_call x0 -> x1, Pallas kernels: none -> 336 us  [scatter_gradients(): pl.pallas_call(scatter_kernel, out_shape=[jax.ShapeDtypeStruct(maps.shape...]
    dynamic_slice x6 -> x0, local copies, waits for them, and re-layouts: 88.5 us -> none  [pick(): return lax.dynamic_index_in_dim(value, index, axis, keepdims=False)]
    reduce_sum x4 -> x3, other arithmetic: 85.8 us -> 3.04 us  [layer_norm(): centred = values - jnp.mean(values, axis=-1, keepdims=True)]
    ppermute x24 -> x18, waiting for transfers between devices: 109 us -> 35.5 us  [swap(): return lax.ppermute(value, axis, [(i, i ^ mask) for i in range(size)])]
    psum x1 -> x0, blocking collectives: 61.8 us -> none  [local(): lax.psum((grad_attn_gain, grad_mlp_gain, grad_merge, grad_adapter_taps, g...]
    reduce_sum x5 -> x2, other arithmetic: 62.5 us -> 2.94 us  [depthwise(): window * taps_table[offset_row * kernel_side + offset_col]]
    mul x3 -> x0, other arithmetic: 57 us -> none  [depthwise(): window * taps_table[offset_row * kernel_side + offset_col]]
    add_any x2 -> x1, other arithmetic: 50.5 us -> 0.36 us  [depthwise(): padded[:, offset_row:offset_row + map_side, offset_col:offset_col + map_s...]
  transfers between devices with their start and end apart: 36 -> 23, of which waited for: 10 -> 6; matrix products, arithmetic and copies ran while one was open for 52% -> 25% of each run, Pallas kernels for 21% -> 24%
where the time goes in v2:
time: 999 us; the launch traced here: 991 us
  Pallas kernels  578 us (58%)
  matrix products  182 us (18%)
  local copies, waits for them, and re-layouts  96 us (10%)
  other arithmetic  52.2 us (5%)
  waiting for transfers between devices  52.2 us (5%)
  starting transfers between devices  26.8 us (3%)
    pallas_call x1, Pallas kernels, scatter_gradients(): pl.pallas_call(scatter_kernel, out_shape=[jax.ShapeDtypeStruct(maps.shape...  336 us
    pallas_call x1, Pallas kernels, gather_weights(): pl.pallas_call(functools.partial(gather_kernel, jobs, n), out_shape=[jax....  242 us
    dot_general x7, matrix products, pair_gradient(): lax.dot_general(rows, jnp.concatenate([mine, theirs]), (((0,), (0,)), (()...  50.5 us
    unnamed x185, local copies, waits for them, and re-layouts  38 us
    ppermute x18, waiting for transfers between devices, swap(): return lax.ppermute(value, axis, [(i, i ^ mask) for i in range(size)])  35.5 us
    dot_general x1, matrix products, local(): jnp.dot(grad_reduced, full_reduce.T, preferred_element_type=jnp.float32)  24.7 us
    dot_general x1, matrix products, local(): jnp.dot(section_rows, full_expand, preferred_element_type=jnp.float32)  22.8 us
  transfers between devices with their start and end apart: 23, of which 6 were waited for; matrix products, arithmetic and copies ran while one was open for 25% of the time, Pallas kernels for 24%

profile of v2, /device:TPU:0, one launch (start us, length us, event | category | flops | bytes accessed | tf_op | source)
XLA Modules:
  0.0 990.5 jit_solution(6197941066348052955)
XLA Ops:
  1.9 5.2 all-to-all-start
  19.1 241.6 %shard_map.305 = (bf16[1536,6144]{1,0:T(8,128)(2,1)}, bf16[6144,1536]{1,0:T(8,128)(2,1)}, bf16[1536,1024]{1,0:T(8,128)(2,1)}, bf16[1024,3072]{1,0:T(8,128)(2,1)}...) custom-call(bf16[192,6144]{1,0:T(8,128)(2,1)S(1)} %copy-done.2, ...), custom_call_target="tpu_custom_call" | custom-call | tf_op jit(solution)/shard_map/pallas_call | solution.py:172
  260.7 22.8 %multiply_convert_fusion = (bf16[576,6144]{1,0:T(8,128)(2,1)}, f32[576,6144]{1,0:T(8,128)}) fusion(bf16[576,1536]{1,0:T(8,128)(2,1)S(1)} %bitcast.180, bf16[1536,6144]{1,0:T(8,128)(2,1)} %get-tuple-element.39), kind=kOutput, calls=%fused_computation.14 | convolution fusion | flops 10903486464 | bytes 41877504 | tf_op jit(solution)/shard_map/dot_general | solution.py:589
  283.5 16.4 %fusion.116 = f32[576,1536]{1,0:T(8,128)S(1)} fusion(bf16[576,6144]{1,0:T(8,128)(2,1)} %get-tuple-element.123, bf16[6144,1536]{1,0:T(8,128)(2,1)} %get-tuple-element.40), kind=kOutput, calls=%fused_computation.241 | convolution fusion | flops 10871635968 | bytes 29491200 | tf_op jit(solution)/shard_map/dot_general | solution.py:592
  304.0 5.3 reshape.485
  309.3 4.6 reduce_sum.210
  321.0 7.8 all-to-all-done.1
  335.3 6.0 all-to-all-done.2
  350.2 4.0 convolution_convert_fusion.4
  366.3 6.9 multiply_convert_fusion.3
  393.7 6.5 multiply_reduce_fusion.14
  413.7 5.9 fusion.58
  464.3 3.9 multiply_reduce_fusion
  469.4 24.7 %fusion.7 = bf16[576,6144]{1,0:T(8,128)(2,1)} fusion(f32[576,6144]{1,0:T(8,128)} %get-tuple-element.124, bf16[576,1536]{1,0:T(8,128)(2,1)S(1)} %get-tuple-element.86, bf16[6144,1536]{1,0:T(8,128)(2,1)} %get-tuple-element.40), kind=kOutput, calls=%fused_computation.9 | convolution fusion | flops 10942414848 | bytes 41877504 | tf_op jit(solution)/shard_map/dot_general | solution.py:726
  497.7 4.0 convolution_convert_fusion.1
  510.7 14.4 %collective-permute-done.7 = bf16[4,2,2,32,2048]{4,3,2,1,0:T(8,128)(2,1)} collective-permute-done((bf16[4,2,2,32,2048]{4,3,2,1,0:T(8,128)(2,1)}, bf16[4,2,2,32,2048]{4,3,2,1,0:T(8,128)(2,1)}, u32[]{:S(2)}, u32[]{:S(2)}) %collective-permute-start.7) | collective-permute-done | bytes 2097184 | tf_op jit(solution)/shard_map/ppermute | solution.py:487
  528.7 20.4 %collective-permute-done.4 = bf16[4,2,2,128,512]{4,3,2,1,0:T(8,128)(2,1)S(1)} collective-permute-done((bf16[4,2,2,128,512]{4,3,2,1,0:T(8,128)(2,1)S(1)}, bf16[4,2,2,128,512]{4,3,2,1,0:T(8,128)(2,1)S(1)}, u32[]{:S(2)}, u32[]{:S(2)}) %collective-permute-start.4) | collective-permute-done | bytes 2097184 | tf_op jit(solution)/shard_map/ppermute | solution.py:487
  552.1 18.8 %fusion.12 = bf16[6144,768]{1,0:T(8,128)(2,1)} fusion(bf16[576,6144]{1,0:T(8,128)(2,1)} %collective-permute-done, bf16[576,6144]{1,0:T(8,128)(2,1)} %get-tuple-element.123, bf16[576,768]{1,0:T(8,128)(2,1)} %copy-done.83, bf16[576,768]{1,0:T(8,128)(2,1)S(1)} %get-tuple-element.87), kind=kOutput, calls=%fused_computation.16 | convolution fusion | flops 10908205056 | bytes 25362432 | tf_op jit(solution)/shard_map/dot_general | solution.py:513
  570.9 5.2 broadcast_select_fusion.1
  576.1 18.3 %fusion.118 = f32[576,1536]{1,0:T(8,128)} fusion(bf16[576,6144]{1,0:T(8,128)(2,1)} %fusion.7, bf16[1536,6144]{1,0:T(8,128)(2,1)} %get-tuple-element.39), kind=kOutput, calls=%fused_computation.243 | convolution fusion | flops 10871635968 | bytes 29491200 | tf_op jit(solution)/shard_map/dot_general | solution.py:734
  594.4 18.1 %convolution_convert_fusion = bf16[1536,3072]{1,0:T(8,128)(2,1)} fusion(bf16[576,3072]{1,0:T(8,128)(2,1)} %collective-permute-done.9, bf16[576,3072]{1,0:T(8,128)(2,1)} %get-tuple-element.83, bf16[576,1536]{1,0:T(8,128)(2,1)S(1)} %collective-permute-done.8, bf16[576,1536]{1,0:T(8,128)(2,1)S(1)} %bitcast.182), kind=kOutput, calls=%fused_computation.15 | convolution fusion | flops 10897588224 | bytes 20054016 | tf_op jit(solution)/shard_map/dot_general | solution.py:513
  612.5 336.5 %shard_map.306 = (f32[24,24,1536]{2,1,0:T(8,128)}, f32[64,1536]{1,0:T(8,128)}, bf16[4,2,128,512]{3,2,1,0:T(8,128)(2,1)}, bf16[4,2,32,2048]{3,2,1,0:T(8,128)(2,1)...) custom-call(bf16[4,2,2,2,192,768]{5,4,3,2,1,0:T(8,128)(2,1)} %bitcas, ...), custom_call_target="tpu_custom_call" | custom-call | tf_op jit(solution)/shard_map/pallas_call | solution.py:442
  974.4 4.0 copy.165
  978.8 3.9 copy.143
  (342 shorter events, 182.3 us)
Async XLA Ops:
  1.9 314.9 %all-to-all-start = ((s32[4,1,1]{2,1,0:T(1,128)}), s32[4,1,1]{2,1,0:T(1,128)S(1)}, u32[]{:S(2)}, u32[]{:S(2)}) async-start(s32[4,1,1]{2,1,0:T(1,128)} %broadcast_in_dim.81), calls=%async_computation | async-start | bytes 4096 | tf_op jit(solution)/shard_map/all_to_all | solution.py:603
  7.7 252.9 %copy-start.10 = (f32[1,1536]{1,0:T(1,128)}, f32[1,1536]{1,0:T(1,128)S(1)}, u32[]{:S(2)}) copy-start(f32[1,1536]{1,0:T(1,128)S(1)} %reshape.482.refs_9_.gain) | copy-start | bytes 18436
  316.8 12.1 %all-to-all-start.1 = ((bf16[4,36,1536]{2,1,0:T(8,128)(2,1)}), bf16[4,36,1536]{2,1,0:T(8,128)(2,1)S(1)}, u32[]{:S(2)}, u32[]{:S(2)}) async-start(bf16[4,36,1536]{2,1,0:T(8,128)(2,1)} %convert_element_type.229), calls=%async_computation.1 | async-start | bytes 983040 | tf_op jit(solution)/shard_map/all_to_all | solution.py:602
  320.4 231.7 %collective-permute-start = (bf16[576,6144]{1,0:T(8,128)(2,1)}, bf16[576,6144]{1,0:T(8,128)(2,1)}, u32[]{:S(2)}, u32[]{:S(2)}) collective-permute-start(bf16[576,6144]{1,0:T(8,128)(2,1)} %get-tuple-element.123), channel_id=1, source_target_pairs={{0,1},{1,0},{2,3},{3,2},{4,5},{5,4},{6,7},{7,6},{8,9},{9,8},{10,11... | collective-permute-start | bytes 21233672 | tf_op jit(solution)/shard_map/ppermute | solution.py:487
  330.3 11.1 %all-to-all-start.2 = ((bf16[4,36,1536]{2,1,0:T(8,128)(2,1)}), bf16[4,36,1536]{2,1,0:T(8,128)(2,1)S(1)}, u32[]{:S(2)}, u32[]{:S(2)}) async-start(bf16[4,36,1536]{2,1,0:T(8,128)(2,1)} %copy.113), calls=%async_computation.2 | async-start | bytes 983040 | tf_op jit(solution)/shard_map/all_to_all | solution.py:611
  334.7 133.4 %collective-permute-start.3 = (bf16[144,512]{1,0:T(8,128)(2,1)}, bf16[144,512]{1,0:T(8,128)(2,1)}, u32[]{:S(2)}, u32[]{:S(2)}) collective-permute-start(bf16[144,512]{1,0:T(8,128)(2,1)} %get-tuple-element.110), channel_id=1, source_target_pairs={{0,1},{1,0},{2,3},{3,2},{4,5},{5,4},{6,7},{7,6},{8,9},{9,8},{10,11... | collective-permute-start | bytes 442376 | tf_op jit(solution)/shard_map/ppermute | solution.py:487
  413.0 14.5 %collective-permute-start.13 = (bf16[144,1024]{0,1:T(8,128)(2,1)S(1)}, bf16[144,1024]{0,1:T(8,128)(2,1)}, u32[]{:S(2)}, u32[]{:S(2)}) collective-permute-start(bf16[144,1024]{0,1:T(8,128)(2,1)S(1)} %bitcast.225), channel_id=1, source_target_pairs={{0,1},{1,0},{2,3},{3,2},{4,5},{5,4},{6,7},{7,6},{8,9},{9,8},{10,11... | collective-permute-start | bytes 884744 | tf_op jit(solution)/shard_map/ppermute | solution.py:487
  420.6 12.2 %all-to-all-start.3 = ((bf16[4,36,1536]{2,1,0:T(8,128)(2,1)}), bf16[4,36,1536]{2,1,0:T(8,128)(2,1)S(1)}, u32[]{:S(2)}, u32[]{:S(2)}) async-start(bf16[4,36,1536]{2,1,0:T(8,128)(2,1)} %reshape.498), calls=%async_computation.3 | async-start | bytes 983040 | tf_op jit(solution)/shard_map/all_to_all | solution.py:706
  425.4 13.0 %collective-permute-start.11 = (bf16[144,1536]{1,0:T(8,128)(2,1)}, bf16[144,1536]{1,0:T(8,128)(2,1)}, u32[]{:S(2)}, u32[]{:S(2)}) collective-permute-start(bf16[144,1536]{1,0:T(8,128)(2,1)} %get-tuple-element.92), channel_id=1, source_target_pairs={{0,1},{1,0},{2,3},{3,2},{4,5},{5,4},{6,7},{7,6},{8,9},{9,8},{10,11... | collective-permute-start | bytes 1327112 | tf_op jit(solution)/shard_map/ppermute | solution.py:487
  425.9 1.5 collective-permute-start.14
  427.4 10.9 %collective-permute-start.10 = (bf16[144,1024]{1,0:T(8,128)(2,1)S(1)}, bf16[144,1024]{1,0:T(8,128)(2,1)}, u32[]{:S(2)}, u32[]{:S(2)}) collective-permute-start(bf16[144,1024]{1,0:T(8,128)(2,1)S(1)} %copy-done.43), channel_id=1, source_target_pairs={{0,1},{1,0},{2,3},{3,2},{4,5},{5,4},{6,7},{7,6},{8,9},{9,8},{10,11... | collective-permute-start | bytes 884744 | tf_op jit(solution)/shard_map/ppermute | solution.py:487
  427.5 14.5 %collective-permute-start.15 = (bf16[144,1536]{1,0:T(8,128)(2,1)S(1)}, bf16[144,1536]{1,0:T(8,128)(2,1)}, u32[]{:S(2)}, u32[]{:S(2)}) collective-permute-start(bf16[144,1536]{1,0:T(8,128)(2,1)S(1)} %copy-done.47), channel_id=1, source_target_pairs={{0,1},{1,0},{2,3},{3,2},{4,5},{5,4},{6,7},{7,6},{8,9},{9,8},{10,11... | collective-permute-start | bytes 1327112 | tf_op jit(solution)/shard_map/ppermute | solution.py:487
  434.8 21.8 %all-to-all-start.4 = ((bf16[4,36,1536]{2,1,0:T(8,128)(2,1)}), bf16[4,36,1536]{2,1,0:T(8,128)(2,1)S(1)}, u32[]{:S(2)}, u32[]{:S(2)}) async-start(bf16[4,36,1536]{2,1,0:T(8,128)(2,1)} %copy.127), calls=%async_computation.4 | async-start | bytes 983040 | tf_op jit(solution)/shard_map/all_to_all | solution.py:710
  438.3 11.0 %collective-permute-start.6 = (bf16[144,2048]{1,0:T(8,128)(2,1)S(1)}, bf16[144,2048]{1,0:T(8,128)(2,1)S(1)}, u32[]{:S(2)}, u32[]{:S(2)}) collective-permute-start(bf16[144,2048]{1,0:T(8,128)(2,1)S(1)} %copy-done.55), channel_id=1, source_target_pairs={{0,1},{1,0},{2,3},{3,2},{4,5},{5,4},{6,7},{7,6},{8,9},{9,8},{10,11... | collective-permute-start | bytes 1769480 | tf_op jit(solution)/shard_map/ppermute | solution.py:487
  438.4 3.5 collective-permute-start.16
  441.9 55.8 %collective-permute-start.2 = (bf16[144,4096]{1,0:T(8,128)(2,1)}, bf16[144,4096]{1,0:T(8,128)(2,1)}, u32[]{:S(2)}, u32[]{:S(2)}) collective-permute-start(bf16[144,4096]{1,0:T(8,128)(2,1)} %get-tuple-element.129), channel_id=1, source_target_pairs={{0,1},{1,0},{2,3},{3,2},{4,5},{5,4},{6,7},{7,6},{8,9},{9,8},{10,11... | collective-permute-start | bytes 3538952 | tf_op jit(solution)/shard_map/ppermute | solution.py:487
  442.1 5.3 collective-permute-start.5
  447.4 60.1 %collective-permute-start.12 = (bf16[4,2,2,32,1536]{4,3,2,1,0:T(8,128)(2,1)}, bf16[4,2,2,32,1536]{4,3,2,1,0:T(8,128)(2,1)}, u32[]{:S(2)}, u32[]{:S(2)}) collective-permute-start(bf16[4,2,2,32,1536]{4,3,2,1,0:T(8,128)(2,1)} %dynamic-slice_bitcast_fusion.2), channel_id=1, source_target_pairs={{0,8},{8,0},{16,24},{24,16},{1,9},{9,1},{17,25},{25,17},{2,10},{10... | collective-permute-start | bytes 4718600 | tf_op jit(solution)/shard_map/ppermute | solution.py:487
  449.3 54.4 %collective-permute-start.17 = (bf16[4,2,2,80,512]{4,3,2,1,0:T(8,128)(2,1)}, bf16[4,2,2,80,512]{4,3,2,1,0:T(8,128)(2,1)}, u32[]{:S(2)}, u32[]{:S(2)}) collective-permute-start(bf16[4,2,2,80,512]{4,3,2,1,0:T(8,128)(2,1)} %fusion.48), channel_id=1, source_target_pairs={{0,16},{8,24},{16,0},{24,8},{1,17},{9,25},{17,1},{25,9},{2,18},{10... | collective-permute-start | bytes 3932168 | tf_op jit(solution)/shard_map/ppermute | solution.py:487
  468.2 56.9 %collective-permute-start.7 = (bf16[4,2,2,32,2048]{4,3,2,1,0:T(8,128)(2,1)}, bf16[4,2,2,32,2048]{4,3,2,1,0:T(8,128)(2,1)}, u32[]{:S(2)}, u32[]{:S(2)}) collective-permute-start(bf16[4,2,2,32,2048]{4,3,2,1,0:T(8,128)(2,1)} %dynamic-slice_bitcast_fusion), channel_id=1, source_target_pairs={{0,16},{8,24},{16,0},{24,8},{1,17},{9,25},{17,1},{25,9},{2,18},{10... | collective-permute-start | bytes 6291464 | tf_op jit(solution)/shard_map/ppermute | solution.py:487
  502.0 47.2 %collective-permute-start.4 = (bf16[4,2,2,128,512]{4,3,2,1,0:T(8,128)(2,1)S(1)}, bf16[4,2,2,128,512]{4,3,2,1,0:T(8,128)(2,1)S(1)}, u32[]{:S(2)}, u32[]{:S(2)}) collective-permute-start(bf16[4,2,2,128,512]{4,3,2,1,0:T(8,128)(2,1)S(1)} %dynamic-slice_bitcast_fusion.1), channel_id=1, source_target_pairs={{0,8},{8,0},{16,24},{24,16},{1,9},{9,1},{17,25},{25,17},{2,10},{10... | collective-permute-start | bytes 6291464 | tf_op jit(solution)/shard_map/ppermute | solution.py:487
  503.9 90.6 %collective-permute-start.8 = (bf16[576,1536]{1,0:T(8,128)(2,1)S(1)}, bf16[576,1536]{1,0:T(8,128)(2,1)S(1)}, u32[]{:S(2)}, u32[]{:S(2)}) collective-permute-start(bf16[576,1536]{1,0:T(8,128)(2,1)S(1)} %bitcast.181), channel_id=1, source_target_pairs={{0,1},{1,0},{2,3},{3,2},{4,5},{5,4},{6,7},{7,6},{8,9},{9,8},{10,11... | collective-permute-start | bytes 5308424 | tf_op jit(solution)/shard_map/ppermute | solution.py:487
  507.5 43.7 %collective-permute-start.1 = (bf16[576,768]{1,0:T(8,128)(2,1)S(1)}, bf16[576,768]{1,0:T(8,128)(2,1)S(1)}, u32[]{:S(2)}, u32[]{:S(2)}) collective-permute-start(bf16[576,768]{1,0:T(8,128)(2,1)S(1)} %get-tuple-element.88), channel_id=1, source_target_pairs={{0,1},{1,0},{2,3},{3,2},{4,5},{5,4},{6,7},{7,6},{8,9},{9,8},{10,11... | collective-permute-start | bytes 2654216 | tf_op jit(solution)/shard_map/ppermute | solution.py:487
  576.1 18.4 %collective-permute-start.9 = (bf16[576,3072]{1,0:T(8,128)(2,1)}, bf16[576,3072]{1,0:T(8,128)(2,1)}, u32[]{:S(2)}, u32[]{:S(2)}) collective-permute-start(bf16[576,3072]{1,0:T(8,128)(2,1)} %get-tuple-element.84), channel_id=1, source_target_pairs={{0,1},{1,0},{2,3},{3,2},{4,5},{5,4},{6,7},{7,6},{8,9},{9,8},{10,11... | collective-permute-start | bytes 10616840 | tf_op jit(solution)/shard_map/ppermute | solution.py:487
  (88 other events, 485.4 us)

commit v3 on v2

--- a/solution.py
+++ b/solution.py
@@ -53,14 +53,7 @@
     lax.fori_loop(0, side // GROUP, rows, 0)
 
 
-def norm_rows(h, mixed, gain, rows):
-    v = mixed[h]
-    centred = v - jnp.mean(v, axis=-1, keepdims=True)
-    scale = lax.rsqrt(jnp.mean(centred * centred, axis=-1, keepdims=True) + 1e-06)
-    rows[h] = (centred * scale * gain[...]).astype(jnp.bfloat16)
-
-
-def section_forward_kernel(maps, taps, gain, mixed, rows, pad):
+def section_mix(maps, taps, gain, mixed, rows, pad):
     side, _, channels = maps.shape
     clear_edges(pad, side)
 
@@ -70,118 +63,253 @@
 
     lax.fori_loop(0, channels // LANES, blocks, 0)
 
-    def norm(h, carry):
-        norm_rows(h, mixed, gain, rows)
+    def norm(pair, carry):
+        v = mixed[pl.ds(2 * pair, 2)].reshape(2 * side, channels)
+        centred = v - jnp.mean(v, axis=-1, keepdims=True)
+        scale = lax.rsqrt(jnp.mean(centred * centred, axis=-1, keepdims=True) + 1e-06)
+        at = pl.ds(pl.multiple_of(pair * 2 * side, 2 * side), 2 * side)
+        rows[at, :] = (centred * scale * gain[...]).astype(jnp.bfloat16)
         return carry
 
-    lax.fori_loop(0, side, norm, 0)
+    lax.fori_loop(0, side // 2, norm, 0)
+
+
+STEP = 512
+
+
+def product(left, right, total, left_at, right_at):
+    total[...] = jnp.zeros_like(total)
+
+    def step(k, carry):
+        here = pl.multiple_of(k * STEP, STEP)
+        total[...] += jnp.dot(
+            left[:, pl.ds(left_at + here, STEP)],
+            right[pl.ds(here, STEP), pl.ds(pl.multiple_of(right_at, STEP), STEP)],
+            preferred_element_type=jnp.float32,
+        )
+        return carry
+
+    lax.fori_loop(0, right.shape[0] // STEP, step, 0)
 
 
 def gather_jobs(shapes):
     jobs = []
     for w, (r, n) in enumerate(shapes):
-        q = r // 4
-        size = q * n
-        parts = max(1, round(size / (16 * 6144)))
-        while parts > 1 and (n // 2) % (parts * 128): parts -= 1
-        for k in range(parts):
-            jobs.append((w, q, k * (n // parts), n // parts))
+        parts = max(1, round(r // 4 * n / (16 * 6144)))
+        while n % (parts * STEP):
+            parts -= 1
+        jobs += [(w, r // 4, k * (n // parts), n // parts) for k in range(parts)]
     return jobs
 
-def gather_kernel(jobs, count, *refs):
+
+def gather_kernel(jobs, count, expand, reduce, *refs):
     shards = refs[:count]
-    maps, taps, gain = refs[count : count + 3]
-    fulls = refs[count + 3 : 2 * count + 3]
-    mixed, rows_out, pad, zs, zr, ps, pr, cs, cr, ls = refs[2 * count + 3 :]
-    p = lax.axis_index("path"); d = lax.axis_index("dev")
-    masks = [(0,1),(0,2),(0,4),(0,6),(1,0),(2,0)]
-    def at(m): return (p ^ m[0], d ^ m[1])
+    maps, taps, gain, scale, target = refs[count : count + 5]
+    fulls = refs[count + 5 : 2 * count + 5]
+    mixed, rows, targets, expanded, active, reduced, pooled = refs[2 * count + 5 : 2 * count + 12]
+    pad, wide_w, deep_w, total, stage, pair_sum = refs[2 * count + 12 : 2 * count + 18]
+    zs, zr, ps, pr, cs, cr, os, orr, ls, ts, tr, ws, es = refs[2 * count + 18 :]
+    p, d = lax.axis_index("path"), lax.axis_index("dev")
+
+    def at(m):
+        return (p ^ m[0], d ^ m[1])
+
+    masks = [(0, 1), (0, 2), (0, 4), (0, 6), (1, 0), (2, 0), (3, 0)]
     bar = pltpu.get_barrier_semaphore()
-    for m in masks: pl.semaphore_signal(bar, inc=1, device_id=at(m), device_id_type=MESH)
+    for m in masks:
+        pl.semaphore_signal(bar, inc=1, device_id=at(m), device_id_type=MESH)
     pl.semaphore_wait(bar, len(masks))
-    def rows(w, owner):
-        r = shards[w].shape[0]; return r, owner * r
+
     def copy(src, dst, ss, rs, m):
         return pltpu.make_async_remote_copy(src, dst, ss, rs, device_id=at(m), device_id_type=MESH)
+
     def quarter(w, owner, q, nq, c0, nc):
         r = shards[w].shape[0]
         return fulls[w].at[pl.ds(pl.multiple_of(owner * r + q * nq, 16), nq), pl.ds(c0, nc)]
+
+    J = len(jobs)
+
+    def Z(i, k):
+        w, nq, c0, nc = jobs[i]
+        src = shards[w].at[pl.ds(pl.multiple_of(p * nq, 16), nq), pl.ds(c0, nc)]
+        return copy(src, quarter(w, d, p, nq, c0, nc), zs.at[i, k], zr.at[i, k], (0, 2 * (k + 1)))
+
+    def XY(i, k, axis):
+        w, nq, c0, nc = jobs[i]
+        ref = quarter(w, d ^ (2 * (k + 1)), p, nq, c0, nc)
+        return copy(ref, ref, ps.at[i, k, axis], pr.at[i, k, axis], (1 + axis, 0))
+
+    def DG(i, k, axis):
+        w, nq, c0, nc = jobs[i]
+        h = nc // 2
+        ref = quarter(w, d ^ (2 * (k + 1)), p ^ (2 - axis), nq, c0 + axis * h, h)
+        return copy(ref, ref, ps.at[i, k, 2 + axis], pr.at[i, k, 2 + axis], (1 + axis, 0))
+
+    def S(i, k):
+        w, nq, c0, nc = jobs[i]
+        r = shards[w].shape[0]
+        ref = fulls[w].at[pl.ds(pl.multiple_of((d ^ (2 * (k + 1))) * r, 16), r), pl.ds(c0, nc)]
+        return copy(ref, ref, cs.at[i, k], cr.at[i, k], (0, 1))
+
+    for i in range(min(AHEAD, J)):
+        for k in range(3):
+            Z(i, k).start()
     own = []
     for w in range(count):
         r = shards[w].shape[0]
         place = fulls[w].at[pl.ds(pl.multiple_of(d * r, 16), r)]
-        a = pltpu.make_async_copy(shards[w], place, ls.at[w]); a.start()
-        b = copy(shards[w], place, cs.at[w, 0], cr.at[w, 0], (0,1)); b.start()
-        own.append((a, b))
-    J = len(jobs)
-    def Z(i, k):
-        w, nq, c0, nc = jobs[i]
-        return copy(shards[w].at[pl.ds(pl.multiple_of(p * nq, 16), nq), pl.ds(c0, nc)], quarter(w, d, p, nq, c0, nc), zs.at[i,k], zr.at[i,k], (0, 2*(k+1)))
-    def XY(i, k, axis):
-        w, nq, c0, nc = jobs[i]
-        ref = quarter(w, d ^ (2*(k+1)), p, nq, c0, nc)
-        return copy(ref, ref, ps.at[i,k,axis], pr.at[i,k,axis], (1+axis, 0))
-    def DG(i, k, axis):
-        w, nq, c0, nc = jobs[i]
-        h = nc // 2
-        ref = quarter(w, d ^ (2*(k+1)), p ^ (2 - axis), nq, c0 + axis * h, h)
-        return copy(ref, ref, ps.at[i,k,2+axis], pr.at[i,k,2+axis], (1+axis, 0))
-    def S(w, k):
-        r = shards[w].shape[0]
-        ref = fulls[w].at[pl.ds(pl.multiple_of((d ^ (2*(k+1))) * r, 16), r)]
-        return copy(ref, ref, cs.at[w,1+k], cr.at[w,1+k], (0,1))
-    last = {}
-    for i,(w,*_) in enumerate(jobs): last[w] = i
-    AHEAD = 3
-    for i in range(min(AHEAD, J)):
-        for k in range(3): Z(i,k).start()
-    section_forward_kernel(maps, taps, gain, mixed, rows_out, pad)
-    sent = []
-    for i in range(J + 2):
+        pair = pltpu.make_async_copy(shards[w], place, ls.at[w]), copy(shards[w], place, os.at[w], orr.at[w], (0, 1))
+        for c in pair:
+            c.start()
+        own.append(pair)
+    targets[p] = target[...]
+    named = [copy(target, targets.at[p], ts.at[m - 1], tr.at[m - 1], (m, 0)) for m in (1, 2, 3)]
+    for c in named:
+        c.start()
+    section_mix(maps, taps, gain, mixed, rows, pad)
+
+    ready = set()
+
+    def ensure(w):
+        if w not in ready:
+            ready.add(w)
+            own[w][0].wait()
+            own[w][1].wait_recv()
+
+    def expand_block(c0, nc):
+        load = pltpu.make_async_copy(fulls[expand].at[:, pl.ds(c0, nc)], wide_w, ws.at[0])
+        load.start()
+        load.wait()
+
+        def chunk(j, carry):
+            here = pl.multiple_of(j * STEP, STEP)
+            product(rows, wide_w, total, 0, here)
+            stage[...] = total[...]
+            active[:, pl.ds(c0 + here, STEP)] = jax.nn.gelu(total[...]).astype(jnp.bfloat16)
+            out = pltpu.make_async_copy(stage, expanded.at[:, pl.ds(c0 + here, STEP)], es.at[0])
+            out.start()
+            out.wait()
+            return carry
+
+        lax.fori_loop(0, nc // STEP, chunk, 0)
+
+    def reduce_block(c0, nc):
+        load = pltpu.make_async_copy(fulls[reduce].at[:, pl.ds(c0, nc)], deep_w, ws.at[1])
+        load.start()
+        load.wait()
+        cols = pl.ds(c0, nc)
+        product(active, deep_w, total, 0, 0)
+        reduced[:, cols] = total[...]
+        side = maps.shape[0]
+
+        def pool(h, carry):
+            both = jnp.zeros((side, nc), jnp.float32)
+            for r in range(2):
+                row = 2 * h + r
+                part = total[pl.ds(pl.multiple_of(row * side, 8), side), :]
+                both += maps[row, :, cols].astype(jnp.float32) + scale[:, cols] * part
+            half = side // 2
+            for k in range(nc // LANES):
+                pair_sum[k] = both[:, k * LANES : (k + 1) * LANES]
+            for k in range(nc // LANES):
+                even = pair_sum[k, pl.ds(0, half, stride=2), :]
+                odd = pair_sum[k, pl.ds(1, half, stride=2), :]
+                pooled[h, :, c0 + k * LANES : c0 + (k + 1) * LANES] = (even + odd) * 0.25
+            return carry
+
+        lax.fori_loop(0, side // 2, pool, 0)
+
+    for i in range(J + 3):
         if i < J:
             for k in range(3):
-                Z(i,k).wait_recv()
-                XY(i,k,0).start(); XY(i,k,1).start()
+                Z(i, k).wait_recv()
+                XY(i, k, 0).start()
+                XY(i, k, 1).start()
             if i + AHEAD < J:
-                for k in range(3): Z(i+AHEAD,k).start()
-        if 0 <= i-1 < J:
+                for k in range(3):
+                    Z(i + AHEAD, k).start()
+        if 0 <= i - 1 < J:
             for k in range(3):
-                XY(i-1,k,0).wait_recv(); DG(i-1,k,1).start()
-                XY(i-1,k,1).wait_recv(); DG(i-1,k,0).start()
-        if 0 <= i-2 < J:
+                XY(i - 1, k, 0).wait_recv()
+                DG(i - 1, k, 1).start()
+                XY(i - 1, k, 1).wait_recv()
+                DG(i - 1, k, 0).start()
+        if 0 <= i - 2 < J:
             for k in range(3):
-                DG(i-2,k,0).wait_recv(); DG(i-2,k,1).wait_recv()
-            w = jobs[i-2][0]
-            if last[w] == i-2:
-                for k in range(3): S(w,k).start()
+                DG(i - 2, k, 0).wait_recv()
+                DG(i - 2, k, 1).wait_recv()
+                S(i - 2, k).start()
+        if 0 <= i - 3 < J:
+            for k in range(3):
+                S(i - 3, k).wait_recv()
+            w, _, c0, nc = jobs[i - 3]
+            ensure(w)
+            if w == expand:
+                expand_block(c0, nc)
+            if w == reduce:
+                reduce_block(c0, nc)
+    for c in named:
+        c.wait()
     for w in range(count):
-        own[w][0].wait(); own[w][1].wait()
-        for k in range(3): S(w,k).wait()
+        ensure(w)
+        own[w][1].wait_send()
     for i in range(J):
         for k in range(3):
-            Z(i,k).wait_send()
-            for a in range(2): XY(i,k,a).wait_send(); DG(i,k,a).wait_send()
-
-def gather_weights(shards, maps, taps, gain):
+            Z(i, k).wait_send()
+            S(i, k).wait_send()
+            for a in range(2):
+                XY(i, k, a).wait_send()
+                DG(i, k, a).wait_send()
+
+
+AHEAD = 3
+GATHER_ORDER = (4, 0, 1, 5, 6, 3, 2)
+
+
+def gather_weights(shards, maps, taps, gain, scale, target, expand, reduce):
     shapes = [s.shape for s in shards]
     jobs = gather_jobs(shapes)
     n, J = len(shards), len(jobs)
     side, _, channels = maps.shape
+    cells, hidden = side * side, shapes[expand][1]
+    wide = max(nc for w, _, _, nc in jobs if w == expand)
+    low, full = jnp.bfloat16, jnp.float32
     anyspec, whole = pl.BlockSpec(memory_space=pl.ANY), pl.BlockSpec(memory_space=VMEM)
     dma = pltpu.SemaphoreType.DMA
+    shape = jax.ShapeDtypeStruct
     results = pl.pallas_call(
-        functools.partial(gather_kernel, jobs, n),
-        out_shape=[jax.ShapeDtypeStruct((8 * r, c), jnp.bfloat16) for r, c in shapes]
-        + [jax.ShapeDtypeStruct(maps.shape, jnp.float32), jax.ShapeDtypeStruct(maps.shape, jnp.bfloat16)],
-        in_specs=[anyspec] * n + [whole] * 3,
-        out_specs=[anyspec] * n + [whole] * 2,
-        scratch_shapes=[VMEM((side + 2 * REACH, side + 2 * EDGE, LANES), jnp.float32)]
-        + [dma((J, 3)), dma((J, 3)), dma((J, 3, 4)), dma((J, 3, 4)), dma((n, 4)), dma((n, 4)), dma((n,))],
+        functools.partial(gather_kernel, jobs, n, expand, reduce),
+        out_shape=[shape((8 * r, c), low) for r, c in shapes]
+        + [
+            shape(maps.shape, full),
+            shape((cells, channels), low),
+            shape((4, 8, LANES), jnp.int32),
+            shape((cells, hidden), full),
+            shape((cells, hidden), low),
+            shape((cells, channels), full),
+            shape((side // 2, side // 2, channels), full),
+        ],
+        in_specs=[anyspec] * n + [whole] * 5,
+        out_specs=[anyspec] * n + [whole] * 3 + [anyspec] + [whole] * 3,
+        scratch_shapes=[
+            VMEM((side + 2 * REACH, side + 2 * EDGE, LANES), full),
+            VMEM((channels, wide), low),
+            VMEM((hidden, STEP), low),
+            VMEM((cells, STEP), full),
+            VMEM((cells, STEP), full),
+            VMEM((STEP // LANES, side, LANES), full),
+        ]
+        + [dma((J, 3)), dma((J, 3)), dma((J, 3, 4)), dma((J, 3, 4)), dma((J, 3)), dma((J, 3))]
+        + [dma((n,)), dma((n,)), dma((n,)), dma((3,)), dma((3,)), dma((2,)), dma((1,))],
         compiler_params=pltpu.CompilerParams(
-            collective_id=0, has_side_effects=True, vmem_limit_bytes=40 * 2**20
+            collective_id=0, has_side_effects=True, vmem_limit_bytes=60 * 2**20
         ),
-    )(*shards, maps, taps, gain.reshape(1, channels))
-    return results[:n], results[n], results[n + 1]
+    )(
+        *shards, maps, taps, gain.reshape(1, channels), scale.reshape(1, channels),
+        jnp.broadcast_to(target, (8, LANES)),
+    )
+    rest = results[n:]
+    return results[:n], rest[0], rest[1], rest[2][:, 0, 0], rest[3], rest[4], rest[5], rest[6]
 
 
 def add_block(total, term):
@@ -189,8 +317,8 @@
 
 
 def scatter_kernel(
-    big0, big1, t0, t1, t2, t3, small_in, grad_normed, mixed, maps, taps, gain,
-    grad_maps, small_out, o0, o1, o2, o3, o4, o5, land0a, land0b, land1a, land1b,
+    big0, big1, land0a, land0b, t0, t1, t2, t3, small_in, grad_normed, mixed, maps, taps, gain,
+    grad_maps, small_out, o0, o1, o2, o3, o4, o5, land1a, land1b,
     acc0a, acc0b, acc1a, acc1b, two0a, two0b, two1a, two1b, tmp0, tmp1,
     own0, own1, own2, own3, two0, two1, two2, two3,
     zr0, zr1, zr2, zr3, zr4, zr5, low0, low1, low2, low3, low4, low5,
@@ -238,24 +366,26 @@
         loaded = fetch(src.at[:, :, index], own)
         return loaded, send(src.at[:, :, 1 - index], two, mask)
 
-    def wide_one(w):
+    def wide_one(w, ours):
         src, acc, land, _, _ = wide[w]
         half = src.shape[5] // 2
         a, b = pl.ds(0, half), pl.ds(half, half)
-        return (
-            fetch(src.at[:, :, :, across, :, a], acc[0]),
-            fetch(src.at[:, :, up, :, :, b], acc[1]),
+        loaded = [fetch(src.at[:, :, :, across, :, a], acc[0]), fetch(src.at[:, :, up, :, :, b], acc[1])]
+        if not ours:
+            return loaded
+        return loaded + [
             send(src.at[:, :, :, 1 - across, :, a], land[0], (1, 0)),
             send(src.at[:, :, 1 - up, :, :, b], land[1], (2, 0)),
-        )
+        ]
 
     def wide_two(w, started):
         src, acc, land, two, tmp = wide[w]
         started[0].wait()
         started[1].wait()
         sent = []
+        for copy in started[2:]:
+            copy.wait_recv()
         for k in range(2):
-            started[2 + k].wait_recv()
             loads = [fetch(land[k].at[0], tmp.at[0])]
             for z in range(4):
                 if z < 3:
@@ -268,13 +398,11 @@
             sent.append(send(acc[k].at[:, :, 1 - index], two[k], mask))
         return sent
 
-    def heights(n, parts):
+    def heights(n, parts, k):
         zr = zrs[n]
         half = zr.shape[3] // len(parts)
         return [
-            send(part.at[height ^ m], zr.at[m - 1, :, :, pl.ds(k * half, half)], (0, 2 * m))
-            for m in (1, 2, 3)
-            for k, part in enumerate(parts)
+            send(parts[k].at[height ^ m], zr.at[m - 1, :, :, pl.ds(k * half, half)], (0, 2 * m)) for m in (1, 2, 3)
         ]
 
     def thin_three(i, started):
@@ -284,7 +412,7 @@
         for z in range(4):
             for c in range(2):
                 two[z, c] = add_block(two[z, c], own[z, c])
-        return heights(i, [two])
+        return heights(i, [two], 0)
 
     def wide_three(w, sent):
         _, acc, _, two, _ = wide[w]
@@ -294,26 +422,37 @@
             for z in range(4):
                 for c in range(2):
                     two[k][z, c] = add_block(two[k][z, c], acc[k][z, c, index])
-        return heights(4 + w, two)
-
-    def total(n, parts, sent):
+        return heights(4 + w, two, 0)
+
+    def total(n, parts, k, sent):
         for copy in sent:
             copy.wait_recv()
         zr, low, whole = zrs[n], lows[n], wholes[n]
-        half = zr.shape[3] // len(parts)
-        for k, part in enumerate(parts):
-            cols = slice(k * half, (k + 1) * half)
-            for c in range(2):
-                value = part[height, c].astype(jnp.float32)
-                for m in range(3):
-                    value = value + zr[m, c, :, cols].astype(jnp.float32)
-                low[c, :, cols] = value.astype(jnp.bfloat16)
-        whole[side] = low[side]
-        return send(low.at[1 - side], whole.at[side], (0, 1))
+        size = zr.shape[3]
+        half = size // len(parts)
+        cols = slice(k * half, (k + 1) * half)
+        for c in range(2):
+            value = parts[k][height, c].astype(jnp.float32)
+            for m in range(3):
+                value = value + zr[m, c, :, cols].astype(jnp.float32)
+            low[c, :, cols] = value.astype(jnp.bfloat16)
+        place = (slice(None), pl.ds(pl.multiple_of(side * size + k * half, LANES), half))
+        whole[place] = low[side, :, cols]
+        return send(low.at[1 - side, :, cols], whole.at[place], (0, 1))
 
     def spread(n, swapped):
         swapped.wait_recv()
         return [fetch(wholes[n], outs[n].at[p])] + [send(wholes[n], outs[n].at[p], (m, 0)) for m in (1, 2, 3)]
+
+    def spread_part(n, k, swapped):
+        swapped.wait_recv()
+        size = zrs[n].shape[3]
+        copies = []
+        for c in range(2):
+            cols = pl.ds(c * size + k * (size // 2), size // 2)
+            src, dst = wholes[n].at[:, cols], outs[n].at[p, :, cols]
+            copies += [fetch(src, dst)] + [send(src, dst, (m, 0)) for m in (1, 2, 3)]
+        return copies
 
     side_cells, _, channels = maps.shape
     count = channels // LANES
@@ -385,56 +524,64 @@
         small_out[...] = value
 
     thin_sent = [thin_two(i) for i in range(4)]
-    one_reduce = wide_one(0)
+    one_reduce = wide_one(0, False)
     norm_back()
-    blocks(0, count // 2)
-    thin_high = [thin_three(0, thin_sent[0]), thin_three(1, thin_sent[1])]
-    one_expand = wide_one(1)
-    blocks(count // 2, 3 * count // 4)
-    thin_high += [thin_three(2, thin_sent[2]), thin_three(3, thin_sent[3])]
-    blocks(3 * count // 4, count)
+    blocks(0, count // 6)
+    two_reduce = wide_two(0, one_reduce)
+    blocks(count // 6, count // 3)
+    thin_high = [thin_three(i, thin_sent[i]) for i in range(4)]
+    one_expand = wide_one(1, True)
+    blocks(count // 3, count // 2)
+    high_reduce = wide_three(0, two_reduce)
+    high_reduce += heights(4, wide[0][3], 1)
+    blocks(count // 2, count)
     small = small_send(0)
-    two_reduce = wide_two(0, one_reduce)
+    two_expand = wide_two(1, one_expand)
     small = small_step(0, small)
-    swaps = [total(i, [thin[i][2]], thin_high[i]) for i in range(2)]
+    swaps = [total(i, [thin[i][2]], 0, thin_high[i]) for i in range(4)]
     small = small_step(1, small)
-    high_reduce = wide_three(0, two_reduce)
-    two_expand = wide_two(1, one_expand)
+    high_expand = wide_three(1, two_expand)
+    last = [spread(i, swaps[i]) for i in range(4)]
     small = small_step(2, small)
-    swaps += [total(i, [thin[i][2]], thin_high[i]) for i in (2, 3)]
-    last = [spread(i, swaps[i]) for i in range(4)]
-    high_expand = wide_three(1, two_expand)
+    for copy in high_reduce:
+        copy.wait_recv()
+    swap_reduce = [total(4, wide[0][3], k, []) for k in range(2)]
+    swap_reduce[0].wait_recv()
+    last.append(spread(4, swap_reduce[1]))
     small = small_step(3, small)
-    swap_reduce = total(4, wide[0][3], high_reduce)
-    last.append(spread(4, swap_reduce))
+    swap_low = total(5, wide[1][3], 0, high_expand)
+    high_expand = heights(5, wide[1][3], 1)
+    last.append(spread_part(5, 0, swap_low))
     small = small_step(4, small)
-    swap_expand = total(5, wide[1][3], high_expand)
-    last.append(spread(5, swap_expand))
+    swap_high = total(5, wide[1][3], 1, high_expand)
+    last.append(spread_part(5, 1, swap_high))
     for group in last:
-        group[0].wait()
-        for copy in group[1:]:
-            copy.wait_recv()
+        for k, copy in enumerate(group):
+            if k % 4:
+                copy.wait_recv()
+            else:
+                copy.wait()
     for copy in copies:
         copy.wait_send()
 
 
-def scatter_gradients(part_reduce, part_expand, thins, small, grad_normed, mixed, maps, taps, gain):
+def scatter_gradients(part_reduce, part_expand, landed, thins, small, grad_normed, mixed, maps, taps, gain):
     side, _, channels = maps.shape
     low, full = jnp.bfloat16, jnp.float32
     anyspec, whole = pl.BlockSpec(memory_space=pl.ANY), pl.BlockSpec(memory_space=VMEM)
     dma = pltpu.SemaphoreType.DMA
     finals = [(t.shape[3], t.shape[4]) for t in thins] + [w.shape[4:] for w in (part_reduce, part_expand)]
-    landing = []
     scratch = []
     for w in (part_reduce, part_expand):
         shape = w.shape[:3] + (w.shape[4], w.shape[5] // 2)
-        landing += [jax.ShapeDtypeStruct(shape, low)] * 2
+        landing = [jax.ShapeDtypeStruct(shape, low)] * 2
         scratch += [VMEM(shape, low)] * 2
     scratch += [VMEM(w.shape[:2] + (w.shape[4], w.shape[5] // 2), low) for w in (part_reduce, part_expand) for _ in range(2)]
     scratch += [VMEM((2, 2, 2, w.shape[4], w.shape[5] // 2), low) for w in (part_reduce, part_expand)]
     scratch += [VMEM(t.shape[:2] + t.shape[3:], low) for t in thins] * 2
     scratch += [VMEM((3, 2) + f, low) for f in finals]
-    scratch += [VMEM((2,) + f, low) for f in finals] * 2
+    scratch += [VMEM((2,) + f, low) for f in finals]
+    scratch += [VMEM((f[0], 2 * f[1]), low) for f in finals]
     edge = (side + 2 * REACH, side + 2 * EDGE, LANES)
     scratch += [VMEM((5,) + small.shape, full)] * 2
     scratch += [VMEM(edge, full)] * 2 + [VMEM((SIDE * SIDE, 8, LANES), full)]
@@ -442,15 +589,15 @@
     results = pl.pallas_call(
         scatter_kernel,
         out_shape=[jax.ShapeDtypeStruct(maps.shape, full), jax.ShapeDtypeStruct(small.shape, full)]
-        + [jax.ShapeDtypeStruct((4, 2) + f, low) for f in finals]
+        + [jax.ShapeDtypeStruct((4, f[0], 2 * f[1]), low) for f in finals]
         + landing,
-        in_specs=[anyspec] * 6 + [whole] * 6,
-        out_specs=[whole] * 2 + [anyspec] * 10,
+        in_specs=[anyspec] * 8 + [whole] * 6,
+        out_specs=[whole] * 2 + [anyspec] * 8,
         scratch_shapes=scratch,
         compiler_params=pltpu.CompilerParams(
             collective_id=1, has_side_effects=True, vmem_limit_bytes=60 * 2**20
         ),
-    )(part_reduce, part_expand, *thins, small, grad_normed, mixed, maps, taps, gain.reshape(1, channels))
+    )(part_reduce, part_expand, *landed, *thins, small, grad_normed, mixed, maps, taps, gain.reshape(1, channels))
     return results[0], results[1], results[2:8]
 
 
@@ -516,14 +663,20 @@
     return product.astype(jnp.bfloat16).reshape(4, 2, 2, 2, rows.shape[1] // 32, half)
 
 
-def across_sum(share, axis):
-    across = place()[2]
-    return add_low(pick(share, across, axis), swap(pick(share, 1 - across, axis), "path", 1))
-
-
-def up_sum(share, axis):
-    up = place()[1]
-    return add_low(pick(share, up, axis), swap(pick(share, 1 - up, axis), "path", 2))
+def across_half(share, axis):
+    return swap(pick(share, 1 - place()[2], axis), "path", 1)
+
+
+def up_half(share, axis):
+    return swap(pick(share, 1 - place()[1], axis), "path", 2)
+
+
+def across_sum(share, axis, other):
+    return add_low(pick(share, place()[2], axis), other)
+
+
+def up_sum(share, axis, other):
+    return add_low(pick(share, place()[1], axis), other)
 
 
 def tie(*values):
@@ -531,8 +684,7 @@
 
 
 def finish(pieces):
-    parts, _, rows, half = pieces.shape
-    return jnp.moveaxis(pieces, 1, 2).reshape(parts * rows, 2 * half).astype(jnp.float32)
+    return pieces.reshape(-1, pieces.shape[2]).astype(jnp.float32)
 
 
 def plain_sum(rows, grads):
@@ -566,9 +718,17 @@
     tuned = lax.axis_size("path") == 4 and lax.axis_size("dev") == 8
     weights = (w_expand, w_reduce, w_adapter, w_qkv, w_out, w_fc1, w_fc2)
     if tuned:
-        fulls, section_mixed, section_normed = gather_weights(
-            weights, hires_maps[0], section_kernel, section_gain
+        ordered, section_mixed, section_rows, spread_targets, expanded, activated_low, reduced, pooled = gather_weights(
+            [weights[i] for i in GATHER_ORDER],
+            hires_maps[0],
+            section_kernel,
+            section_gain,
+            layer_scale,
+            target_path,
+            GATHER_ORDER.index(0),
+            GATHER_ORDER.index(1),
         )
+        fulls = [ordered[GATHER_ORDER.index(i)] for i in range(len(weights))]
     else:
         fulls = [lax.all_gather(shard, "dev", axis=0, tiled=True) for shard in weights]
     full_expand, full_reduce, full_adapter, full_qkv, full_out, full_fc1, full_fc2 = fulls
@@ -585,23 +745,26 @@
     if not tuned:
         section_mixed, section_back = jax.vjp(section_depthwise, maps_float, section_kernel)
         section_normed, section_norm_back = jax.vjp(layer_norm, section_mixed, section_gain)
-    section_rows = section_normed.reshape(-1, channels).astype(jnp.bfloat16)
-    expanded = jnp.dot(section_rows, full_expand, preferred_element_type=jnp.float32)
-    activated, section_gelu_back = jax.vjp(jax.nn.gelu, expanded)
-    activated_low = activated.astype(jnp.bfloat16)
-    reduced = jnp.dot(activated_low, full_reduce, preferred_element_type=jnp.float32).reshape(
-        maps_float.shape
-    )
-    section_out = maps_float + layer_scale * reduced
-    pooled = jnp.mean(
-        section_out.reshape(grid_side, 2, grid_side, 2, channels), axis=(1, 3)
-    ).reshape(tokens, channels)
+    if tuned:
+        _, section_gelu_back = jax.vjp(jax.nn.gelu, expanded)
+        reduced = reduced.reshape(maps_float.shape)
+    else:
+        section_rows = section_normed.reshape(-1, channels).astype(jnp.bfloat16)
+        expanded = jnp.dot(section_rows, full_expand, preferred_element_type=jnp.float32)
+        activated, section_gelu_back = jax.vjp(jax.nn.gelu, expanded)
+        activated_low = activated.astype(jnp.bfloat16)
+        reduced = jnp.dot(activated_low, full_reduce, preferred_element_type=jnp.float32).reshape(
+            maps_float.shape
+        )
+        section_out = maps_float + layer_scale * reduced
+        pooled = jnp.mean(
+            section_out.reshape(grid_side, 2, grid_side, 2, channels), axis=(1, 3)
+        ).reshape(tokens, channels)
     pieces = pooled.astype(jnp.bfloat16).reshape(path_count, quarter_rows, channels)
-    own_target = jnp.broadcast_to(target_path, (path_count, 1))
-    spread_pieces, spread_targets = (
-        lax.all_to_all(pieces, "path", split_axis=0, concat_axis=0, tiled=True),
-        lax.all_to_all(own_target, "path", split_axis=0, concat_axis=0, tiled=True),
-    )
+    spread_pieces = lax.all_to_all(pieces, "path", split_axis=0, concat_axis=0, tiled=True)
+    if not tuned:
+        own_target = jnp.broadcast_to(target_path, (path_count, 1))
+        spread_targets = lax.all_to_all(own_target, "path", split_axis=0, concat_axis=0, tiled=True)
     selector = (
         jnp.arange(path_count, dtype=jnp.int32)[:, None] == spread_targets.reshape(1, path_count)
     ).astype(jnp.float32)
@@ -702,6 +865,8 @@
     else:
         grad_adapter_w = plain_sum(features, grad_adapted_low)
     grad_features = jnp.dot(grad_adapted_low, full_adapter.T, preferred_element_type=jnp.float32)
+    if tuned:
+        grad_features, part_fc2, part_fc1 = tie(grad_features, part_fc2, part_fc1)
     grad_pieces = grad_features.astype(jnp.bfloat16).reshape(path_count, quarter_rows, channels)
     grad_routed = lax.all_to_all(grad_pieces, "path", split_axis=0, concat_axis=0, tiled=True)
     grad_unrouted = jnp.einsum("pq,ptc->qtc", selector, grad_routed.astype(jnp.float32)).astype(
@@ -709,9 +874,9 @@
     )
     grad_home = lax.all_to_all(grad_unrouted, "path", split_axis=0, concat_axis=0, tiled=True)
     if tuned:
-        step_fc2, step_fc1 = across_sum(part_fc2, 3), up_sum(part_fc1, 2)
-        step_qkv = across_sum(part_qkv, 3)
-        step_rest = up_sum(jnp.concatenate([part_out, part_adapter], axis=4), 2)
+        part_rest = jnp.concatenate([part_out, part_adapter], axis=4)
+        grad_home, part_fc2, part_fc1, part_qkv, part_rest = tie(grad_home, part_fc2, part_fc1, part_qkv, part_rest)
+        half_fc2, half_fc1 = across_half(part_fc2, 3), up_half(part_fc1, 2)
     grad_pooled = grad_home.astype(jnp.float32).reshape(tokens, channels)
     quarter = (grad_pooled * 0.25).reshape(1, grid_side, 1, grid_side, 1, channels)
     grad_section_out = jnp.broadcast_to(quarter, (1, grid_side, 2, grid_side, 2, channels)).reshape(
@@ -721,12 +886,14 @@
     grad_reduced = (grad_section_out * layer_scale).reshape(-1, channels).astype(jnp.bfloat16)
     if tuned:
         part_reduce = pair_gradient(both_images(activated_low), grad_reduced)
+        grad_reduced, part_reduce, half_fc2, half_fc1 = tie(grad_reduced, part_reduce, half_fc2, half_fc1)
+        half_qkv, half_rest = across_half(part_qkv, 3), up_half(part_rest, 2)
+        columns = part_reduce.shape[5] // 2
+        landed = [across_half(part_reduce[..., :columns], 3), up_half(part_reduce[..., columns:], 2)]
     else:
         grad_reduce_w = plain_sum(activated_low, grad_reduced)
     grad_activated = jnp.dot(grad_reduced, full_reduce.T, preferred_element_type=jnp.float32)
     grad_expanded = section_gelu_back(grad_activated)[0].astype(jnp.bfloat16)
-    if tuned:
-        grad_expanded, part_reduce, step_fc2, step_fc1 = tie(grad_expanded, part_reduce, step_fc2, step_fc1)
     if tuned:
         part_expand = pair_gradient(both_images(section_rows), grad_expanded)
     else:
@@ -735,6 +902,9 @@
         grad_expanded, full_expand.T, preferred_element_type=jnp.float32
     ).reshape(maps_float.shape)
     if tuned:
+        part_expand, half_qkv, half_rest = tie(part_expand, half_qkv, half_rest)
+        step_fc2, step_fc1 = across_sum(part_fc2, 3, half_fc2), up_sum(part_fc1, 2, half_fc1)
+        step_qkv, step_rest = across_sum(part_qkv, 3, half_qkv), up_sum(part_rest, 2, half_rest)
         small_rows = jnp.concatenate(
             [
                 jnp.zeros((section_kernel.shape[0] + 1, channels), jnp.float32),
@@ -747,6 +917,7 @@
         grad_maps, small_rows, pieces = scatter_gradients(
             part_reduce,
             part_expand,
+            landed,
             [step_fc2, step_fc1, step_qkv, step_rest],
             small_rows,
             grad_section_normed[0],
@@ -758,7 +929,7 @@
         grad_maps = grad_maps[None] + grad_section_out
         split = part_out.shape[4]
         grad_fc2_w, grad_fc1_w, grad_qkv_w = [finish(piece) for piece in pieces[:3]]
-        grad_out_w, grad_adapter_w = finish(pieces[3][:, :, :split]), finish(pieces[3][:, :, split:])
+        grad_out_w, grad_adapter_w = finish(pieces[3][:, :split]), finish(pieces[3][:, split:])
         grad_reduce_w, grad_expand_w = finish(pieces[4]), finish(pieces[5])
     else:
         grad_section_mixed, grad_section_gain = section_norm_back(grad_section_normed)

time: 999 us -> 896 us (0.90)
  Pallas kernels: 578 us -> 527 us
  matrix products: 182 us -> 144 us
  local copies, waits for them, and re-layouts: 96 us -> 74.2 us
    pallas_call x1, Pallas kernels: 336 us -> 259 us  [scatter_gradients(): pl.pallas_call(scatter_kernel, out_shape=[jax.ShapeDtypeStruct(maps.shape...]
    dot_general x2 -> x0, matrix products: 39.1 us -> none  [the longest x1 22.8 us: local(): jnp.dot(section_rows, full_expand, preferred_element_type=jnp.float32)]
    pallas_call x1, Pallas kernels: 242 us -> 268 us  [gather_weights(): pl.pallas_call(functools.partial(gather_kernel, jobs, n, expand, reduce),...]
    unnamed x185 -> x150, local copies, waits for them, and re-layouts: 38 us -> 11.6 us
    convert_element_type x8 -> x0, local copies, waits for them, and re-layouts: 15 us -> none  [the longest x7 13 us: finish(): jnp.moveaxis(pieces, 1, 2).reshape(parts * rows, 2 * half)]
    ppermute x18 -> x20, waiting for transfers between devices: 35.5 us -> 44.2 us  [swap(): return lax.ppermute(value, axis, [(i, i ^ mask) for i in range(size)])]
  transfers between devices with their start and end apart: 23 -> 24, of which waited for: 6 -> 6; matrix products, arithmetic and copies ran while one was open for 25% -> 26% of each run, Pallas kernels for 24% -> 0%
where the time goes in v3:
time: 896 us; the launch traced here: 888 us
  Pallas kernels  527 us (59%)
  matrix products  144 us (16%)
  local copies, waits for them, and re-layouts  74.2 us (8%)
  waiting for transfers between devices  56.6 us (6%)
  other arithmetic  56 us (6%)
  starting transfers between devices  27.5 us (3%)
    pallas_call x1, Pallas kernels, gather_weights(): pl.pallas_call(functools.partial(gather_kernel, jobs, n, expand, reduce),...  268 us
    pallas_call x1, Pallas kernels, scatter_gradients(): pl.pallas_call(scatter_kernel, out_shape=[jax.ShapeDtypeStruct(maps.shape...  259 us
    dot_general x7, matrix products, pair_gradient(): lax.dot_general(rows, jnp.concatenate([mine, theirs]), (((0,), (0,)), (()...  57.8 us
    ppermute x20, waiting for transfers between devices, swap(): return lax.ppermute(value, axis, [(i, i ^ mask) for i in range(size)])  44.2 us
    dot_general x1, matrix products, local(): jnp.dot(grad_reduced, full_reduce.T, preferred_element_type=jnp.float32)  24.3 us
    dot_general x1, matrix products, local(): jnp.dot(grad_expanded, full_expand.T, preferred_element_type=jnp.float32)  18.3 us
  transfers between devices with their start and end apart: 24, of which 6 were waited for; matrix products, arithmetic and copies ran while one was open for 26% of the time, Pallas kernels for 0%

profile of v3, /device:TPU:0, one launch (start us, length us, event | category | flops | bytes accessed | tf_op | source)
XLA Modules:
  0.0 887.9 jit_solution(14250845458172927249)
XLA Ops:
  4.5 268.0 %shard_map.305 = (bf16[1024,1024]{1,0:T(8,128)(2,1)}, bf16[1536,6144]{1,0:T(8,128)(2,1)}, bf16[6144,1536]{1,0:T(8,128)(2,1)}, bf16[1024,4096]{1,0:T(8,128)(2,1)}...) custom-call(bf16[128,1024]{1,0:T(8,128)(2,1)} %refs_0_.1, ...), custom_call_target="tpu_custom_call" | custom-call | tf_op jit(solution)/shard_map/pallas_call | solution.py:280
  274.7 4.3 all-to-all-start
  280.1 6.7 all-to-all-done
  289.2 4.3 all-to-all-start.1
  295.3 4.9 all-to-all-done.1
  307.0 4.0 convolution_convert_fusion.4
  322.7 7.0 multiply_convert_fusion.2
  329.7 3.7 fusion.31
  373.4 5.7 convolution_convert_fusion.3
  379.7 6.2 convolution_convert_fusion.1
  407.0 4.6 convolution_convert_fusion.2
  419.3 4.0 multiply_reduce_fusion
  434.5 3.7 broadcast_in_dim.99
  442.0 19.1 %fusion.12 = bf16[6144,768]{1,0:T(8,128)(2,1)} fusion(bf16[576,6144]{1,0:T(8,128)(2,1)} %collective-permute-done.10, bf16[576,6144]{1,0:T(8,128)(2,1)} %get-tuple-element.65, bf16[576,768]{1,0:T(8,128)(2,1)} %collective-permute-done.11, bf16[576,768]{1,0:T(8,128)(2,1)} %get-tuple-element.121), kind=kOutput, calls=%fused_computation.15 | convolution fusion | flops 10908205056 | bytes 25362432 | tf_op jit(solution)/shard_map/dot_general | solution.py:660
  461.0 14.0 %collective-permute-done.12 = bf16[4,2,2,128,512]{4,3,2,1,0:T(8,128)(2,1)} collective-permute-done((bf16[4,2,2,128,512]{4,3,2,1,0:T(8,128)(2,1)}, bf16[4,2,2,128,512]{4,3,2,1,0:T(8,128)(2,1)}, u32[]{:S(2)}, u32[]{:S(2)}) %collective-permute-start.12) | collective-permute-done | bytes 2097184 | tf_op jit(solution)/shard_map/ppermute | solution.py:634
  478.5 24.3 %fusion.7 = bf16[576,6144]{1,0:T(8,128)(2,1)} fusion(f32[576,6144]{1,0:T(8,128)} %get-tuple-element.72, bf16[576,1536]{1,0:T(8,128)(2,1)S(1)} %copy-done.8, bf16[6144,1536]{1,0:T(8,128)(2,1)} %get-tuple-element.71), kind=kOutput, calls=%fused_computation.9 | convolution fusion | flops 10942414848 | bytes 41877504 | tf_op jit(solution)/shard_map/dot_general | solution.py:895
  502.8 6.1 broadcast_select_fusion.1
  511.1 5.5 fusion.107
  521.7 18.3 %fusion.115 = f32[576,1536]{1,0:T(8,128)} fusion(bf16[576,6144]{1,0:T(8,128)(2,1)} %fusion.7, bf16[1536,6144]{1,0:T(8,128)(2,1)} %get-tuple-element.81), kind=kOutput, calls=%fused_computation.237 | convolution fusion | flops 10871635968 | bytes 29491200 | tf_op jit(solution)/shard_map/dot_general | solution.py:901
  543.1 3.7 fusion.19.t0
  546.8 3.8 fusion.18.t1
  552.2 17.3 %convolution_convert_fusion = bf16[1536,3072]{1,0:T(8,128)(2,1)} fusion(bf16[576,3072]{1,0:T(8,128)(2,1)} %collective-permute-done.15, bf16[576,3072]{1,0:T(8,128)(2,1)S(1)} %copy-done.16, bf16[576,1536]{1,0:T(8,128)(2,1)} %collective-permute-done.14, bf16[576,1536]{1,0:T(8,128)(2,1)S(1)} %copy-done.62), kind=kOutput, calls=%fused_computation.14 | convolution fusion | flops 10897588224 | bytes 20054016 | tf_op jit(solution)/shard_map/dot_general | solution.py:660
  575.5 26.7 %collective-permute-done.19.land0b = bf16[4,2,2,192,384]{4,3,2,1,0:T(8,128)(2,1)S(1)} collective-permute-done((bf16[4,2,2,192,384]{4,3,2,1,0:T(8,128)(2,1)}, bf16[4,2,2,192,384]{4,3,2,1,0:T(8,128)(2,1)S(1)}, u32[]{:S(2)}, u32[]{:S(2)}) %collective-permute-start.19) | collective-permute-done | bytes 2359328 | tf_op jit(solution)/shard_map/ppermute | solution.py:634
  603.6 258.9 %shard_map.306 = (f32[24,24,1536]{2,1,0:T(8,128)}, f32[64,1536]{1,0:T(8,128)}, bf16[4,128,1024]{2,1,0:T(8,128)(2,1)}, bf16[4,32,4096]{2,1,0:T(8,128)(2,1)}, bf16...) custom-call(bf16[4,2,2,2,192,768]{5,4,3,2,1,0:T(8,128)(2,1)} %bitcas, ...), custom_call_target="tpu_custom_call" | custom-call | tf_op jit(solution)/shard_map/pallas_call | solution.py:589
  (308 shorter events, 160.5 us)
Async XLA Ops:
  274.7 12.0 %all-to-all-start = ((bf16[4,36,1536]{2,1,0:T(8,128)(2,1)}), bf16[4,36,1536]{2,1,0:T(8,128)(2,1)}, u32[]{:S(2)}, u32[]{:S(2)}) async-start(bf16[4,36,1536]{2,1,0:T(8,128)(2,1)} %reshape.457), calls=%async_computation | async-start | bytes 983040 | tf_op jit(solution)/shard_map/all_to_all | solution.py:764
  289.2 11.0 %all-to-all-start.1 = ((bf16[4,36,1536]{2,1,0:T(8,128)(2,1)}), bf16[4,36,1536]{2,1,0:T(8,128)(2,1)}, u32[]{:S(2)}, u32[]{:S(2)}) async-start(bf16[4,36,1536]{2,1,0:T(8,128)(2,1)} %copy.74), calls=%async_computation.1 | async-start | bytes 983040 | tf_op jit(solution)/shard_map/all_to_all | solution.py:774
  294.3 84.8 %collective-permute-start.1 = (bf16[144,512]{1,0:T(8,128)(2,1)}, bf16[144,512]{1,0:T(8,128)(2,1)}, u32[]{:S(2)}, u32[]{:S(2)}) collective-permute-start(bf16[144,512]{1,0:T(8,128)(2,1)} %get-tuple-element.144), channel_id=1, source_target_pairs={{0,1},{1,0},{2,3},{3,2},{4,5},{5,4},{6,7},{7,6},{8,9},{9,8},{10,11... | collective-permute-start | bytes 442376 | tf_op jit(solution)/shard_map/ppermute | solution.py:634
  294.3 147.1 %collective-permute-start.10 = (bf16[576,6144]{1,0:T(8,128)(2,1)}, bf16[576,6144]{1,0:T(8,128)(2,1)}, u32[]{:S(2)}, u32[]{:S(2)}) collective-permute-start(bf16[576,6144]{1,0:T(8,128)(2,1)} %get-tuple-element.65), channel_id=1, source_target_pairs={{0,1},{1,0},{2,3},{3,2},{4,5},{5,4},{6,7},{7,6},{8,9},{9,8},{10,11... | collective-permute-start | bytes 21233672 | tf_op jit(solution)/shard_map/ppermute | solution.py:634
  349.4 23.5 %collective-permute-start.2 = (bf16[144,1024]{1,0:T(8,128)(2,1)}, bf16[144,1024]{1,0:T(8,128)(2,1)}, u32[]{:S(2)}, u32[]{:S(2)}) collective-permute-start(bf16[144,1024]{1,0:T(8,128)(2,1)} %multiply_convert_fusion.3), channel_id=1, source_target_pairs={{0,1},{1,0},{2,3},{3,2},{4,5},{5,4},{6,7},{7,6},{8,9},{9,8},{10,11... | collective-permute-start | bytes 884744 | tf_op jit(solution)/shard_map/ppermute | solution.py:634
  353.7 25.9 %collective-permute-start = (bf16[144,4096]{1,0:T(8,128)(2,1)}, bf16[144,4096]{1,0:T(8,128)(2,1)}, u32[]{:S(2)}, u32[]{:S(2)}) collective-permute-start(bf16[144,4096]{1,0:T(8,128)(2,1)} %get-tuple-element.161), channel_id=1, source_target_pairs={{0,1},{1,0},{2,3},{3,2},{4,5},{5,4},{6,7},{7,6},{8,9},{9,8},{10,11... | collective-permute-start | bytes 3538952 | tf_op jit(solution)/shard_map/ppermute | solution.py:634
  354.2 19.1 %collective-permute-start.3 = (bf16[144,2048]{1,0:T(8,128)(2,1)}, bf16[144,2048]{1,0:T(8,128)(2,1)}, u32[]{:S(2)}, u32[]{:S(2)}) collective-permute-start(bf16[144,2048]{1,0:T(8,128)(2,1)} %get-tuple-element.124), channel_id=1, source_target_pairs={{0,1},{1,0},{2,3},{3,2},{4,5},{5,4},{6,7},{7,6},{8,9},{9,8},{10,11... | collective-permute-start | bytes 1769480 | tf_op jit(solution)/shard_map/ppermute | solution.py:634
  372.9 21.8 %collective-permute-start.8 = (bf16[144,1536]{1,0:T(8,128)(2,1)}, bf16[144,1536]{1,0:T(8,128)(2,1)S(1)}, u32[]{:S(2)}, u32[]{:S(2)}) collective-permute-start(bf16[144,1536]{1,0:T(8,128)(2,1)} %reshape.458), channel_id=1, source_target_pairs={{0,1},{1,0},{2,3},{3,2},{4,5},{5,4},{6,7},{7,6},{8,9},{9,8},{10,11... | collective-permute-start | bytes 1327112 | tf_op jit(solution)/shard_map/ppermute | solution.py:634
  373.3 17.9 %collective-permute-start.6 = (bf16[144,1024]{0,1:T(8,128)(2,1)}, bf16[144,1024]{0,1:T(8,128)(2,1)S(1)}, u32[]{:S(2)}, u32[]{:S(2)}) collective-permute-start(bf16[144,1024]{0,1:T(8,128)(2,1)} %bitcast.14), channel_id=1, source_target_pairs={{0,1},{1,0},{2,3},{3,2},{4,5},{5,4},{6,7},{7,6},{8,9},{9,8},{10,11... | collective-permute-start | bytes 884744 | tf_op jit(solution)/shard_map/ppermute | solution.py:634
  379.1 15.1 %collective-permute-start.9 = (bf16[144,512]{1,0:T(8,128)(2,1)S(1)}, bf16[144,512]{1,0:T(8,128)(2,1)S(1)}, u32[]{:S(2)}, u32[]{:S(2)}) collective-permute-start(bf16[144,512]{1,0:T(8,128)(2,1)S(1)} %copy-done.51), channel_id=1, source_target_pairs={{0,1},{1,0},{2,3},{3,2},{4,5},{5,4},{6,7},{7,6},{8,9},{9,8},{10,11... | collective-permute-start | bytes 442376 | tf_op jit(solution)/shard_map/ppermute | solution.py:634
  379.6 11.3 %collective-permute-start.7 = (bf16[144,512]{1,0:T(8,128)(2,1)S(1)}, bf16[144,512]{1,0:T(8,128)(2,1)S(1)}, u32[]{:S(2)}, u32[]{:S(2)}) collective-permute-start(bf16[144,512]{1,0:T(8,128)(2,1)S(1)} %copy-done.52), channel_id=1, source_target_pairs={{0,1},{1,0},{2,3},{3,2},{4,5},{5,4},{6,7},{7,6},{8,9},{9,8},{10,11... | collective-permute-start | bytes 442376 | tf_op jit(solution)/shard_map/ppermute | solution.py:634
  386.7 12.0 %all-to-all-start.2 = ((bf16[4,36,1536]{2,1,0:T(8,128)(2,1)}), bf16[4,36,1536]{2,1,0:T(8,128)(2,1)S(1)}, u32[]{:S(2)}, u32[]{:S(2)}) async-start(bf16[4,36,1536]{2,1,0:T(8,128)(2,1)} %reshape.472), calls=%async_computation.2 | async-start | bytes 983040 | tf_op jit(solution)/shard_map/all_to_all | solution.py:871
  390.9 159.8 %collective-permute-start.14 = (bf16[576,1536]{1,0:T(8,128)(2,1)}, bf16[576,1536]{1,0:T(8,128)(2,1)}, u32[]{:S(2)}, u32[]{:S(2)}) collective-permute-start(bf16[576,1536]{1,0:T(8,128)(2,1)} %get-tuple-element.69), channel_id=1, source_target_pairs={{0,1},{1,0},{2,3},{3,2},{4,5},{5,4},{6,7},{7,6},{8,9},{9,8},{10,11... | collective-permute-start | bytes 5308424 | tf_op jit(solution)/shard_map/ppermute | solution.py:634
  391.3 15.7 %collective-permute-start.4 = (bf16[144,1024]{1,0:T(8,128)(2,1)S(1)}, bf16[144,1024]{1,0:T(8,128)(2,1)}, u32[]{:S(2)}, u32[]{:S(2)}) collective-permute-start(bf16[144,1024]{1,0:T(8,128)(2,1)S(1)} %copy-done.29), channel_id=1, source_target_pairs={{0,1},{1,0},{2,3},{3,2},{4,5},{5,4},{6,7},{7,6},{8,9},{9,8},{10,11... | collective-permute-start | bytes 884744 | tf_op jit(solution)/shard_map/ppermute | solution.py:634
  394.2 12.8 %collective-permute-start.5 = (bf16[144,1536]{1,0:T(8,128)(2,1)S(1)}, bf16[144,1536]{1,0:T(8,128)(2,1)}, u32[]{:S(2)}, u32[]{:S(2)}) collective-permute-start(bf16[144,1536]{1,0:T(8,128)(2,1)S(1)} %copy-done.45), channel_id=1, source_target_pairs={{0,1},{1,0},{2,3},{3,2},{4,5},{5,4},{6,7},{7,6},{8,9},{9,8},{10,11... | collective-permute-start | bytes 1327112 | tf_op jit(solution)/shard_map/ppermute | solution.py:634
  400.0 11.6 %all-to-all-start.3 = ((bf16[4,36,1536]{2,1,0:T(8,128)(2,1)}), bf16[4,36,1536]{2,1,0:T(8,128)(2,1)S(1)}, u32[]{:S(2)}, u32[]{:S(2)}) async-start(bf16[4,36,1536]{2,1,0:T(8,128)(2,1)} %copy.88), calls=%async_computation.3 | async-start | bytes 983040 | tf_op jit(solution)/shard_map/all_to_all | solution.py:875
  424.8 15.2 %collective-permute-start.11 = (bf16[576,768]{1,0:T(8,128)(2,1)}, bf16[576,768]{1,0:T(8,128)(2,1)}, u32[]{:S(2)}, u32[]{:S(2)}) collective-permute-start(bf16[576,768]{1,0:T(8,128)(2,1)} %get-tuple-element.122), channel_id=1, source_target_pairs={{0,1},{1,0},{2,3},{3,2},{4,5},{5,4},{6,7},{7,6},{8,9},{9,8},{10,11... | collective-permute-start | bytes 2654216 | tf_op jit(solution)/shard_map/ppermute | solution.py:634
  426.2 48.8 %collective-permute-start.12 = (bf16[4,2,2,128,512]{4,3,2,1,0:T(8,128)(2,1)}, bf16[4,2,2,128,512]{4,3,2,1,0:T(8,128)(2,1)}, u32[]{:S(2)}, u32[]{:S(2)}) collective-permute-start(bf16[4,2,2,128,512]{4,3,2,1,0:T(8,128)(2,1)} %dynamic-slice_bitcast_fusion.3), channel_id=1, source_target_pairs={{0,8},{8,0},{16,24},{24,16},{1,9},{9,1},{17,25},{25,17},{2,10},{10... | collective-permute-start | bytes 6291464 | tf_op jit(solution)/shard_map/ppermute | solution.py:634
  429.7 48.8 %collective-permute-start.13 = (bf16[4,2,2,32,2048]{4,3,2,1,0:T(8,128)(2,1)}, bf16[4,2,2,32,2048]{4,3,2,1,0:T(8,128)(2,1)}, u32[]{:S(2)}, u32[]{:S(2)}) collective-permute-start(bf16[4,2,2,32,2048]{4,3,2,1,0:T(8,128)(2,1)} %dynamic-slice_bitcast_fusion.2), channel_id=1, source_target_pairs={{0,16},{8,24},{16,0},{24,8},{1,17},{9,25},{17,1},{25,9},{2,18},{10... | collective-permute-start | bytes 6291464 | tf_op jit(solution)/shard_map/ppermute | solution.py:634
  439.9 129.6 %collective-permute-start.16 = (bf16[4,2,2,32,1536]{4,3,2,1,0:T(8,128)(2,1)}, bf16[4,2,2,32,1536]{4,3,2,1,0:T(8,128)(2,1)}, u32[]{:S(2)}, u32[]{:S(2)}) collective-permute-start(bf16[4,2,2,32,1536]{4,3,2,1,0:T(8,128)(2,1)} %dynamic-slice_bitcast_fusion.4), channel_id=1, source_target_pairs={{0,8},{8,0},{16,24},{24,16},{1,9},{9,1},{17,25},{25,17},{2,10},{10... | collective-permute-start | bytes 4718600 | tf_op jit(solution)/shard_map/ppermute | solution.py:634
  441.4 128.1 %collective-permute-start.17 = (bf16[4,2,2,80,512]{4,3,2,1,0:T(8,128)(2,1)}, bf16[4,2,2,80,512]{4,3,2,1,0:T(8,128)(2,1)}, u32[]{:S(2)}, u32[]{:S(2)}) collective-permute-start(bf16[4,2,2,80,512]{4,3,2,1,0:T(8,128)(2,1)} %dynamic-slice_bitcast_fusion.5), channel_id=1, source_target_pairs={{0,16},{8,24},{16,0},{24,8},{1,17},{9,25},{17,1},{25,9},{2,18},{10... | collective-permute-start | bytes 3932168 | tf_op jit(solution)/shard_map/ppermute | solution.py:634
  508.9 43.2 %collective-permute-start.15 = (bf16[576,3072]{1,0:T(8,128)(2,1)}, bf16[576,3072]{1,0:T(8,128)(2,1)}, u32[]{:S(2)}, u32[]{:S(2)}) collective-permute-start(bf16[576,3072]{1,0:T(8,128)(2,1)} %get-tuple-element.118), channel_id=1, source_target_pairs={{0,1},{1,0},{2,3},{3,2},{4,5},{5,4},{6,7},{7,6},{8,9},{9,8},{10,11... | collective-permute-start | bytes 10616840 | tf_op jit(solution)/shard_map/ppermute | solution.py:634
  520.2 55.3 %collective-permute-start.18 = (bf16[4,2,2,192,384]{4,3,2,1,0:T(8,128)(2,1)}, bf16[4,2,2,192,384]{4,3,2,1,0:T(8,128)(2,1)}, u32[]{:S(2)}, u32[]{:S(2)}) collective-permute-start(bf16[4,2,2,192,384]{4,3,2,1,0:T(8,128)(2,1)} %dynamic-slice_bitcast_fusion.1), channel_id=1, source_target_pairs={{0,8},{8,0},{16,24},{24,16},{1,9},{9,1},{17,25},{25,17},{2,10},{10... | collective-permute-start | bytes 7077896 | tf_op jit(solution)/shard_map/ppermute | solution.py:634
  550.7 51.5 %collective-permute-start.19 = (bf16[4,2,2,192,384]{4,3,2,1,0:T(8,128)(2,1)}, bf16[4,2,2,192,384]{4,3,2,1,0:T(8,128)(2,1)S(1)}, u32[]{:S(2)}, u32[]{:S(2)}) collective-permute-start(bf16[4,2,2,192,384]{4,3,2,1,0:T(8,128)(2,1)} %dynamic-slice_bitcast_fusion), channel_id=1, source_target_pairs={{0,16},{8,24},{16,0},{24,8},{1,17},{9,25},{17,1},{25,9},{2,18},{10... | collective-permute-start | bytes 7077896 | tf_op jit(solution)/shard_map/ppermute | solution.py:634
  (75 other events, 495.8 us)

commit v4 on v3

--- a/solution.py
+++ b/solution.py
@@ -106,9 +106,9 @@
     shards = refs[:count]
     maps, taps, gain, scale, target = refs[count : count + 5]
     fulls = refs[count + 5 : 2 * count + 5]
-    mixed, rows, targets, expanded, active, reduced, pooled = refs[2 * count + 5 : 2 * count + 12]
-    pad, wide_w, deep_w, total, stage, pair_sum = refs[2 * count + 12 : 2 * count + 18]
-    zs, zr, ps, pr, cs, cr, os, orr, ls, ts, tr, ws, es = refs[2 * count + 18 :]
+    mixed, rows, targets, expanded, active, reduced, features = refs[2 * count + 5 : 2 * count + 12]
+    pad, wide_w, deep_w, total, stage, pair_sum, pooled, leaving, met, sorted_maps, landing = refs[2 * count + 12 : 2 * count + 23]
+    zs, zr, ps, pr, cs, cr, os, orr, ls, ts, tr, ws, es, fs, fr, gs, gr = refs[2 * count + 23 :]
     p, d = lax.axis_index("path"), lax.axis_index("dev")
 
     def at(m):
@@ -219,6 +219,43 @@
 
         lax.fori_loop(0, side // 2, pool, 0)
 
+    parts = maps.shape[2] // 4
+
+    def hop(src, dst, ss, rs):
+        return [copy(src.at[p ^ m], dst.at[p], ss.at[m - 1], rs.at[m - 1], (m, 0)) for m in (1, 2, 3)]
+
+    def route_one():
+        for k in range(4):
+            leaving[k] = pooled[..., k * parts : (k + 1) * parts].reshape(leaving.shape[1:]).astype(jnp.bfloat16)
+        met[p] = leaving[p]
+        sent = hop(leaving, met, fs, fr)
+        for c in sent:
+            c.start()
+        return sent
+
+    def route_two(sent):
+        for c in sent + named:
+            c.wait()
+        for k in range(4):
+            chosen = jnp.zeros(met.shape[1:], jnp.float32)
+            for q in range(4):
+                here = targets[q, :1, :1] == k
+                chosen += jnp.where(here, met[q].astype(jnp.float32), 0.0)
+            sorted_maps[k] = chosen.astype(jnp.bfloat16)
+        landing[p] = sorted_maps[p]
+        sent = hop(sorted_maps, landing, gs, gr)
+        for c in sent:
+            c.start()
+        return sent
+
+    def route_three(sent):
+        for c in sent:
+            c.wait()
+        for k in range(4):
+            features[:, k * parts : (k + 1) * parts] = landing[k]
+
+    last_reduce = max(i for i in range(J) if jobs[i][0] == reduce)
+    routed = None
     for i in range(J + 3):
         if i < J:
             for k in range(3):
@@ -248,8 +285,12 @@
                 expand_block(c0, nc)
             if w == reduce:
                 reduce_block(c0, nc)
-    for c in named:
-        c.wait()
+            if i - 3 == last_reduce:
+                routed = route_one()
+            if i - 3 == last_reduce + 1:
+                routed = route_two(routed)
+            if i - 3 == last_reduce + 2:
+                route_three(routed)
     for w in range(count):
         ensure(w)
         own[w][1].wait_send()
@@ -287,7 +328,7 @@
             shape((cells, hidden), full),
             shape((cells, hidden), low),
             shape((cells, channels), full),
-            shape((side // 2, side // 2, channels), full),
+            shape((cells // 4, channels), low),
         ],
         in_specs=[anyspec] * n + [whole] * 5,
         out_specs=[anyspec] * n + [whole] * 3 + [anyspec] + [whole] * 3,
@@ -298,9 +339,14 @@
             VMEM((cells, STEP), full),
             VMEM((cells, STEP), full),
             VMEM((STEP // LANES, side, LANES), full),
+            VMEM((side // 2, side // 2, channels), full),
+            VMEM((4, cells // 4, channels // 4), low),
+            VMEM((4, cells // 4, channels // 4), low),
+            VMEM((4, cells // 4, channels // 4), low),
+            VMEM((4, cells // 4, channels // 4), low),
         ]
         + [dma((J, 3)), dma((J, 3)), dma((J, 3, 4)), dma((J, 3, 4)), dma((J, 3)), dma((J, 3))]
-        + [dma((n,)), dma((n,)), dma((n,)), dma((3,)), dma((3,)), dma((2,)), dma((1,))],
+        + [dma((n,)), dma((n,)), dma((n,)), dma((3,)), dma((3,)), dma((2,)), dma((1,))] + [dma((3,))] * 4,
         compiler_params=pltpu.CompilerParams(
             collective_id=0, has_side_effects=True, vmem_limit_bytes=60 * 2**20
         ),
@@ -317,7 +363,7 @@
 
 
 def scatter_kernel(
-    big0, big1, land0a, land0b, t0, t1, t2, t3, small_in, grad_normed, mixed, maps, taps, gain,
+    big0, big1, land0a, land0b, land0c, land0d, t0, t1, t2, t3, small_in, grad_normed, mixed, maps, taps, gain,
     grad_maps, small_out, o0, o1, o2, o3, o4, o5, land1a, land1b,
     acc0a, acc0b, acc1a, acc1b, two0a, two0b, two1a, two1b, tmp0, tmp1,
     own0, own1, own2, own3, two0, two1, two2, two3,
@@ -354,8 +400,8 @@
 
     thin = [(t0, own0, two0, True), (t1, own1, two1, False), (t2, own2, two2, True), (t3, own3, two3, False)]
     wide = [
-        (big0, (acc0a, acc0b), (land0a, land0b), (two0a, two0b), tmp0),
-        (big1, (acc1a, acc1b), (land1a, land1b), (two1a, two1b), tmp1),
+        (big0, (acc0a, acc0b), ((land0a, land0b), (land0c, land0d)), (two0a, two0b), tmp0),
+        (big1, (acc1a, acc1b), ((land1a,), (land1b,)), (two1a, two1b), tmp1),
     ]
     outs = [o0, o1, o2, o3, o4, o5]
     zrs, lows, wholes = [zr0, zr1, zr2, zr3, zr4, zr5], [low0, low1, low2, low3, low4, low5], [full0, full1, full2, full3, full4, full5]
@@ -374,8 +420,8 @@
         if not ours:
             return loaded
         return loaded + [
-            send(src.at[:, :, :, 1 - across, :, a], land[0], (1, 0)),
-            send(src.at[:, :, 1 - up, :, :, b], land[1], (2, 0)),
+            send(src.at[:, :, :, 1 - across, :, a], land[0][0], (1, 0)),
+            send(src.at[:, :, 1 - up, :, :, b], land[1][0], (2, 0)),
         ]
 
     def wide_two(w, started):
@@ -386,10 +432,11 @@
         for copy in started[2:]:
             copy.wait_recv()
         for k in range(2):
-            loads = [fetch(land[k].at[0], tmp.at[0])]
+            each = 4 // len(land[k])
+            loads = [fetch(land[k][0].at[0], tmp.at[0])]
             for z in range(4):
                 if z < 3:
-                    loads.append(fetch(land[k].at[z + 1], tmp.at[(z + 1) % 2]))
+                    loads.append(fetch(land[k][(z + 1) // each].at[(z + 1) % each], tmp.at[(z + 1) % 2]))
                 loads[z].wait()
                 for c in range(2):
                     for q in range(2):
@@ -591,7 +638,7 @@
         out_shape=[jax.ShapeDtypeStruct(maps.shape, full), jax.ShapeDtypeStruct(small.shape, full)]
         + [jax.ShapeDtypeStruct((4, f[0], 2 * f[1]), low) for f in finals]
         + landing,
-        in_specs=[anyspec] * 8 + [whole] * 6,
+        in_specs=[anyspec] * 10 + [whole] * 6,
         out_specs=[whole] * 2 + [anyspec] * 8,
         scratch_shapes=scratch,
         compiler_params=pltpu.CompilerParams(
@@ -651,16 +698,21 @@
     return jnp.concatenate([rows, swap(rows, "dev", 1)])
 
 
-def pair_gradient(rows, grads):
+def pair_halves(grads):
     side = place()[4]
     half = grads.shape[1] // 2
     low, high = grads[:, :half], grads[:, half:]
-    mine = jnp.where(side == 0, low, high)
     theirs = swap(jnp.where(side == 0, high, low), "dev", 1)
-    product = lax.dot_general(
-        rows, jnp.concatenate([mine, theirs]), (((0,), (0,)), ((), ())), preferred_element_type=jnp.float32
-    )
-    return product.astype(jnp.bfloat16).reshape(4, 2, 2, 2, rows.shape[1] // 32, half)
+    return jnp.concatenate([jnp.where(side == 0, low, high), theirs])
+
+
+def pair_product(rows, grads):
+    result = lax.dot_general(rows, grads, (((0,), (0,)), ((), ())), preferred_element_type=jnp.float32)
+    return result.astype(jnp.bfloat16).reshape(4, 2, 2, 2, rows.shape[1] // 32, grads.shape[1])
+
+
+def pair_gradient(rows, grads):
+    return pair_product(rows, pair_halves(grads))
 
 
 def across_half(share, axis):
@@ -718,7 +770,7 @@
     tuned = lax.axis_size("path") == 4 and lax.axis_size("dev") == 8
     weights = (w_expand, w_reduce, w_adapter, w_qkv, w_out, w_fc1, w_fc2)
     if tuned:
-        ordered, section_mixed, section_rows, spread_targets, expanded, activated_low, reduced, pooled = gather_weights(
+        ordered, section_mixed, section_rows, spread_targets, expanded, activated_low, reduced, features = gather_weights(
             [weights[i] for i in GATHER_ORDER],
             hires_maps[0],
             section_kernel,
@@ -760,19 +812,18 @@
         pooled = jnp.mean(
             section_out.reshape(grid_side, 2, grid_side, 2, channels), axis=(1, 3)
         ).reshape(tokens, channels)
-    pieces = pooled.astype(jnp.bfloat16).reshape(path_count, quarter_rows, channels)
-    spread_pieces = lax.all_to_all(pieces, "path", split_axis=0, concat_axis=0, tiled=True)
     if not tuned:
+        pieces = pooled.astype(jnp.bfloat16).reshape(path_count, quarter_rows, channels)
         own_target = jnp.broadcast_to(target_path, (path_count, 1))
+        spread_pieces = lax.all_to_all(pieces, "path", split_axis=0, concat_axis=0, tiled=True)
         spread_targets = lax.all_to_all(own_target, "path", split_axis=0, concat_axis=0, tiled=True)
     selector = (
         jnp.arange(path_count, dtype=jnp.int32)[:, None] == spread_targets.reshape(1, path_count)
     ).astype(jnp.float32)
-    routed = jnp.einsum("pq,qtc->ptc", selector, spread_pieces.astype(jnp.float32)).astype(
-        jnp.bfloat16
-    )
-    arrived = lax.all_to_all(routed, "path", split_axis=0, concat_axis=0, tiled=True)
-    features = arrived.reshape(tokens, channels)
+    if not tuned:
+        routed = jnp.einsum("pq,qtc->ptc", selector, spread_pieces.astype(jnp.float32)).astype(jnp.bfloat16)
+        arrived = lax.all_to_all(routed, "path", split_axis=0, concat_axis=0, tiled=True)
+        features = arrived.reshape(tokens, channels)
     adapted = jnp.dot(features, full_adapter, preferred_element_type=jnp.float32)
     spread_map, adapter_back = jax.vjp(
         adapter_depthwise, adapted.reshape(1, grid_side, grid_side, model_width), adapter_kernel
@@ -886,23 +937,30 @@
     grad_reduced = (grad_section_out * layer_scale).reshape(-1, channels).astype(jnp.bfloat16)
     if tuned:
         part_reduce = pair_gradient(both_images(activated_low), grad_reduced)
-        grad_reduced, part_reduce, half_fc2, half_fc1 = tie(grad_reduced, part_reduce, half_fc2, half_fc1)
         half_qkv, half_rest = across_half(part_qkv, 3), up_half(part_rest, 2)
         columns = part_reduce.shape[5] // 2
-        landed = [across_half(part_reduce[..., :columns], 3), up_half(part_reduce[..., columns:], 2)]
+        leaving = [
+            pick(part_reduce[first : first + 2, ..., :columns], 1 - place()[2], 3) for first in (0, 2)
+        ] + [pick(part_reduce[first : first + 2, ..., columns:], 1 - place()[1], 2) for first in (0, 2)]
+        grad_reduced, part_reduce, *leaving = tie(grad_reduced, part_reduce, *leaving)
+        landed = [swap(piece, "path", 1 + k // 2) for k, piece in enumerate(leaving)]
     else:
         grad_reduce_w = plain_sum(activated_low, grad_reduced)
     grad_activated = jnp.dot(grad_reduced, full_reduce.T, preferred_element_type=jnp.float32)
     grad_expanded = section_gelu_back(grad_activated)[0].astype(jnp.bfloat16)
     if tuned:
-        part_expand = pair_gradient(both_images(section_rows), grad_expanded)
+        grad_expanded, half_fc2, half_fc1 = tie(grad_expanded, half_fc2, half_fc1)
     else:
         grad_expand_w = plain_sum(section_rows, grad_expanded)
     grad_section_normed = jnp.dot(
         grad_expanded, full_expand.T, preferred_element_type=jnp.float32
     ).reshape(maps_float.shape)
     if tuned:
-        part_expand, half_qkv, half_rest = tie(part_expand, half_qkv, half_rest)
+        halves_expand = pair_halves(grad_expanded)
+        grad_section_normed, halves_expand, half_qkv, half_rest, landed[0], landed[2] = tie(
+            grad_section_normed, halves_expand, half_qkv, half_rest, landed[0], landed[2]
+        )
+        part_expand = pair_product(both_images(section_rows), halves_expand)
         step_fc2, step_fc1 = across_sum(part_fc2, 3, half_fc2), up_sum(part_fc1, 2, half_fc1)
         step_qkv, step_rest = across_sum(part_qkv, 3, half_qkv), up_sum(part_rest, 2, half_rest)
         small_rows = jnp.concatenate(

time: 896 us -> 847 us (0.945)
  waiting for transfers between devices: 56.6 us -> 17.5 us
  local copies, waits for them, and re-layouts: 74.2 us -> 58.4 us
  matrix products: 144 us -> 153 us
    ppermute x20 -> x22, waiting for transfers between devices: 44.2 us -> 16.9 us  [swap(): return lax.ppermute(value, axis, [(i, i ^ mask) for i in range(size)])]
    all_to_all x2 -> x0, waiting for transfers between devices: 11.5 us -> none  [the longest x1 6.67 us: local(): lax.all_to_all(pieces, 'path', split_axis=0, concat_axis=0, tiled=True)]
    dot_general x8 -> x7, matrix products: 59.4 us -> 58.7 us  [pair_product(): lax.dot_general(rows, grads, (((0,), (0,)), ((), ())), preferred_element_...]
  transfers between devices with their start and end apart: 24 -> 24, of which waited for: 6 -> 4; matrix products, arithmetic and copies ran while one was open for 26% -> 28% of each run, Pallas kernels for 0% -> 0%
where the time goes in v4:
time: 847 us; the launch traced here: 840 us
  Pallas kernels  530 us (63%)
  matrix products  153 us (18%)
  local copies, waits for them, and re-layouts  58.4 us (7%)
  other arithmetic  57.7 us (7%)
  starting transfers between devices  20 us (2%)
  waiting for transfers between devices  17.5 us (2%)
    pallas_call x1, Pallas kernels, gather_weights(): pl.pallas_call(functools.partial(gather_kernel, jobs, n, expand, reduce),...  268 us
    pallas_call x1, Pallas kernels, scatter_gradients(): pl.pallas_call(scatter_kernel, out_shape=[jax.ShapeDtypeStruct(maps.shape...  263 us
    dot_general x7, matrix products, pair_product(): lax.dot_general(rows, grads, (((0,), (0,)), ((), ())), preferred_element_...  58.7 us
    dot_general x1, matrix products, local(): jnp.dot(grad_reduced, full_reduce.T, preferred_element_type=jnp.float32)  24.5 us
    dot_general x1, matrix products, local(): jnp.dot(grad_expanded, full_expand.T, preferred_element_type=jnp.float32)  18.6 us
  transfers between devices with their start and end apart: 24, of which 4 were waited for; matrix products, arithmetic and copies ran while one was open for 28% of the time, Pallas kernels for 0%

profile of v4, /device:TPU:0, one launch (start us, length us, event | category | flops | bytes accessed | tf_op | source)
XLA Modules:
  0.0 840.0 jit_solution(7118125797001536257)
XLA Ops:
  4.5 267.8 %shard_map.305 = (bf16[1024,1024]{1,0:T(8,128)(2,1)}, bf16[1536,6144]{1,0:T(8,128)(2,1)}, bf16[6144,1536]{1,0:T(8,128)(2,1)}, bf16[1024,4096]{1,0:T(8,128)(2,1)}...) custom-call(bf16[128,1024]{1,0:T(8,128)(2,1)} %refs_0_.1, ...), custom_call_target="tpu_custom_call" | custom-call | tf_op jit(solution)/shard_map/pallas_call | solution.py:321
  276.9 4.0 convolution_convert_fusion.4
  291.2 7.3 multiply_convert_fusion.2
  298.5 8.0 fusion.28
  308.1 6.5 multiply_reduce_fusion.13
  334.6 5.9 fusion.51
  351.2 5.7 convolution_convert_fusion.3
  357.5 6.1 convolution_convert_fusion.1
  364.5 3.7 all-to-all-start
  377.8 3.8 all-to-all-start.1
  384.9 4.6 convolution_convert_fusion.2
  397.2 3.7 broadcast_in_dim.99
  401.0 4.0 multiply_reduce_fusion
  418.8 18.9 %fusion.12 = bf16[6144,768]{1,0:T(8,128)(2,1)} fusion(bf16[576,6144]{1,0:T(8,128)(2,1)} %collective-permute-done.10, bf16[576,6144]{1,0:T(8,128)(2,1)} %get-tuple-element.73, bf16[576,768]{1,0:T(8,128)(2,1)} %copy-done.57, bf16[576,768]{1,0:T(8,128)(2,1)} %get-tuple-element.139), kind=kOutput, calls=%fused_computation.15 | convolution fusion | flops 10908205056 | bytes 25362432 | tf_op jit(solution)/shard_map/dot_general | solution.py:710
  437.7 4.3 fusion.101
  445.4 24.5 %fusion.7 = bf16[576,6144]{1,0:T(8,128)(2,1)} fusion(f32[576,6144]{1,0:T(8,128)} %get-tuple-element.78, bf16[576,1536]{1,0:T(8,128)(2,1)S(1)} %get-tuple-element.76, bf16[6144,1536]{1,0:T(8,128)(2,1)} %get-tuple-element.77), kind=kOutput, calls=%fused_computation.9 | convolution fusion | flops 10942414848 | bytes 41877504 | tf_op jit(solution)/shard_map/dot_general | solution.py:949
  469.8 4.5 broadcast_select_fusion.1
  475.0 18.6 %fusion.109 = f32[576,1536]{1,0:T(8,128)} fusion(bf16[576,6144]{1,0:T(8,128)(2,1)} %fusion.7, bf16[1536,6144]{1,0:T(8,128)(2,1)} %get-tuple-element.82), kind=kOutput, calls=%fused_computation.234 | convolution fusion | flops 10871635968 | bytes 29491200 | tf_op jit(solution)/shard_map/dot_general | solution.py:955
  493.6 4.6 fusion.15.t1
  503.2 5.4 pad_maximum_fusion
  510.6 4.7 collective-permute-done.18.land0a
  515.3 12.0 %collective-permute-done.19.land0c = bf16[2,2,2,192,384]{4,3,2,1,0:T(8,128)(2,1)} collective-permute-done((bf16[2,2,2,192,384]{4,3,2,1,0:T(8,128)(2,1)}, bf16[2,2,2,192,384]{4,3,2,1,0:T(8,128)(2,1)}, u32[]{:S(2)}, u32[]{:S(2)}) %collective-permute-start.19) | collective-permute-done | bytes 1179680 | tf_op jit(solution)/shard_map/ppermute | solution.py:681
  527.3 18.5 %convolution_convert_fusion = bf16[1536,3072]{1,0:T(8,128)(2,1)} fusion(bf16[1152,3072]{1,0:T(8,128)(2,1)} %pad_maximum_fusion, bf16[576,1536]{1,0:T(8,128)(2,1)} %collective-permute-done.12, bf16[576,1536]{1,0:T(8,128)(2,1)} %get-tuple-element.75), kind=kOutput, calls=%fused_computation.14 | convolution fusion | flops 10883432448 | bytes 20054016 | tf_op jit(solution)/shard_map/dot_general | solution.py:710
  551.9 262.7 %shard_map.306 = (f32[24,24,1536]{2,1,0:T(8,128)}, f32[64,1536]{1,0:T(8,128)}, bf16[4,128,1024]{2,1,0:T(8,128)(2,1)}, bf16[4,32,4096]{2,1,0:T(8,128)(2,1)}, bf16...) custom-call(bf16[4,2,2,2,192,768]{5,4,3,2,1,0:T(8,128)(2,1)} %bitcas, ...), custom_call_target="tpu_custom_call" | custom-call | tf_op jit(solution)/shard_map/pallas_call | solution.py:636
  (272 shorter events, 127.7 us)
Async XLA Ops:
  272.3 101.0 %collective-permute-start.8 = (bf16[144,1536]{1,0:T(8,128)(2,1)}, bf16[144,1536]{1,0:T(8,128)(2,1)}, u32[]{:S(2)}, u32[]{:S(2)}) collective-permute-start(bf16[144,1536]{1,0:T(8,128)(2,1)} %get-tuple-element.62), channel_id=1, source_target_pairs={{0,1},{1,0},{2,3},{3,2},{4,5},{5,4},{6,7},{7,6},{8,9},{9,8},{10,11... | collective-permute-start | bytes 1327112 | tf_op jit(solution)/shard_map/ppermute | solution.py:681
  290.7 60.0 %collective-permute-start.2 = (bf16[144,1024]{1,0:T(8,128)(2,1)}, bf16[144,1024]{1,0:T(8,128)(2,1)}, u32[]{:S(2)}, u32[]{:S(2)}) collective-permute-start(bf16[144,1024]{1,0:T(8,128)(2,1)} %multiply_convert_fusion.3), channel_id=1, source_target_pairs={{0,1},{1,0},{2,3},{3,2},{4,5},{5,4},{6,7},{7,6},{8,9},{9,8},{10,11... | collective-permute-start | bytes 884744 | tf_op jit(solution)/shard_map/ppermute | solution.py:681
  298.4 58.9 %collective-permute-start = (bf16[144,4096]{1,0:T(8,128)(2,1)}, bf16[144,4096]{1,0:T(8,128)(2,1)}, u32[]{:S(2)}, u32[]{:S(2)}) collective-permute-start(bf16[144,4096]{1,0:T(8,128)(2,1)} %get-tuple-element.179), channel_id=1, source_target_pairs={{0,1},{1,0},{2,3},{3,2},{4,5},{5,4},{6,7},{7,6},{8,9},{9,8},{10,11... | collective-permute-start | bytes 3538952 | tf_op jit(solution)/shard_map/ppermute | solution.py:681
  307.6 43.5 %collective-permute-start.3 = (bf16[144,2048]{1,0:T(8,128)(2,1)}, bf16[144,2048]{1,0:T(8,128)(2,1)}, u32[]{:S(2)}, u32[]{:S(2)}) collective-permute-start(bf16[144,2048]{1,0:T(8,128)(2,1)} %get-tuple-element.142), channel_id=1, source_target_pairs={{0,1},{1,0},{2,3},{3,2},{4,5},{5,4},{6,7},{7,6},{8,9},{9,8},{10,11... | collective-permute-start | bytes 1769480 | tf_op jit(solution)/shard_map/ppermute | solution.py:681
  308.1 110.1 %collective-permute-start.10 = (bf16[576,6144]{1,0:T(8,128)(2,1)}, bf16[576,6144]{1,0:T(8,128)(2,1)}, u32[]{:S(2)}, u32[]{:S(2)}) collective-permute-start(bf16[576,6144]{1,0:T(8,128)(2,1)} %get-tuple-element.73), channel_id=1, source_target_pairs={{0,1},{1,0},{2,3},{3,2},{4,5},{5,4},{6,7},{7,6},{8,9},{9,8},{10,11... | collective-permute-start | bytes 21233672 | tf_op jit(solution)/shard_map/ppermute | solution.py:681
  350.7 19.3 %collective-permute-start.6 = (bf16[144,1024]{0,1:T(8,128)(2,1)}, bf16[144,1024]{0,1:T(8,128)(2,1)S(1)}, u32[]{:S(2)}, u32[]{:S(2)}) collective-permute-start(bf16[144,1024]{0,1:T(8,128)(2,1)} %bitcast.13), channel_id=1, source_target_pairs={{0,1},{1,0},{2,3},{3,2},{4,5},{5,4},{6,7},{7,6},{8,9},{9,8},{10,11... | collective-permute-start | bytes 884744 | tf_op jit(solution)/shard_map/ppermute | solution.py:681
  351.1 5.8 collective-permute-start.1
  356.9 16.2 %collective-permute-start.9 = (bf16[144,512]{1,0:T(8,128)(2,1)S(1)}, bf16[144,512]{1,0:T(8,128)(2,1)S(1)}, u32[]{:S(2)}, u32[]{:S(2)}) collective-permute-start(bf16[144,512]{1,0:T(8,128)(2,1)S(1)} %copy-done.48), channel_id=1, source_target_pairs={{0,1},{1,0},{2,3},{3,2},{4,5},{5,4},{6,7},{7,6},{8,9},{9,8},{10,11... | collective-permute-start | bytes 442376 | tf_op jit(solution)/shard_map/ppermute | solution.py:681
  357.3 12.4 %collective-permute-start.7 = (bf16[144,512]{1,0:T(8,128)(2,1)S(1)}, bf16[144,512]{1,0:T(8,128)(2,1)S(1)}, u32[]{:S(2)}, u32[]{:S(2)}) collective-permute-start(bf16[144,512]{1,0:T(8,128)(2,1)S(1)} %copy-done.49), channel_id=1, source_target_pairs={{0,1},{1,0},{2,3},{3,2},{4,5},{5,4},{6,7},{7,6},{8,9},{9,8},{10,11... | collective-permute-start | bytes 442376 | tf_op jit(solution)/shard_map/ppermute | solution.py:681
  364.5 12.0 %all-to-all-start = ((bf16[4,36,1536]{2,1,0:T(8,128)(2,1)}), bf16[4,36,1536]{2,1,0:T(8,128)(2,1)S(1)}, u32[]{:S(2)}, u32[]{:S(2)}) async-start(bf16[4,36,1536]{2,1,0:T(8,128)(2,1)} %reshape.467), calls=%async_computation | async-start | bytes 983040 | tf_op jit(solution)/shard_map/all_to_all | solution.py:922
  369.7 15.2 %collective-permute-start.4 = (bf16[144,1024]{1,0:T(8,128)(2,1)S(1)}, bf16[144,1024]{1,0:T(8,128)(2,1)}, u32[]{:S(2)}, u32[]{:S(2)}) collective-permute-start(bf16[144,1024]{1,0:T(8,128)(2,1)S(1)} %copy-done.27), channel_id=1, source_target_pairs={{0,1},{1,0},{2,3},{3,2},{4,5},{5,4},{6,7},{7,6},{8,9},{9,8},{10,11... | collective-permute-start | bytes 884744 | tf_op jit(solution)/shard_map/ppermute | solution.py:681
  370.0 14.9 %collective-permute-start.5 = (bf16[144,1536]{1,0:T(8,128)(2,1)S(1)}, bf16[144,1536]{1,0:T(8,128)(2,1)}, u32[]{:S(2)}, u32[]{:S(2)}) collective-permute-start(bf16[144,1536]{1,0:T(8,128)(2,1)S(1)} %copy-done.42), channel_id=1, source_target_pairs={{0,1},{1,0},{2,3},{3,2},{4,5},{5,4},{6,7},{7,6},{8,9},{9,8},{10,11... | collective-permute-start | bytes 1327112 | tf_op jit(solution)/shard_map/ppermute | solution.py:681
  373.1 154.2 %collective-permute-start.12 = (bf16[576,1536]{1,0:T(8,128)(2,1)}, bf16[576,1536]{1,0:T(8,128)(2,1)}, u32[]{:S(2)}, u32[]{:S(2)}) collective-permute-start(bf16[576,1536]{1,0:T(8,128)(2,1)} %get-tuple-element.75), channel_id=1, source_target_pairs={{0,1},{1,0},{2,3},{3,2},{4,5},{5,4},{6,7},{7,6},{8,9},{9,8},{10,11... | collective-permute-start | bytes 5308424 | tf_op jit(solution)/shard_map/ppermute | solution.py:681
  377.8 11.8 %all-to-all-start.1 = ((bf16[4,36,1536]{2,1,0:T(8,128)(2,1)}), bf16[4,36,1536]{2,1,0:T(8,128)(2,1)S(1)}, u32[]{:S(2)}, u32[]{:S(2)}) async-start(bf16[4,36,1536]{2,1,0:T(8,128)(2,1)} %copy.80), calls=%async_computation.1 | async-start | bytes 983040 | tf_op jit(solution)/shard_map/all_to_all | solution.py:926
  406.0 9.8 %collective-permute-start.11 = (bf16[576,768]{1,0:T(8,128)(2,1)S(1)}, bf16[576,768]{1,0:T(8,128)(2,1)S(1)}, u32[]{:S(2)}, u32[]{:S(2)}) collective-permute-start(bf16[576,768]{1,0:T(8,128)(2,1)S(1)} %get-tuple-element.140), channel_id=1, source_target_pairs={{0,1},{1,0},{2,3},{3,2},{4,5},{5,4},{6,7},{7,6},{8,9},{9,8},{10,11... | collective-permute-start | bytes 2654216 | tf_op jit(solution)/shard_map/ppermute | solution.py:681
  407.5 62.3 %collective-permute-start.13 = (bf16[4,2,2,128,512]{4,3,2,1,0:T(8,128)(2,1)}, bf16[4,2,2,128,512]{4,3,2,1,0:T(8,128)(2,1)}, u32[]{:S(2)}, u32[]{:S(2)}) collective-permute-start(bf16[4,2,2,128,512]{4,3,2,1,0:T(8,128)(2,1)} %dynamic-slice_bitcast_fusion.1), channel_id=1, source_target_pairs={{0,8},{8,0},{16,24},{24,16},{1,9},{9,1},{17,25},{25,17},{2,10},{10... | collective-permute-start | bytes 6291464 | tf_op jit(solution)/shard_map/ppermute | solution.py:681
  411.0 58.9 %collective-permute-start.14 = (bf16[4,2,2,32,2048]{4,3,2,1,0:T(8,128)(2,1)}, bf16[4,2,2,32,2048]{4,3,2,1,0:T(8,128)(2,1)}, u32[]{:S(2)}, u32[]{:S(2)}) collective-permute-start(bf16[4,2,2,32,2048]{4,3,2,1,0:T(8,128)(2,1)} %dynamic-slice_bitcast_fusion), channel_id=1, source_target_pairs={{0,16},{8,24},{16,0},{24,8},{1,17},{9,25},{17,1},{25,9},{2,18},{10... | collective-permute-start | bytes 6291464 | tf_op jit(solution)/shard_map/ppermute | solution.py:681
  416.7 93.3 %collective-permute-start.16 = (bf16[4,2,2,32,1536]{4,3,2,1,0:T(8,128)(2,1)}, bf16[4,2,2,32,1536]{4,3,2,1,0:T(8,128)(2,1)}, u32[]{:S(2)}, u32[]{:S(2)}) collective-permute-start(bf16[4,2,2,32,1536]{4,3,2,1,0:T(8,128)(2,1)} %dynamic-slice_bitcast_fusion.2), channel_id=1, source_target_pairs={{0,8},{8,0},{16,24},{24,16},{1,9},{9,1},{17,25},{25,17},{2,10},{10... | collective-permute-start | bytes 4718600 | tf_op jit(solution)/shard_map/ppermute | solution.py:681
  418.2 90.4 %collective-permute-start.17 = (bf16[4,2,2,80,512]{4,3,2,1,0:T(8,128)(2,1)}, bf16[4,2,2,80,512]{4,3,2,1,0:T(8,128)(2,1)}, u32[]{:S(2)}, u32[]{:S(2)}) collective-permute-start(bf16[4,2,2,80,512]{4,3,2,1,0:T(8,128)(2,1)} %dynamic-slice_bitcast_fusion.3), channel_id=1, source_target_pairs={{0,16},{8,24},{16,0},{24,8},{1,17},{9,25},{17,1},{25,9},{2,18},{10... | collective-permute-start | bytes 3932168 | tf_op jit(solution)/shard_map/ppermute | solution.py:681
  474.4 23.9 %collective-permute-start.15 = (bf16[576,3072]{1,0:T(8,128)(2,1)}, bf16[576,3072]{1,0:T(8,128)(2,1)}, u32[]{:S(2)}, u32[]{:S(2)}) collective-permute-start(bf16[576,3072]{1,0:T(8,128)(2,1)} %get-tuple-element.136), channel_id=1, source_target_pairs={{0,1},{1,0},{2,3},{3,2},{4,5},{5,4},{6,7},{7,6},{8,9},{9,8},{10,11... | collective-permute-start | bytes 10616840 | tf_op jit(solution)/shard_map/ppermute | solution.py:681
  474.4 40.9 %collective-permute-start.18 = (bf16[2,2,2,192,384]{4,3,2,1,0:T(8,128)(2,1)}, bf16[2,2,2,192,384]{4,3,2,1,0:T(8,128)(2,1)}, u32[]{:S(2)}, u32[]{:S(2)}) collective-permute-start(bf16[2,2,2,192,384]{4,3,2,1,0:T(8,128)(2,1)} %get-tuple-element.85), channel_id=1, source_target_pairs={{0,8},{8,0},{16,24},{24,16},{1,9},{9,1},{17,25},{25,17},{2,10},{10... | collective-permute-start | bytes 3538952 | tf_op jit(solution)/shard_map/ppermute | solution.py:681
  498.2 29.1 %collective-permute-start.19 = (bf16[2,2,2,192,384]{4,3,2,1,0:T(8,128)(2,1)}, bf16[2,2,2,192,384]{4,3,2,1,0:T(8,128)(2,1)}, u32[]{:S(2)}, u32[]{:S(2)}) collective-permute-start(bf16[2,2,2,192,384]{4,3,2,1,0:T(8,128)(2,1)} %get-tuple-element.86), channel_id=1, source_target_pairs={{0,16},{8,24},{16,0},{24,8},{1,17},{9,25},{17,1},{25,9},{2,18},{10... | collective-permute-start | bytes 3538952 | tf_op jit(solution)/shard_map/ppermute | solution.py:681
  508.6 43.1 %collective-permute-start.20 = (bf16[2,2,2,192,384]{4,3,2,1,0:T(8,128)(2,1)}, bf16[2,2,2,192,384]{4,3,2,1,0:T(8,128)(2,1)}, u32[]{:S(2)}, u32[]{:S(2)}) collective-permute-start(bf16[2,2,2,192,384]{4,3,2,1,0:T(8,128)(2,1)} %get-tuple-element.89), channel_id=1, source_target_pairs={{0,8},{8,0},{16,24},{24,16},{1,9},{9,1},{17,25},{25,17},{2,10},{10... | collective-permute-start | bytes 3538952 | tf_op jit(solution)/shard_map/ppermute | solution.py:681
  510.0 41.9 %collective-permute-start.21 = (bf16[2,2,2,192,384]{4,3,2,1,0:T(8,128)(2,1)}, bf16[2,2,2,192,384]{4,3,2,1,0:T(8,128)(2,1)}, u32[]{:S(2)}, u32[]{:S(2)}) collective-permute-start(bf16[2,2,2,192,384]{4,3,2,1,0:T(8,128)(2,1)} %get-tuple-element.91), channel_id=1, source_target_pairs={{0,16},{8,24},{16,0},{24,8},{1,17},{9,25},{17,1},{25,9},{2,18},{10... | collective-permute-start | bytes 3538952 | tf_op jit(solution)/shard_map/ppermute | solution.py:681
  (61 other events, 242.9 us)

commit v5 on v4

--- a/solution.py
+++ b/solution.py
@@ -445,12 +445,21 @@
             sent.append(send(acc[k].at[:, :, 1 - index], two[k], mask))
         return sent
 
+    def columns_of(n, parts, k):
+        half = zrs[n].shape[3] // len(parts)
+        return pl.ds(k * half, half)
+
     def heights(n, parts, k):
-        zr = zrs[n]
-        half = zr.shape[3] // len(parts)
-        return [
-            send(parts[k].at[height ^ m], zr.at[m - 1, :, :, pl.ds(k * half, half)], (0, 2 * m)) for m in (1, 2, 3)
-        ]
+        cols = columns_of(n, parts, k)
+        return [send(parts[k].at[height ^ m], zrs[n].at[m // 2, :, :, cols], (0, 2)) for m in (1, 3)]
+
+    def further(n, parts, k, sent):
+        for copy in sent:
+            copy.wait_recv()
+        cols = columns_of(n, parts, k)
+        for c in range(2):
+            zrs[n][1, c, :, cols] = add_block(zrs[n][1, c, :, cols], parts[k][height ^ 2, c])
+        return send(zrs[n].at[1, :, :, cols], zrs[n].at[2, :, :, cols], (0, 4))
 
     def thin_three(i, started):
         _, own, two, _ = thin[i]
@@ -472,34 +481,39 @@
         return heights(4 + w, two, 0)
 
     def total(n, parts, k, sent):
-        for copy in sent:
-            copy.wait_recv()
+        sent.wait_recv()
         zr, low, whole = zrs[n], lows[n], wholes[n]
         size = zr.shape[3]
         half = size // len(parts)
         cols = slice(k * half, (k + 1) * half)
         for c in range(2):
             value = parts[k][height, c].astype(jnp.float32)
-            for m in range(3):
+            for m in (0, 2):
                 value = value + zr[m, c, :, cols].astype(jnp.float32)
             low[c, :, cols] = value.astype(jnp.bfloat16)
         place = (slice(None), pl.ds(pl.multiple_of(side * size + k * half, LANES), half))
         whole[place] = low[side, :, cols]
         return send(low.at[1 - side, :, cols], whole.at[place], (0, 1))
 
-    def spread(n, swapped):
-        swapped.wait_recv()
-        return [fetch(wholes[n], outs[n].at[p])] + [send(wholes[n], outs[n].at[p], (m, 0)) for m in (1, 2, 3)]
-
-    def spread_part(n, k, swapped):
+    def spread(n, swapped, first=0, parts=1):
         swapped.wait_recv()
         size = zrs[n].shape[3]
-        copies = []
+        group = []
         for c in range(2):
-            cols = pl.ds(c * size + k * (size // 2), size // 2)
+            cols = pl.ds(c * size + first * (size // parts), size // parts)
             src, dst = wholes[n].at[:, cols], outs[n].at[p, :, cols]
-            copies += [fetch(src, dst)] + [send(src, dst, (m, 0)) for m in (1, 2, 3)]
-        return copies
+            group.append((n, cols, fetch(src, dst), send(src, dst, (1, 0)), send(src, dst, (2, 0))))
+        return group
+
+    def relay(group):
+        sent = []
+        for n, cols, _, along_x, along_y in group:
+            half = cols.size // 2
+            for k, (copy, other, mask) in enumerate(((along_x, 1, (2, 0)), (along_y, 2, (1, 0)))):
+                copy.wait_recv()
+                ref = outs[n].at[p ^ other, :, pl.ds(cols.start + k * half, half)]
+                sent.append(send(ref, ref, mask))
+        return sent
 
     side_cells, _, channels = maps.shape
     count = channels // LANES
@@ -557,19 +571,26 @@
 
         lax.fori_loop(first, last, one, 0)
 
-    small_masks = [(0, 1), (1, 0), (2, 0), (0, 2), (0, 4)]
-
-    def small_send(s):
-        return send(small_at.at[s], small_from.at[s], small_masks[s])
+    small_masks = [(0, 1), (1, 0), (2, 0), (0, 2), (0, 4), (0, 1)]
+    small_half = small_in.shape[0] // 2
+    small_rows = pl.ds(pl.multiple_of(side * small_half, 8), small_half)
+    small_rest = pl.ds(pl.multiple_of((1 - side) * small_half, 8), small_half)
+
+    def small_send(s, rows):
+        return send(small_at.at[s, rows], small_from.at[s, rows], small_masks[s])
 
     def small_step(s, copy):
         copy.wait_recv()
-        value = small_at[s] + small_from[s]
-        if s + 1 < len(small_masks):
-            small_at[s + 1] = value
-            return small_send(s + 1)
-        small_out[...] = value
-
+        small_at[s + 1, small_rows] = small_at[s, small_rows] + small_from[s, small_rows]
+        return small_send(s + 1, small_rows)
+
+    def small_end(copy):
+        copy.wait_recv()
+        small_out[small_rows] = small_at[5, small_rows]
+        small_out[small_rest] = small_from[5, small_rest]
+
+    thin_parts = [[group[2]] for group in thin]
+    parts_reduce, parts_expand = wide[0][3], wide[1][3]
     thin_sent = [thin_two(i) for i in range(4)]
     one_reduce = wide_one(0, False)
     norm_back()
@@ -579,35 +600,41 @@
     thin_high = [thin_three(i, thin_sent[i]) for i in range(4)]
     one_expand = wide_one(1, True)
     blocks(count // 3, count // 2)
-    high_reduce = wide_three(0, two_reduce)
-    high_reduce += heights(4, wide[0][3], 1)
+    high_reduce = [wide_three(0, two_reduce), heights(4, parts_reduce, 1)]
+    thin_high = [further(i, thin_parts[i], 0, thin_high[i]) for i in range(4)]
     blocks(count // 2, count)
-    small = small_send(0)
+    small = small_send(0, small_rest)
+    small = small_step(0, small)
+    high_reduce = [further(4, parts_reduce, k, high_reduce[k]) for k in range(2)]
+    small = small_step(1, small)
     two_expand = wide_two(1, one_expand)
-    small = small_step(0, small)
-    swaps = [total(i, [thin[i][2]], 0, thin_high[i]) for i in range(4)]
-    small = small_step(1, small)
-    high_expand = wide_three(1, two_expand)
-    last = [spread(i, swaps[i]) for i in range(4)]
+    swaps = [total(i, thin_parts[i], 0, thin_high[i]) for i in range(4)]
     small = small_step(2, small)
-    for copy in high_reduce:
-        copy.wait_recv()
-    swap_reduce = [total(4, wide[0][3], k, []) for k in range(2)]
+    small = small_step(3, small)
+    high_low = wide_three(1, two_expand)
+    thin_out = [spread(i, swaps[i]) for i in range(4)]
+    small = small_step(4, small)
+    swap_reduce = [total(4, parts_reduce, k, high_reduce[k]) for k in range(2)]
+    high_low = further(5, parts_expand, 0, high_low)
+    high_high = heights(5, parts_expand, 1)
+    small_end(small)
     swap_reduce[0].wait_recv()
-    last.append(spread(4, swap_reduce[1]))
-    small = small_step(3, small)
-    swap_low = total(5, wide[1][3], 0, high_expand)
-    high_expand = heights(5, wide[1][3], 1)
-    last.append(spread_part(5, 0, swap_low))
-    small = small_step(4, small)
-    swap_high = total(5, wide[1][3], 1, high_expand)
-    last.append(spread_part(5, 1, swap_high))
+    reduce_out = spread(4, swap_reduce[1])
+    last = [relay(group) for group in thin_out]
+    swap_low = total(5, parts_expand, 0, high_low)
+    high_high = further(5, parts_expand, 1, high_high)
+    low_out = spread(5, swap_low, 0, 2)
+    last.append(relay(reduce_out))
+    swap_high = total(5, parts_expand, 1, high_high)
+    high_out = spread(5, swap_high, 1, 2)
+    last.append(relay(low_out))
+    last.append(relay(high_out))
+    for group in thin_out + [reduce_out, low_out, high_out]:
+        for entry in group:
+            entry[2].wait()
     for group in last:
-        for k, copy in enumerate(group):
-            if k % 4:
-                copy.wait_recv()
-            else:
-                copy.wait()
+        for copy in group:
+            copy.wait_recv()
     for copy in copies:
         copy.wait_send()
 
@@ -630,9 +657,9 @@
     scratch += [VMEM((2,) + f, low) for f in finals]
     scratch += [VMEM((f[0], 2 * f[1]), low) for f in finals]
     edge = (side + 2 * REACH, side + 2 * EDGE, LANES)
-    scratch += [VMEM((5,) + small.shape, full)] * 2
+    scratch += [VMEM((6,) + small.shape, full)] * 2
     scratch += [VMEM(edge, full)] * 2 + [VMEM((SIDE * SIDE, 8, LANES), full)]
-    scratch += [dma((80,)), dma((80,)), dma((40,))]
+    scratch += [dma((120,)), dma((120,)), dma((48,))]
     results = pl.pallas_call(
         scatter_kernel,
         out_shape=[jax.ShapeDtypeStruct(maps.shape, full), jax.ShapeDtypeStruct(small.shape, full)]
@@ -916,8 +943,6 @@
     else:
         grad_adapter_w = plain_sum(features, grad_adapted_low)
     grad_features = jnp.dot(grad_adapted_low, full_adapter.T, preferred_element_type=jnp.float32)
-    if tuned:
-        grad_features, part_fc2, part_fc1 = tie(grad_features, part_fc2, part_fc1)
     grad_pieces = grad_features.astype(jnp.bfloat16).reshape(path_count, quarter_rows, channels)
     grad_routed = lax.all_to_all(grad_pieces, "path", split_axis=0, concat_axis=0, tiled=True)
     grad_unrouted = jnp.einsum("pq,ptc->qtc", selector, grad_routed.astype(jnp.float32)).astype(
@@ -926,8 +951,12 @@
     grad_home = lax.all_to_all(grad_unrouted, "path", split_axis=0, concat_axis=0, tiled=True)
     if tuned:
         part_rest = jnp.concatenate([part_out, part_adapter], axis=4)
-        grad_home, part_fc2, part_fc1, part_qkv, part_rest = tie(grad_home, part_fc2, part_fc1, part_qkv, part_rest)
-        half_fc2, half_fc1 = across_half(part_fc2, 3), up_half(part_fc1, 2)
+        _, up, across, _, _ = place()
+        going = [pick(part_fc2, 1 - across, 3), pick(part_fc1, 1 - up, 2), pick(part_qkv, 1 - across, 3), pick(part_rest, 1 - up, 2)]
+        grad_home, part_fc2, part_fc1, part_qkv, part_rest, *going = tie(
+            grad_home, part_fc2, part_fc1, part_qkv, part_rest, *going
+        )
+        half_fc2, half_fc1, half_qkv, half_rest = [swap(piece, "path", 1 + k % 2) for k, piece in enumerate(going)]
     grad_pooled = grad_home.astype(jnp.float32).reshape(tokens, channels)
     quarter = (grad_pooled * 0.25).reshape(1, grid_side, 1, grid_side, 1, channels)
     grad_section_out = jnp.broadcast_to(quarter, (1, grid_side, 2, grid_side, 2, channels)).reshape(
@@ -937,7 +966,6 @@
     grad_reduced = (grad_section_out * layer_scale).reshape(-1, channels).astype(jnp.bfloat16)
     if tuned:
         part_reduce = pair_gradient(both_images(activated_low), grad_reduced)
-        half_qkv, half_rest = across_half(part_qkv, 3), up_half(part_rest, 2)
         columns = part_reduce.shape[5] // 2
         leaving = [
             pick(part_reduce[first : first + 2, ..., :columns], 1 - place()[2], 3) for first in (0, 2)
@@ -971,7 +999,7 @@
             ]
         )
         small_count = small_rows.shape[0]
-        small_rows = jnp.pad(small_rows, ((0, -small_count % 8), (0, 0)))
+        small_rows = jnp.pad(small_rows, ((0, -small_count % 16), (0, 0)))
         grad_maps, small_rows, pieces = scatter_gradients(
             part_reduce,
             part_expand,

time: 847 us -> 804 us (0.949)
  Pallas kernels: 530 us -> 493 us
  matrix products: 153 us -> 139 us
    pallas_call x1, Pallas kernels: 263 us -> 225 us  [scatter_gradients(): pl.pallas_call(scatter_kernel, out_shape=[jax.ShapeDtypeStruct(maps.shape...]
  transfers between devices with their start and end apart: 24 -> 24, of which waited for: 4 -> 2; matrix products, arithmetic and copies ran while one was open for 28% -> 26% of each run, Pallas kernels for 0% -> 0%
where the time goes in v5:
time: 804 us; the launch traced here: 798 us
  Pallas kernels  493 us (61%)
  matrix products  139 us (17%)
  local copies, waits for them, and re-layouts  66.6 us (8%)
  other arithmetic  57.4 us (7%)
  waiting for transfers between devices  19.6 us (2%)
  starting transfers between devices  19.5 us (2%)
    pallas_call x1, Pallas kernels, gather_weights(): pl.pallas_call(functools.partial(gather_kernel, jobs, n, expand, reduce),...  268 us
    pallas_call x1, Pallas kernels, scatter_gradients(): pl.pallas_call(scatter_kernel, out_shape=[jax.ShapeDtypeStruct(maps.shape...  225 us
    dot_general x7, matrix products, pair_product(): lax.dot_general(rows, grads, (((0,), (0,)), ((), ())), preferred_element_...  50.7 us
    dot_general x1, matrix products, local(): jnp.dot(grad_reduced, full_reduce.T, preferred_element_type=jnp.float32)  24.5 us
    ppermute x22, waiting for transfers between devices, swap(): return lax.ppermute(value, axis, [(i, i ^ mask) for i in range(size)])  19.6 us
    dot_general x1, matrix products, local(): jnp.dot(grad_expanded, full_expand.T, preferred_element_type=jnp.float32)  18.6 us
  transfers between devices with their start and end apart: 24, of which 2 were waited for; matrix products, arithmetic and copies ran while one was open for 26% of the time, Pallas kernels for 0%

profile of v5, /device:TPU:0, one launch (start us, length us, event | category | flops | bytes accessed | tf_op | source)
XLA Modules:
  0.0 797.8 jit_solution(5627014411640378818)
XLA Ops:
  4.5 267.8 %shard_map.305 = (bf16[1024,1024]{1,0:T(8,128)(2,1)}, bf16[1536,6144]{1,0:T(8,128)(2,1)}, bf16[6144,1536]{1,0:T(8,128)(2,1)}, bf16[1024,4096]{1,0:T(8,128)(2,1)}...) custom-call(bf16[128,1024]{1,0:T(8,128)(2,1)} %refs_0_.1, ...), custom_call_target="tpu_custom_call" | custom-call | tf_op jit(solution)/shard_map/pallas_call | solution.py:321
  278.4 4.0 convolution_convert_fusion.4
  286.4 3.4 fusion.105
  296.3 6.7 multiply_convert_fusion.2
  303.0 3.9 fusion.28
  334.9 3.9 all-to-all-start
  352.7 4.2 all-to-all-start.1
  368.5 3.4 convolution_convert_fusion.3
  385.3 4.0 broadcast_in_dim.87
  389.4 3.9 multiply_reduce_fusion
  396.2 5.5 fusion.51
  401.8 3.7 broadcast_in_dim.99
  411.2 18.5 %fusion.12 = bf16[6144,768]{1,0:T(8,128)(2,1)} fusion(bf16[576,6144]{1,0:T(8,128)(2,1)} %collective-permute-done.10, bf16[576,6144]{1,0:T(8,128)(2,1)} %get-tuple-element.71, bf16[576,768]{1,0:T(8,128)(2,1)} %collective-permute-done.11, bf16[576,768]{1,0:T(8,128)(2,1)} %get-tuple-element.141), kind=kOutput, calls=%fused_computation.15 | convolution fusion | flops 10908205056 | bytes 25362432 | tf_op jit(solution)/shard_map/dot_general | solution.py:737
  429.7 4.3 fusion.101
  438.0 24.5 %fusion.7 = bf16[576,6144]{1,0:T(8,128)(2,1)} fusion(f32[576,6144]{1,0:T(8,128)} %get-tuple-element.76, bf16[576,1536]{1,0:T(8,128)(2,1)S(1)} %copy-done.6, bf16[6144,1536]{1,0:T(8,128)(2,1)} %get-tuple-element.75), kind=kOutput, calls=%fused_computation.9 | convolution fusion | flops 10942414848 | bytes 41877504 | tf_op jit(solution)/shard_map/dot_general | solution.py:977
  462.5 4.5 broadcast_select_fusion.1
  469.0 18.6 %fusion.108 = f32[576,1536]{1,0:T(8,128)} fusion(bf16[576,6144]{1,0:T(8,128)(2,1)} %fusion.7, bf16[1536,6144]{1,0:T(8,128)(2,1)} %get-tuple-element.80), kind=kOutput, calls=%fused_computation.234 | convolution fusion | flops 10871635968 | bytes 29491200 | tf_op jit(solution)/shard_map/dot_general | solution.py:983
  487.6 4.6 fusion.15.t1
  495.7 5.5 pad_maximum_fusion
  501.8 11.4 %collective-permute-done.18.land0a = bf16[2,2,2,192,384]{4,3,2,1,0:T(8,128)(2,1)} collective-permute-done((bf16[2,2,2,192,384]{4,3,2,1,0:T(8,128)(2,1)}, bf16[2,2,2,192,384]{4,3,2,1,0:T(8,128)(2,1)}, u32[]{:S(2)}, u32[]{:S(2)}) %collective-permute-start.18) | collective-permute-done | bytes 1179680 | tf_op jit(solution)/shard_map/ppermute | solution.py:708
  513.2 8.1 %collective-permute-done.19.land0c = bf16[2,2,2,192,384]{4,3,2,1,0:T(8,128)(2,1)} collective-permute-done((bf16[2,2,2,192,384]{4,3,2,1,0:T(8,128)(2,1)}, bf16[2,2,2,192,384]{4,3,2,1,0:T(8,128)(2,1)}, u32[]{:S(2)}, u32[]{:S(2)}) %collective-permute-start.19) | collective-permute-done | bytes 1179680 | tf_op jit(solution)/shard_map/ppermute | solution.py:708
  521.3 18.6 %convolution_convert_fusion = bf16[1536,3072]{1,0:T(8,128)(2,1)} fusion(bf16[1152,3072]{1,0:T(8,128)(2,1)} %pad_maximum_fusion, bf16[576,1536]{1,0:T(8,128)(2,1)} %collective-permute-done.12, bf16[576,1536]{1,0:T(8,128)(2,1)} %get-tuple-element.73), kind=kOutput, calls=%fused_computation.14 | convolution fusion | flops 10883432448 | bytes 20054016 | tf_op jit(solution)/shard_map/dot_general | solution.py:737
  547.2 225.1 %shard_map.306 = (f32[24,24,1536]{2,1,0:T(8,128)}, f32[64,1536]{1,0:T(8,128)}, bf16[4,128,1024]{2,1,0:T(8,128)(2,1)}, bf16[4,32,4096]{2,1,0:T(8,128)(2,1)}, bf16...) custom-call(bf16[4,2,2,2,192,768]{5,4,3,2,1,0:T(8,128)(2,1)} %bitcas, ...), custom_call_target="tpu_custom_call" | custom-call | tf_op jit(solution)/shard_map/pallas_call | solution.py:663
  790.1 3.2 bitcast_convert_fusion
  (280 shorter events, 133.8 us)
Async XLA Ops:
  292.9 56.0 %collective-permute-start.6 = (bf16[144,1024]{0,1:T(8,128)(2,1)}, bf16[144,1024]{0,1:T(8,128)(2,1)}, u32[]{:S(2)}, u32[]{:S(2)}) collective-permute-start(bf16[144,1024]{0,1:T(8,128)(2,1)} %bitcast.13), channel_id=1, source_target_pairs={{0,1},{1,0},{2,3},{3,2},{4,5},{5,4},{6,7},{7,6},{8,9},{9,8},{10,11... | collective-permute-start | bytes 884744 | tf_op jit(solution)/shard_map/ppermute | solution.py:708
  295.7 72.7 %collective-permute-start.2 = (bf16[144,1024]{1,0:T(8,128)(2,1)}, bf16[144,1024]{1,0:T(8,128)(2,1)}, u32[]{:S(2)}, u32[]{:S(2)}) collective-permute-start(bf16[144,1024]{1,0:T(8,128)(2,1)} %multiply_convert_fusion.3), channel_id=1, source_target_pairs={{0,1},{1,0},{2,3},{3,2},{4,5},{5,4},{6,7},{7,6},{8,9},{9,8},{10,11... | collective-permute-start | bytes 884744 | tf_op jit(solution)/shard_map/ppermute | solution.py:708
  296.3 114.9 %collective-permute-start.10 = (bf16[576,6144]{1,0:T(8,128)(2,1)}, bf16[576,6144]{1,0:T(8,128)(2,1)}, u32[]{:S(2)}, u32[]{:S(2)}) collective-permute-start(bf16[576,6144]{1,0:T(8,128)(2,1)} %get-tuple-element.71), channel_id=1, source_target_pairs={{0,1},{1,0},{2,3},{3,2},{4,5},{5,4},{6,7},{7,6},{8,9},{9,8},{10,11... | collective-permute-start | bytes 21233672 | tf_op jit(solution)/shard_map/ppermute | solution.py:708
  334.9 16.5 %all-to-all-start = ((bf16[4,36,1536]{2,1,0:T(8,128)(2,1)}), bf16[4,36,1536]{2,1,0:T(8,128)(2,1)S(1)}, u32[]{:S(2)}, u32[]{:S(2)}) async-start(bf16[4,36,1536]{2,1,0:T(8,128)(2,1)} %reshape.465), calls=%async_computation | async-start | bytes 983040 | tf_op jit(solution)/shard_map/all_to_all | solution.py:947
  342.7 14.3 %collective-permute-start.5 = (bf16[144,1536]{1,0:T(8,128)(2,1)}, bf16[144,1536]{1,0:T(8,128)(2,1)}, u32[]{:S(2)}, u32[]{:S(2)}) collective-permute-start(bf16[144,1536]{1,0:T(8,128)(2,1)} %get-tuple-element.146), channel_id=1, source_target_pairs={{0,1},{1,0},{2,3},{3,2},{4,5},{5,4},{6,7},{7,6},{8,9},{9,8},{10,11... | collective-permute-start | bytes 1327112 | tf_op jit(solution)/shard_map/ppermute | solution.py:708
  343.6 5.0 collective-permute-start.7
  348.6 8.3 %collective-permute-start.4 = (bf16[144,1024]{1,0:T(8,128)(2,1)S(1)}, bf16[144,1024]{1,0:T(8,128)(2,1)}, u32[]{:S(2)}, u32[]{:S(2)}) collective-permute-start(bf16[144,1024]{1,0:T(8,128)(2,1)S(1)} %copy-done.27), channel_id=1, source_target_pairs={{0,1},{1,0},{2,3},{3,2},{4,5},{5,4},{6,7},{7,6},{8,9},{9,8},{10,11... | collective-permute-start | bytes 884744 | tf_op jit(solution)/shard_map/ppermute | solution.py:708
  348.9 11.9 %collective-permute-start.8 = (bf16[144,1536]{1,0:T(8,128)(2,1)}, bf16[144,1536]{1,0:T(8,128)(2,1)}, u32[]{:S(2)}, u32[]{:S(2)}) collective-permute-start(bf16[144,1536]{1,0:T(8,128)(2,1)} %get-tuple-element.63), channel_id=1, source_target_pairs={{0,1},{1,0},{2,3},{3,2},{4,5},{5,4},{6,7},{7,6},{8,9},{9,8},{10,11... | collective-permute-start | bytes 1327112 | tf_op jit(solution)/shard_map/ppermute | solution.py:708
  352.7 28.6 %all-to-all-start.1 = ((bf16[4,36,1536]{2,1,0:T(8,128)(2,1)}), bf16[4,36,1536]{2,1,0:T(8,128)(2,1)S(1)}, u32[]{:S(2)}, u32[]{:S(2)}) async-start(bf16[4,36,1536]{2,1,0:T(8,128)(2,1)} %copy.80), calls=%async_computation.1 | async-start | bytes 983040 | tf_op jit(solution)/shard_map/all_to_all | solution.py:951
  356.9 18.5 %collective-permute-start = (bf16[144,4096]{1,0:T(8,128)(2,1)S(1)}, bf16[144,4096]{1,0:T(8,128)(2,1)S(1)}, u32[]{:S(2)}, u32[]{:S(2)}) collective-permute-start(bf16[144,4096]{1,0:T(8,128)(2,1)S(1)} %copy-done.13), channel_id=1, source_target_pairs={{0,1},{1,0},{2,3},{3,2},{4,5},{5,4},{6,7},{7,6},{8,9},{9,8},{10,11... | collective-permute-start | bytes 3538952 | tf_op jit(solution)/shard_map/ppermute | solution.py:708
  357.0 3.7 collective-permute-start.9
  360.6 14.8 %collective-permute-start.1 = (bf16[144,512]{1,0:T(8,128)(2,1)S(1)}, bf16[144,512]{1,0:T(8,128)(2,1)S(1)}, u32[]{:S(2)}, u32[]{:S(2)}) collective-permute-start(bf16[144,512]{1,0:T(8,128)(2,1)S(1)} %copy-done.47), channel_id=1, source_target_pairs={{0,1},{1,0},{2,3},{3,2},{4,5},{5,4},{6,7},{7,6},{8,9},{9,8},{10,11... | collective-permute-start | bytes 442376 | tf_op jit(solution)/shard_map/ppermute | solution.py:708
  360.8 7.7 collective-permute-start.3
  368.4 152.9 %collective-permute-start.12 = (bf16[576,1536]{1,0:T(8,128)(2,1)}, bf16[576,1536]{1,0:T(8,128)(2,1)}, u32[]{:S(2)}, u32[]{:S(2)}) collective-permute-start(bf16[576,1536]{1,0:T(8,128)(2,1)} %get-tuple-element.73), channel_id=1, source_target_pairs={{0,1},{1,0},{2,3},{3,2},{4,5},{5,4},{6,7},{7,6},{8,9},{9,8},{10,11... | collective-permute-start | bytes 5308424 | tf_op jit(solution)/shard_map/ppermute | solution.py:708
  395.8 14.8 %collective-permute-start.11 = (bf16[576,768]{1,0:T(8,128)(2,1)}, bf16[576,768]{1,0:T(8,128)(2,1)}, u32[]{:S(2)}, u32[]{:S(2)}) collective-permute-start(bf16[576,768]{1,0:T(8,128)(2,1)} %get-tuple-element.142), channel_id=1, source_target_pairs={{0,1},{1,0},{2,3},{3,2},{4,5},{5,4},{6,7},{7,6},{8,9},{9,8},{10,11... | collective-permute-start | bytes 2654216 | tf_op jit(solution)/shard_map/ppermute | solution.py:708
  405.5 57.0 %collective-permute-start.13 = (bf16[4,2,2,128,512]{4,3,2,1,0:T(8,128)(2,1)}, bf16[4,2,2,128,512]{4,3,2,1,0:T(8,128)(2,1)S(1)}, u32[]{:S(2)}, u32[]{:S(2)}) collective-permute-start(bf16[4,2,2,128,512]{4,3,2,1,0:T(8,128)(2,1)} %dynamic-slice_bitcast_fusion.1), channel_id=1, source_target_pairs={{0,8},{8,0},{16,24},{24,16},{1,9},{9,1},{17,25},{25,17},{2,10},{10... | collective-permute-start | bytes 6291464 | tf_op jit(solution)/shard_map/ppermute | solution.py:708
  407.4 55.1 %collective-permute-start.14 = (bf16[4,2,2,32,2048]{4,3,2,1,0:T(8,128)(2,1)}, bf16[4,2,2,32,2048]{4,3,2,1,0:T(8,128)(2,1)}, u32[]{:S(2)}, u32[]{:S(2)}) collective-permute-start(bf16[4,2,2,32,2048]{4,3,2,1,0:T(8,128)(2,1)} %dynamic-slice_bitcast_fusion), channel_id=1, source_target_pairs={{0,16},{8,24},{16,0},{24,8},{1,17},{9,25},{17,1},{25,9},{2,18},{10... | collective-permute-start | bytes 6291464 | tf_op jit(solution)/shard_map/ppermute | solution.py:708
  410.6 91.1 %collective-permute-start.16 = (bf16[4,2,2,32,1536]{4,3,2,1,0:T(8,128)(2,1)}, bf16[4,2,2,32,1536]{4,3,2,1,0:T(8,128)(2,1)}, u32[]{:S(2)}, u32[]{:S(2)}) collective-permute-start(bf16[4,2,2,32,1536]{4,3,2,1,0:T(8,128)(2,1)} %dynamic-slice_bitcast_fusion.2), channel_id=1, source_target_pairs={{0,8},{8,0},{16,24},{24,16},{1,9},{9,1},{17,25},{25,17},{2,10},{10... | collective-permute-start | bytes 4718600 | tf_op jit(solution)/shard_map/ppermute | solution.py:708
  411.1 90.0 %collective-permute-start.17 = (bf16[4,2,2,80,512]{4,3,2,1,0:T(8,128)(2,1)}, bf16[4,2,2,80,512]{4,3,2,1,0:T(8,128)(2,1)}, u32[]{:S(2)}, u32[]{:S(2)}) collective-permute-start(bf16[4,2,2,80,512]{4,3,2,1,0:T(8,128)(2,1)} %dynamic-slice_bitcast_fusion.3), channel_id=1, source_target_pairs={{0,16},{8,24},{16,0},{24,8},{1,17},{9,25},{17,1},{25,9},{2,18},{10... | collective-permute-start | bytes 3932168 | tf_op jit(solution)/shard_map/ppermute | solution.py:708
  467.0 25.2 %collective-permute-start.15 = (bf16[576,3072]{1,0:T(8,128)(2,1)}, bf16[576,3072]{1,0:T(8,128)(2,1)}, u32[]{:S(2)}, u32[]{:S(2)}) collective-permute-start(bf16[576,3072]{1,0:T(8,128)(2,1)} %get-tuple-element.138), channel_id=1, source_target_pairs={{0,1},{1,0},{2,3},{3,2},{4,5},{5,4},{6,7},{7,6},{8,9},{9,8},{10,11... | collective-permute-start | bytes 10616840 | tf_op jit(solution)/shard_map/ppermute | solution.py:708
  467.0 46.2 %collective-permute-start.18 = (bf16[2,2,2,192,384]{4,3,2,1,0:T(8,128)(2,1)}, bf16[2,2,2,192,384]{4,3,2,1,0:T(8,128)(2,1)}, u32[]{:S(2)}, u32[]{:S(2)}) collective-permute-start(bf16[2,2,2,192,384]{4,3,2,1,0:T(8,128)(2,1)} %get-tuple-element.83), channel_id=1, source_target_pairs={{0,8},{8,0},{16,24},{24,16},{1,9},{9,1},{17,25},{25,17},{2,10},{10... | collective-permute-start | bytes 3538952 | tf_op jit(solution)/shard_map/ppermute | solution.py:708
  492.2 29.1 %collective-permute-start.19 = (bf16[2,2,2,192,384]{4,3,2,1,0:T(8,128)(2,1)}, bf16[2,2,2,192,384]{4,3,2,1,0:T(8,128)(2,1)}, u32[]{:S(2)}, u32[]{:S(2)}) collective-permute-start(bf16[2,2,2,192,384]{4,3,2,1,0:T(8,128)(2,1)} %get-tuple-element.84), channel_id=1, source_target_pairs={{0,16},{8,24},{16,0},{24,8},{1,17},{9,25},{17,1},{25,9},{2,18},{10... | collective-permute-start | bytes 3538952 | tf_op jit(solution)/shard_map/ppermute | solution.py:708
  501.2 44.7 %collective-permute-start.20 = (bf16[2,2,2,192,384]{4,3,2,1,0:T(8,128)(2,1)S(1)}, bf16[2,2,2,192,384]{4,3,2,1,0:T(8,128)(2,1)S(1)}, u32[]{:S(2)}, u32[]{:S(2)}) collective-permute-start(bf16[2,2,2,192,384]{4,3,2,1,0:T(8,128)(2,1)S(1)} %copy-done.36), channel_id=1, source_target_pairs={{0,8},{8,0},{16,24},{24,16},{1,9},{9,1},{17,25},{25,17},{2,10},{10... | collective-permute-start | bytes 3538952 | tf_op jit(solution)/shard_map/ppermute | solution.py:708
  501.7 44.1 %collective-permute-start.21 = (bf16[2,2,2,192,384]{4,3,2,1,0:T(8,128)(2,1)}, bf16[2,2,2,192,384]{4,3,2,1,0:T(8,128)(2,1)S(1)}, u32[]{:S(2)}, u32[]{:S(2)}) collective-permute-start(bf16[2,2,2,192,384]{4,3,2,1,0:T(8,128)(2,1)} %get-tuple-element.89), channel_id=1, source_target_pairs={{0,16},{8,24},{16,0},{24,8},{1,17},{9,25},{17,1},{25,9},{2,18},{10... | collective-permute-start | bytes 3538952 | tf_op jit(solution)/shard_map/ppermute | solution.py:708
  (64 other events, 275.9 us)

commit v6 on v5

--- a/solution.py
+++ b/solution.py
@@ -53,15 +53,16 @@
     lax.fori_loop(0, side // GROUP, rows, 0)
 
 
-def section_mix(maps, taps, gain, mixed, rows, pad):
-    side, _, channels = maps.shape
-    clear_edges(pad, side)
-
+def mix_blocks(first, last, maps, taps, mixed, pad):
     def blocks(block, carry):
         mix_block(block, maps, taps, mixed, pad)
         return carry
 
-    lax.fori_loop(0, channels // LANES, blocks, 0)
+    lax.fori_loop(first, last, blocks, 0)
+
+
+def norm_all(gain, mixed, rows):
+    side, _, channels = mixed.shape
 
     def norm(pair, carry):
         v = mixed[pl.ds(2 * pair, 2)].reshape(2 * side, channels)
@@ -106,9 +107,10 @@
     shards = refs[:count]
     maps, taps, gain, scale, target = refs[count : count + 5]
     fulls = refs[count + 5 : 2 * count + 5]
-    mixed, rows, targets, expanded, active, reduced, features = refs[2 * count + 5 : 2 * count + 12]
+    mixed_out, rows_out, targets, expanded, block_active, block_reduced, features = refs[2 * count + 5 : 2 * count + 12]
     pad, wide_w, deep_w, total, stage, pair_sum, pooled, leaving, met, sorted_maps, landing = refs[2 * count + 12 : 2 * count + 23]
-    zs, zr, ps, pr, cs, cr, os, orr, ls, ts, tr, ws, es, fs, fr, gs, gr = refs[2 * count + 23 :]
+    mixed, rows, active = refs[2 * count + 23 : 2 * count + 26]
+    zs, zr, ps, pr, cs, cr, os, orr, ls, ts, tr, ws, es, fs, fr, gs, gr, xs = refs[2 * count + 26 :]
     p, d = lax.axis_index("path"), lax.axis_index("dev")
 
     def at(m):
@@ -166,7 +168,14 @@
     named = [copy(target, targets.at[p], ts.at[m - 1], tr.at[m - 1], (m, 0)) for m in (1, 2, 3)]
     for c in named:
         c.start()
-    section_mix(maps, taps, gain, mixed, rows, pad)
+    clear_edges(pad, maps.shape[0])
+    blocks = maps.shape[2] // LANES
+    leaving_vmem = []
+
+    def write_out(src, dst):
+        c = pltpu.make_async_copy(src, dst, xs.at[len(leaving_vmem)])
+        c.start()
+        leaving_vmem.append(c)
 
     ready = set()
 
@@ -176,6 +185,18 @@
             own[w][0].wait()
             own[w][1].wait_recv()
 
+    def cell_row(row):
+        side = maps.shape[0]
+        return pl.ds(pl.multiple_of(row * side, 8), side)
+
+    def pairs(value):
+        blocks, half = value.shape[1] // LANES, value.shape[0] // 2
+        for k in range(blocks):
+            pair_sum[k] = value[:, k * LANES : (k + 1) * LANES]
+        return [
+            pair_sum[k, pl.ds(0, half, stride=2), :] + pair_sum[k, pl.ds(1, half, stride=2), :] for k in range(blocks)
+        ]
+
     def expand_block(c0, nc):
         load = pltpu.make_async_copy(fulls[expand].at[:, pl.ds(c0, nc)], wide_w, ws.at[0])
         load.start()
@@ -185,7 +206,18 @@
             here = pl.multiple_of(j * STEP, STEP)
             product(rows, wide_w, total, 0, here)
             stage[...] = total[...]
-            active[:, pl.ds(c0 + here, STEP)] = jax.nn.gelu(total[...]).astype(jnp.bfloat16)
+            low = jax.nn.gelu(total[...]).astype(jnp.bfloat16)
+            active[:, pl.ds(c0 + here, STEP)] = low
+            total[...] = low.astype(jnp.float32)
+
+            def block_sums(h, inner):
+                sums = pairs(total[cell_row(2 * h), :] + total[cell_row(2 * h + 1), :])
+                for k, value in enumerate(sums):
+                    lanes = pl.ds(pl.multiple_of(c0 + here + k * LANES, LANES), LANES)
+                    block_active[h, :, lanes] = value.astype(jnp.bfloat16)
+                return inner
+
+            lax.fori_loop(0, maps.shape[0] // 2, block_sums, 0)
             out = pltpu.make_async_copy(stage, expanded.at[:, pl.ds(c0 + here, STEP)], es.at[0])
             out.start()
             out.wait()
@@ -199,22 +231,16 @@
         load.wait()
         cols = pl.ds(c0, nc)
         product(active, deep_w, total, 0, 0)
-        reduced[:, cols] = total[...]
         side = maps.shape[0]
 
         def pool(h, carry):
-            both = jnp.zeros((side, nc), jnp.float32)
-            for r in range(2):
-                row = 2 * h + r
-                part = total[pl.ds(pl.multiple_of(row * side, 8), side), :]
-                both += maps[row, :, cols].astype(jnp.float32) + scale[:, cols] * part
-            half = side // 2
-            for k in range(nc // LANES):
-                pair_sum[k] = both[:, k * LANES : (k + 1) * LANES]
-            for k in range(nc // LANES):
-                even = pair_sum[k, pl.ds(0, half, stride=2), :]
-                odd = pair_sum[k, pl.ds(1, half, stride=2), :]
-                pooled[h, :, c0 + k * LANES : c0 + (k + 1) * LANES] = (even + odd) * 0.25
+            part = pairs(total[cell_row(2 * h), :] + total[cell_row(2 * h + 1), :])
+            for k, value in enumerate(part):
+                block_reduced[h, :, c0 + k * LANES : c0 + (k + 1) * LANES] = value * 0.25
+            cells = pairs(maps[2 * h, :, cols].astype(jnp.float32) + maps[2 * h + 1, :, cols].astype(jnp.float32))
+            for k, value in enumerate(cells):
+                lanes = slice(c0 + k * LANES, c0 + (k + 1) * LANES)
+                pooled[h, :, lanes] = value * 0.25 + scale[:, lanes] * block_reduced[h, :, lanes]
             return carry
 
         lax.fori_loop(0, side // 2, pool, 0)
@@ -276,6 +302,12 @@
                 DG(i - 2, k, 0).wait_recv()
                 DG(i - 2, k, 1).wait_recv()
                 S(i - 2, k).start()
+        if i < MIX_STEPS:
+            mix_blocks(i * blocks // MIX_STEPS, (i + 1) * blocks // MIX_STEPS, maps, taps, mixed, pad)
+        if i + 1 == MIX_STEPS:
+            norm_all(gain, mixed, rows)
+            write_out(mixed, mixed_out)
+            write_out(rows, rows_out)
         if 0 <= i - 3 < J:
             for k in range(3):
                 S(i - 3, k).wait_recv()
@@ -291,6 +323,8 @@
                 routed = route_two(routed)
             if i - 3 == last_reduce + 2:
                 route_three(routed)
+    for c in leaving_vmem:
+        c.wait()
     for w in range(count):
         ensure(w)
         own[w][1].wait_send()
@@ -304,6 +338,7 @@
 
 
 AHEAD = 3
+MIX_STEPS = 3
 GATHER_ORDER = (4, 0, 1, 5, 6, 3, 2)
 
 
@@ -326,12 +361,12 @@
             shape((cells, channels), low),
             shape((4, 8, LANES), jnp.int32),
             shape((cells, hidden), full),
-            shape((cells, hidden), low),
-            shape((cells, channels), full),
+            shape((side // 2, side // 2, hidden), low),
+            shape((side // 2, side // 2, channels), full),
             shape((cells // 4, channels), low),
         ],
         in_specs=[anyspec] * n + [whole] * 5,
-        out_specs=[anyspec] * n + [whole] * 3 + [anyspec] + [whole] * 3,
+        out_specs=[anyspec] * n + [anyspec] * 2 + [whole] + [anyspec] + [whole] * 3,
         scratch_shapes=[
             VMEM((side + 2 * REACH, side + 2 * EDGE, LANES), full),
             VMEM((channels, wide), low),
@@ -344,9 +379,12 @@
             VMEM((4, cells // 4, channels // 4), low),
             VMEM((4, cells // 4, channels // 4), low),
             VMEM((4, cells // 4, channels // 4), low),
+            VMEM(maps.shape, full),
+            VMEM((cells, channels), low),
+            VMEM((cells, hidden), low),
         ]
         + [dma((J, 3)), dma((J, 3)), dma((J, 3, 4)), dma((J, 3, 4)), dma((J, 3)), dma((J, 3))]
-        + [dma((n,)), dma((n,)), dma((n,)), dma((3,)), dma((3,)), dma((2,)), dma((1,))] + [dma((3,))] * 4,
+        + [dma((n,)), dma((n,)), dma((n,)), dma((3,)), dma((3,)), dma((2,)), dma((1,))] + [dma((3,))] * 4 + [dma((4,))],
         compiler_params=pltpu.CompilerParams(
             collective_id=0, has_side_effects=True, vmem_limit_bytes=60 * 2**20
         ),
@@ -797,7 +835,7 @@
     tuned = lax.axis_size("path") == 4 and lax.axis_size("dev") == 8
     weights = (w_expand, w_reduce, w_adapter, w_qkv, w_out, w_fc1, w_fc2)
     if tuned:
-        ordered, section_mixed, section_rows, spread_targets, expanded, activated_low, reduced, features = gather_weights(
+        ordered, section_mixed, section_rows, spread_targets, expanded, block_active, block_reduced, features = gather_weights(
             [weights[i] for i in GATHER_ORDER],
             hires_maps[0],
             section_kernel,
@@ -826,7 +864,8 @@
         section_normed, section_norm_back = jax.vjp(layer_norm, section_mixed, section_gain)
     if tuned:
         _, section_gelu_back = jax.vjp(jax.nn.gelu, expanded)
-        reduced = reduced.reshape(maps_float.shape)
+        block_active = block_active.reshape(tokens, -1)
+        block_reduced = block_reduced.reshape(tokens, channels)
     else:
         section_rows = section_normed.reshape(-1, channels).astype(jnp.bfloat16)
         expanded = jnp.dot(section_rows, full_expand, preferred_element_type=jnp.float32)
@@ -962,10 +1001,17 @@
     grad_section_out = jnp.broadcast_to(quarter, (1, grid_side, 2, grid_side, 2, channels)).reshape(
         maps_float.shape
     )
-    grad_scale = jnp.sum((grad_section_out * reduced).reshape(-1, channels), axis=0)
-    grad_reduced = (grad_section_out * layer_scale).reshape(-1, channels).astype(jnp.bfloat16)
-    if tuned:
-        part_reduce = pair_gradient(both_images(activated_low), grad_reduced)
+    if tuned:
+        grad_scale = jnp.sum(grad_pooled * block_reduced, axis=0)
+        block_grad = (grad_pooled * 0.25 * layer_scale).astype(jnp.bfloat16)
+        grad_reduced = jnp.broadcast_to(
+            block_grad.reshape(grid_side, 1, grid_side, 1, channels), (grid_side, 2, grid_side, 2, channels)
+        ).reshape(-1, channels)
+    else:
+        grad_scale = jnp.sum((grad_section_out * reduced).reshape(-1, channels), axis=0)
+        grad_reduced = (grad_section_out * layer_scale).reshape(-1, channels).astype(jnp.bfloat16)
+    if tuned:
+        part_reduce = pair_gradient(both_images(block_active), block_grad)
         columns = part_reduce.shape[5] // 2
         leaving = [
             pick(part_reduce[first : first + 2, ..., :columns], 1 - place()[2], 3) for first in (0, 2)

time: 804 us -> 785 us (0.976)
  matrix products: 139 us -> 130 us
    dot_general x7, matrix products: 50.7 us -> 41 us  [pair_product(): lax.dot_general(rows, grads, (((0,), (0,)), ((), ())), preferred_element_...]
  transfers between devices with their start and end apart: 24 -> 24, of which waited for: 2 -> 4; matrix products, arithmetic and copies ran while one was open for 26% -> 24% of each run, Pallas kernels for 0% -> 0%
where the time goes in v6:
time: 785 us; the launch traced here: 778 us
  Pallas kernels  493 us (63%)
  matrix products  130 us (17%)
  local copies, waits for them, and re-layouts  59.2 us (8%)
  other arithmetic  53 us (7%)
  waiting for transfers between devices  20.3 us (3%)
  starting transfers between devices  20 us (3%)
    pallas_call x1, Pallas kernels, gather_weights(): pl.pallas_call(functools.partial(gather_kernel, jobs, n, expand, reduce),...  264 us
    pallas_call x1, Pallas kernels, scatter_gradients(): pl.pallas_call(scatter_kernel, out_shape=[jax.ShapeDtypeStruct(maps.shape...  229 us
    dot_general x7, matrix products, pair_product(): lax.dot_general(rows, grads, (((0,), (0,)), ((), ())), preferred_element_...  41 us
    dot_general x1, matrix products, local(): jnp.dot(grad_reduced, full_reduce.T, preferred_element_type=jnp.float32)  24.4 us
    ppermute x22, waiting for transfers between devices, swap(): return lax.ppermute(value, axis, [(i, i ^ mask) for i in range(size)])  20.3 us
    dot_general x1, matrix products, local(): jnp.dot(grad_expanded, full_expand.T, preferred_element_type=jnp.float32)  18.3 us
  transfers between devices with their start and end apart: 24, of which 4 were waited for; matrix products, arithmetic and copies ran while one was open for 24% of the time, Pallas kernels for 0%

profile of v6, /device:TPU:0, one launch (start us, length us, event | category | flops | bytes accessed | tf_op | source)
XLA Modules:
  0.0 778.1 jit_solution(8764724577044601216)
XLA Ops:
  4.5 264.1 %shard_map.305 = (bf16[1024,1024]{1,0:T(8,128)(2,1)}, bf16[1536,6144]{1,0:T(8,128)(2,1)}, bf16[6144,1536]{1,0:T(8,128)(2,1)}, bf16[1024,4096]{1,0:T(8,128)(2,1)}...) custom-call(bf16[128,1024]{1,0:T(8,128)(2,1)} %refs_0_.1, ...), custom_call_target="tpu_custom_call" | custom-call | tf_op jit(solution)/shard_map/pallas_call | solution.py:356
  273.9 4.0 convolution_convert_fusion.5
  289.9 6.7 multiply_convert_fusion.1
  296.6 4.1 fusion.24
  322.7 3.2 convolution_convert_fusion.8
  326.7 4.1 all-to-all-start
  335.1 5.9 fusion.44
  343.1 3.9 reshape.479
  353.0 4.0 all-to-all-start.1
  357.7 3.2 convolution_convert_fusion.3
  368.5 3.4 convolution_convert_fusion.4
  375.4 4.0 convolution_convert_fusion.2
  396.8 3.8 broadcast_in_dim.102
  401.2 7.3 convolution_convert_fusion.1
  416.0 24.4 %fusion.7 = bf16[576,6144]{1,0:T(8,128)(2,1)} fusion(f32[576,6144]{1,0:T(8,128)} %get-tuple-element.76, bf16[576,1536]{1,0:T(8,128)(2,1)S(1)} %copy-done.32, bf16[6144,1536]{1,0:T(8,128)(2,1)} %get-tuple-element.75), kind=kOutput, calls=%fused_computation.9 | convolution fusion | flops 10942414848 | bytes 41877504 | tf_op jit(solution)/shard_map/dot_general | solution.py:1023
  442.3 4.5 broadcast_select_fusion.1
  446.8 18.3 %fusion.104 = f32[576,1536]{1,0:T(8,128)} fusion(bf16[576,6144]{1,0:T(8,128)(2,1)} %fusion.7, bf16[1536,6144]{1,0:T(8,128)(2,1)} %get-tuple-element.80), kind=kOutput, calls=%fused_computation.235 | convolution fusion | flops 10871635968 | bytes 29491200 | tf_op jit(solution)/shard_map/dot_general | solution.py:1029
  465.2 4.6 fusion.8.t1
  471.2 3.6 fusion.9.t0
  474.8 5.4 pad_maximum_fusion
  480.8 17.7 %collective-permute-done.18.land0a = bf16[2,2,2,192,384]{4,3,2,1,0:T(8,128)(2,1)} collective-permute-done((bf16[2,2,2,192,384]{4,3,2,1,0:T(8,128)(2,1)}, bf16[2,2,2,192,384]{4,3,2,1,0:T(8,128)(2,1)}, u32[]{:S(2)}, u32[]{:S(2)}) %collective-permute-start.18) | collective-permute-done | bytes 1179680 | tf_op jit(solution)/shard_map/ppermute | solution.py:746
  498.8 18.7 %convolution_convert_fusion = bf16[1536,3072]{1,0:T(8,128)(2,1)} fusion(bf16[1152,3072]{1,0:T(8,128)(2,1)} %pad_maximum_fusion, bf16[576,1536]{1,0:T(8,128)(2,1)} %collective-permute-done.12, bf16[576,1536]{1,0:T(8,128)(2,1)} %get-tuple-element.73), kind=kOutput, calls=%fused_computation.10 | convolution fusion | flops 10883432448 | bytes 20054016 | tf_op jit(solution)/shard_map/dot_general | solution.py:775
  523.7 229.1 %shard_map.306 = (f32[24,24,1536]{2,1,0:T(8,128)}, f32[64,1536]{1,0:T(8,128)}, bf16[4,128,1024]{2,1,0:T(8,128)(2,1)}, bf16[4,32,4096]{2,1,0:T(8,128)(2,1)}, bf16...) custom-call(bf16[4,2,2,2,192,768]{5,4,3,2,1,0:T(8,128)(2,1)} %bitcas, ...), custom_call_target="tpu_custom_call" | custom-call | tf_op jit(solution)/shard_map/pallas_call | solution.py:701
  770.7 3.2 bitcast_convert_fusion
  (270 shorter events, 124.5 us)
Async XLA Ops:
  286.6 61.8 %collective-permute-start.6 = (bf16[144,1024]{0,1:T(8,128)(2,1)}, bf16[144,1024]{0,1:T(8,128)(2,1)}, u32[]{:S(2)}, u32[]{:S(2)}) collective-permute-start(bf16[144,1024]{0,1:T(8,128)(2,1)} %bitcast.13), channel_id=1, source_target_pairs={{0,1},{1,0},{2,3},{3,2},{4,5},{5,4},{6,7},{7,6},{8,9},{9,8},{10,11... | collective-permute-start | bytes 884744 | tf_op jit(solution)/shard_map/ppermute | solution.py:746
  289.4 79.0 %collective-permute-start.2 = (bf16[144,1024]{1,0:T(8,128)(2,1)}, bf16[144,1024]{1,0:T(8,128)(2,1)}, u32[]{:S(2)}, u32[]{:S(2)}) collective-permute-start(bf16[144,1024]{1,0:T(8,128)(2,1)} %multiply_convert_fusion.4), channel_id=1, source_target_pairs={{0,1},{1,0},{2,3},{3,2},{4,5},{5,4},{6,7},{7,6},{8,9},{9,8},{10,11... | collective-permute-start | bytes 884744 | tf_op jit(solution)/shard_map/ppermute | solution.py:746
  326.7 24.0 %all-to-all-start = ((bf16[4,36,1536]{2,1,0:T(8,128)(2,1)}), bf16[4,36,1536]{2,1,0:T(8,128)(2,1)}, u32[]{:S(2)}, u32[]{:S(2)}) async-start(bf16[4,36,1536]{2,1,0:T(8,128)(2,1)} %reshape.471), calls=%async_computation | async-start | bytes 983040 | tf_op jit(solution)/shard_map/all_to_all | solution.py:986
  330.9 44.5 %collective-permute-start = (bf16[144,4096]{1,0:T(8,128)(2,1)}, bf16[144,4096]{1,0:T(8,128)(2,1)}, u32[]{:S(2)}, u32[]{:S(2)}) collective-permute-start(bf16[144,4096]{1,0:T(8,128)(2,1)} %get-tuple-element.181), channel_id=1, source_target_pairs={{0,1},{1,0},{2,3},{3,2},{4,5},{5,4},{6,7},{7,6},{8,9},{9,8},{10,11... | collective-permute-start | bytes 3538952 | tf_op jit(solution)/shard_map/ppermute | solution.py:746
  333.9 23.3 %collective-permute-start.5 = (bf16[144,1536]{1,0:T(8,128)(2,1)}, bf16[144,1536]{1,0:T(8,128)(2,1)}, u32[]{:S(2)}, u32[]{:S(2)}) collective-permute-start(bf16[144,1536]{1,0:T(8,128)(2,1)} %get-tuple-element.144), channel_id=1, source_target_pairs={{0,1},{1,0},{2,3},{3,2},{4,5},{5,4},{6,7},{7,6},{8,9},{9,8},{10,11... | collective-permute-start | bytes 1327112 | tf_op jit(solution)/shard_map/ppermute | solution.py:746
  334.8 13.2 %collective-permute-start.7 = (bf16[144,512]{1,0:T(8,128)(2,1)S(1)}, bf16[144,512]{1,0:T(8,128)(2,1)}, u32[]{:S(2)}, u32[]{:S(2)}) collective-permute-start(bf16[144,512]{1,0:T(8,128)(2,1)S(1)} %get-tuple-element.160), channel_id=1, source_target_pairs={{0,1},{1,0},{2,3},{3,2},{4,5},{5,4},{6,7},{7,6},{8,9},{9,8},{10,11... | collective-permute-start | bytes 442376 | tf_op jit(solution)/shard_map/ppermute | solution.py:746
  348.0 9.0 %collective-permute-start.4 = (bf16[144,1024]{1,0:T(8,128)(2,1)S(1)}, bf16[144,1024]{1,0:T(8,128)(2,1)}, u32[]{:S(2)}, u32[]{:S(2)}) collective-permute-start(bf16[144,1024]{1,0:T(8,128)(2,1)S(1)} %copy-done.23), channel_id=1, source_target_pairs={{0,1},{1,0},{2,3},{3,2},{4,5},{5,4},{6,7},{7,6},{8,9},{9,8},{10,11... | collective-permute-start | bytes 884744 | tf_op jit(solution)/shard_map/ppermute | solution.py:746
  348.3 12.7 %collective-permute-start.8 = (bf16[144,1536]{1,0:T(8,128)(2,1)}, bf16[144,1536]{1,0:T(8,128)(2,1)}, u32[]{:S(2)}, u32[]{:S(2)}) collective-permute-start(bf16[144,1536]{1,0:T(8,128)(2,1)} %get-tuple-element.63), channel_id=1, source_target_pairs={{0,1},{1,0},{2,3},{3,2},{4,5},{5,4},{6,7},{7,6},{8,9},{9,8},{10,11... | collective-permute-start | bytes 1327112 | tf_op jit(solution)/shard_map/ppermute | solution.py:746
  353.0 29.8 %all-to-all-start.1 = ((bf16[4,36,1536]{2,1,0:T(8,128)(2,1)}), bf16[4,36,1536]{2,1,0:T(8,128)(2,1)S(1)}, u32[]{:S(2)}, u32[]{:S(2)}) async-start(bf16[4,36,1536]{2,1,0:T(8,128)(2,1)} %copy.83), calls=%async_computation.1 | async-start | bytes 983040 | tf_op jit(solution)/shard_map/all_to_all | solution.py:990
  357.1 18.3 %collective-permute-start.1 = (bf16[144,512]{1,0:T(8,128)(2,1)S(1)}, bf16[144,512]{1,0:T(8,128)(2,1)S(1)}, u32[]{:S(2)}, u32[]{:S(2)}) collective-permute-start(bf16[144,512]{1,0:T(8,128)(2,1)S(1)} %get-tuple-element.164), channel_id=1, source_target_pairs={{0,1},{1,0},{2,3},{3,2},{4,5},{5,4},{6,7},{7,6},{8,9},{9,8},{10,11... | collective-permute-start | bytes 442376 | tf_op jit(solution)/shard_map/ppermute | solution.py:746
  357.2 3.6 collective-permute-start.9
  360.9 7.6 collective-permute-start.3
  361.0 40.1 %collective-permute-start.10 = (bf16[144,6144]{1,0:T(8,128)(2,1)}, bf16[144,6144]{1,0:T(8,128)(2,1)}, u32[]{:S(2)}, u32[]{:S(2)}) collective-permute-start(bf16[144,6144]{1,0:T(8,128)(2,1)} %reshape.479), channel_id=1, source_target_pairs={{0,1},{1,0},{2,3},{3,2},{4,5},{5,4},{6,7},{7,6},{8,9},{9,8},{10,11... | collective-permute-start | bytes 5308424 | tf_op jit(solution)/shard_map/ppermute | solution.py:746
  368.4 130.5 %collective-permute-start.12 = (bf16[576,1536]{1,0:T(8,128)(2,1)}, bf16[576,1536]{1,0:T(8,128)(2,1)}, u32[]{:S(2)}, u32[]{:S(2)}) collective-permute-start(bf16[576,1536]{1,0:T(8,128)(2,1)} %get-tuple-element.73), channel_id=1, source_target_pairs={{0,1},{1,0},{2,3},{3,2},{4,5},{5,4},{6,7},{7,6},{8,9},{9,8},{10,11... | collective-permute-start | bytes 5308424 | tf_op jit(solution)/shard_map/ppermute | solution.py:746
  390.3 10.2 %collective-permute-start.11 = (bf16[144,768]{1,0:T(8,128)(2,1)}, bf16[144,768]{1,0:T(8,128)(2,1)}, u32[]{:S(2)}, u32[]{:S(2)}) collective-permute-start(bf16[144,768]{1,0:T(8,128)(2,1)} %get-tuple-element.158), channel_id=1, source_target_pairs={{0,1},{1,0},{2,3},{3,2},{4,5},{5,4},{6,7},{7,6},{8,9},{9,8},{10,11... | collective-permute-start | bytes 663560 | tf_op jit(solution)/shard_map/ppermute | solution.py:746
  390.7 49.7 %collective-permute-start.13 = (bf16[4,2,2,128,512]{4,3,2,1,0:T(8,128)(2,1)}, bf16[4,2,2,128,512]{4,3,2,1,0:T(8,128)(2,1)}, u32[]{:S(2)}, u32[]{:S(2)}) collective-permute-start(bf16[4,2,2,128,512]{4,3,2,1,0:T(8,128)(2,1)} %dynamic-slice_bitcast_fusion.1), channel_id=1, source_target_pairs={{0,8},{8,0},{16,24},{24,16},{1,9},{9,1},{17,25},{25,17},{2,10},{10... | collective-permute-start | bytes 6291464 | tf_op jit(solution)/shard_map/ppermute | solution.py:746
  392.8 49.5 %collective-permute-start.14 = (bf16[4,2,2,32,2048]{4,3,2,1,0:T(8,128)(2,1)}, bf16[4,2,2,32,2048]{4,3,2,1,0:T(8,128)(2,1)}, u32[]{:S(2)}, u32[]{:S(2)}) collective-permute-start(bf16[4,2,2,32,2048]{4,3,2,1,0:T(8,128)(2,1)} %dynamic-slice_bitcast_fusion), channel_id=1, source_target_pairs={{0,16},{8,24},{16,0},{24,8},{1,17},{9,25},{17,1},{25,9},{2,18},{10... | collective-permute-start | bytes 6291464 | tf_op jit(solution)/shard_map/ppermute | solution.py:746
  400.6 80.2 %collective-permute-start.16 = (bf16[4,2,2,32,1536]{4,3,2,1,0:T(8,128)(2,1)}, bf16[4,2,2,32,1536]{4,3,2,1,0:T(8,128)(2,1)S(1)}, u32[]{:S(2)}, u32[]{:S(2)}) collective-permute-start(bf16[4,2,2,32,1536]{4,3,2,1,0:T(8,128)(2,1)} %dynamic-slice_bitcast_fusion.2), channel_id=1, source_target_pairs={{0,8},{8,0},{16,24},{24,16},{1,9},{9,1},{17,25},{25,17},{2,10},{10... | collective-permute-start | bytes 4718600 | tf_op jit(solution)/shard_map/ppermute | solution.py:746
  401.1 79.0 %collective-permute-start.17 = (bf16[4,2,2,80,512]{4,3,2,1,0:T(8,128)(2,1)}, bf16[4,2,2,80,512]{4,3,2,1,0:T(8,128)(2,1)S(1)}, u32[]{:S(2)}, u32[]{:S(2)}) collective-permute-start(bf16[4,2,2,80,512]{4,3,2,1,0:T(8,128)(2,1)} %dynamic-slice_bitcast_fusion.3), channel_id=1, source_target_pairs={{0,16},{8,24},{16,0},{24,8},{1,17},{9,25},{17,1},{25,9},{2,18},{10... | collective-permute-start | bytes 3932168 | tf_op jit(solution)/shard_map/ppermute | solution.py:746
  440.4 58.1 %collective-permute-start.18 = (bf16[2,2,2,192,384]{4,3,2,1,0:T(8,128)(2,1)}, bf16[2,2,2,192,384]{4,3,2,1,0:T(8,128)(2,1)}, u32[]{:S(2)}, u32[]{:S(2)}) collective-permute-start(bf16[2,2,2,192,384]{4,3,2,1,0:T(8,128)(2,1)} %get-tuple-element.83), channel_id=1, source_target_pairs={{0,8},{8,0},{16,24},{24,16},{1,9},{9,1},{17,25},{25,17},{2,10},{10... | collective-permute-start | bytes 3538952 | tf_op jit(solution)/shard_map/ppermute | solution.py:746
  446.8 22.9 %collective-permute-start.15 = (bf16[576,3072]{1,0:T(8,128)(2,1)}, bf16[576,3072]{1,0:T(8,128)(2,1)}, u32[]{:S(2)}, u32[]{:S(2)}) collective-permute-start(bf16[576,3072]{1,0:T(8,128)(2,1)} %get-tuple-element.138), channel_id=1, source_target_pairs={{0,1},{1,0},{2,3},{3,2},{4,5},{5,4},{6,7},{7,6},{8,9},{9,8},{10,11... | collective-permute-start | bytes 10616840 | tf_op jit(solution)/shard_map/ppermute | solution.py:746
  469.8 29.1 %collective-permute-start.19 = (bf16[2,2,2,192,384]{4,3,2,1,0:T(8,128)(2,1)}, bf16[2,2,2,192,384]{4,3,2,1,0:T(8,128)(2,1)}, u32[]{:S(2)}, u32[]{:S(2)}) collective-permute-start(bf16[2,2,2,192,384]{4,3,2,1,0:T(8,128)(2,1)} %get-tuple-element.84), channel_id=1, source_target_pairs={{0,16},{8,24},{16,0},{24,8},{1,17},{9,25},{17,1},{25,9},{2,18},{10... | collective-permute-start | bytes 3538952 | tf_op jit(solution)/shard_map/ppermute | solution.py:746
  480.2 43.1 %collective-permute-start.20 = (bf16[2,2,2,192,384]{4,3,2,1,0:T(8,128)(2,1)}, bf16[2,2,2,192,384]{4,3,2,1,0:T(8,128)(2,1)}, u32[]{:S(2)}, u32[]{:S(2)}) collective-permute-start(bf16[2,2,2,192,384]{4,3,2,1,0:T(8,128)(2,1)} %get-tuple-element.87), channel_id=1, source_target_pairs={{0,8},{8,0},{16,24},{24,16},{1,9},{9,1},{17,25},{25,17},{2,10},{10... | collective-permute-start | bytes 3538952 | tf_op jit(solution)/shard_map/ppermute | solution.py:746
  480.8 43.0 %collective-permute-start.21 = (bf16[2,2,2,192,384]{4,3,2,1,0:T(8,128)(2,1)}, bf16[2,2,2,192,384]{4,3,2,1,0:T(8,128)(2,1)}, u32[]{:S(2)}, u32[]{:S(2)}) collective-permute-start(bf16[2,2,2,192,384]{4,3,2,1,0:T(8,128)(2,1)} %get-tuple-element.89), channel_id=1, source_target_pairs={{0,16},{8,24},{16,0},{24,8},{1,17},{9,25},{17,1},{25,9},{2,18},{10... | collective-permute-start | bytes 3538952 | tf_op jit(solution)/shard_map/ppermute | solution.py:746
  (56 other events, 247.0 us)

commit v7 on v6

--- a/solution.py
+++ b/solution.py
@@ -401,13 +401,13 @@
 
 
 def scatter_kernel(
-    big0, big1, land0a, land0b, land0c, land0d, t0, t1, t2, t3, small_in, grad_normed, mixed, maps, taps, gain,
+    big0, big1, land0a, land0b, land0c, land0d, t0, t1, t2, t3, small_in, grad_normed_in, mixed_in, maps_in, taps, gain,
     grad_maps, small_out, o0, o1, o2, o3, o4, o5, land1a, land1b,
     acc0a, acc0b, acc1a, acc1b, two0a, two0b, two1a, two1b, tmp0, tmp1,
     own0, own1, own2, own3, two0, two1, two2, two3,
     zr0, zr1, zr2, zr3, zr4, zr5, low0, low1, low2, low3, low4, low5,
     full0, full1, full2, full3, full4, full5,
-    small_at, small_from, pad, grad_pad, tap_sums, ssem, rsem, lsem,
+    grad_normed, mixed, maps, small_at, small_from, pad, grad_pad, tap_sums, ssem, rsem, lsem,
 ):
     p, d = lax.axis_index("path"), lax.axis_index("dev")
     up, across, height, side = p // 2, lax.rem(p, 2), d // 2, lax.rem(d, 2)
@@ -630,7 +630,10 @@
     thin_parts = [[group[2]] for group in thin]
     parts_reduce, parts_expand = wide[0][3], wide[1][3]
     thin_sent = [thin_two(i) for i in range(4)]
+    arriving = [fetch(grad_normed_in, grad_normed), fetch(mixed_in, mixed), fetch(maps_in, maps)]
     one_reduce = wide_one(0, False)
+    for copy in arriving:
+        copy.wait()
     norm_back()
     blocks(0, count // 6)
     two_reduce = wide_two(0, one_reduce)
@@ -695,6 +698,7 @@
     scratch += [VMEM((2,) + f, low) for f in finals]
     scratch += [VMEM((f[0], 2 * f[1]), low) for f in finals]
     edge = (side + 2 * REACH, side + 2 * EDGE, LANES)
+    scratch += [VMEM(maps.shape, full)] * 2 + [VMEM(maps.shape, low)]
     scratch += [VMEM((6,) + small.shape, full)] * 2
     scratch += [VMEM(edge, full)] * 2 + [VMEM((SIDE * SIDE, 8, LANES), full)]
     scratch += [dma((120,)), dma((120,)), dma((48,))]
@@ -703,7 +707,7 @@
         out_shape=[jax.ShapeDtypeStruct(maps.shape, full), jax.ShapeDtypeStruct(small.shape, full)]
         + [jax.ShapeDtypeStruct((4, f[0], 2 * f[1]), low) for f in finals]
         + landing,
-        in_specs=[anyspec] * 10 + [whole] * 6,
+        in_specs=[anyspec] * 10 + [whole] + [anyspec] * 3 + [whole] * 2,
         out_specs=[whole] * 2 + [anyspec] * 8,
         scratch_shapes=scratch,
         compiler_params=pltpu.CompilerParams(

time: 785 us -> 783 us (level)
  no operation moved by 1% of the time
where the time goes in v7:
time: 783 us; the launch traced here: 776 us
  Pallas kernels  491 us (63%)
  matrix products  130 us (17%)
  local copies, waits for them, and re-layouts  59.2 us (8%)
  other arithmetic  53 us (7%)
  waiting for transfers between devices  20.3 us (3%)
  starting transfers between devices  20 us (3%)
    pallas_call x1, Pallas kernels, gather_weights(): pl.pallas_call(functools.partial(gather_kernel, jobs, n, expand, reduce),...  264 us
    pallas_call x1, Pallas kernels, scatter_gradients(): pl.pallas_call(scatter_kernel, out_shape=[jax.ShapeDtypeStruct(maps.shape...  227 us
    dot_general x7, matrix products, pair_product(): lax.dot_general(rows, grads, (((0,), (0,)), ((), ())), preferred_element_...  41 us
    dot_general x1, matrix products, local(): jnp.dot(grad_reduced, full_reduce.T, preferred_element_type=jnp.float32)  24.4 us
    ppermute x22, waiting for transfers between devices, swap(): return lax.ppermute(value, axis, [(i, i ^ mask) for i in range(size)])  20.3 us
    dot_general x1, matrix products, local(): jnp.dot(grad_expanded, full_expand.T, preferred_element_type=jnp.float32)  18.3 us
  transfers between devices with their start and end apart: 24, of which 4 were waited for; matrix products, arithmetic and copies ran while one was open for 24% of the time, Pallas kernels for 0%

profile of v7, /device:TPU:0, one launch (start us, length us, event | category | flops | bytes accessed | tf_op | source)
XLA Modules:
  0.0 775.7 jit_solution(11789265002371966017)
XLA Ops:
  4.5 264.1 %shard_map.305 = (bf16[1024,1024]{1,0:T(8,128)(2,1)}, bf16[1536,6144]{1,0:T(8,128)(2,1)}, bf16[6144,1536]{1,0:T(8,128)(2,1)}, bf16[1024,4096]{1,0:T(8,128)(2,1)}...) custom-call(bf16[128,1024]{1,0:T(8,128)(2,1)} %refs_0_.1, ...), custom_call_target="tpu_custom_call" | custom-call | tf_op jit(solution)/shard_map/pallas_call | solution.py:356
  273.9 4.0 convolution_convert_fusion.5
  289.9 6.7 multiply_convert_fusion.1
  296.6 4.1 fusion.24
  322.7 3.2 convolution_convert_fusion.8
  326.7 4.1 all-to-all-start
  335.1 5.9 fusion.44
  343.1 3.9 reshape.479
  353.0 4.0 all-to-all-start.1
  357.7 3.2 convolution_convert_fusion.3
  368.5 3.4 convolution_convert_fusion.4
  375.4 4.0 convolution_convert_fusion.2
  396.8 3.8 broadcast_in_dim.102
  401.2 7.3 convolution_convert_fusion.1
  416.0 24.4 %fusion.7 = bf16[576,6144]{1,0:T(8,128)(2,1)} fusion(f32[576,6144]{1,0:T(8,128)} %get-tuple-element.76, bf16[576,1536]{1,0:T(8,128)(2,1)S(1)} %copy-done.32, bf16[6144,1536]{1,0:T(8,128)(2,1)} %get-tuple-element.75), kind=kOutput, calls=%fused_computation.9 | convolution fusion | flops 10942414848 | bytes 41877504 | tf_op jit(solution)/shard_map/dot_general | solution.py:1027
  442.3 4.5 broadcast_select_fusion.1
  446.8 18.3 %fusion.104 = f32[576,1536]{1,0:T(8,128)} fusion(bf16[576,6144]{1,0:T(8,128)(2,1)} %fusion.7, bf16[1536,6144]{1,0:T(8,128)(2,1)} %get-tuple-element.80), kind=kOutput, calls=%fused_computation.235 | convolution fusion | flops 10871635968 | bytes 29491200 | tf_op jit(solution)/shard_map/dot_general | solution.py:1033
  465.2 4.6 fusion.8.t1
  471.2 3.6 fusion.9.t0
  474.8 5.4 pad_maximum_fusion
  480.8 17.7 %collective-permute-done.18.land0a = bf16[2,2,2,192,384]{4,3,2,1,0:T(8,128)(2,1)} collective-permute-done((bf16[2,2,2,192,384]{4,3,2,1,0:T(8,128)(2,1)}, bf16[2,2,2,192,384]{4,3,2,1,0:T(8,128)(2,1)}, u32[]{:S(2)}, u32[]{:S(2)}) %collective-permute-start.18) | collective-permute-done | bytes 1179680 | tf_op jit(solution)/shard_map/ppermute | solution.py:750
  498.8 18.7 %convolution_convert_fusion = bf16[1536,3072]{1,0:T(8,128)(2,1)} fusion(bf16[1152,3072]{1,0:T(8,128)(2,1)} %pad_maximum_fusion, bf16[576,1536]{1,0:T(8,128)(2,1)} %collective-permute-done.12, bf16[576,1536]{1,0:T(8,128)(2,1)} %get-tuple-element.73), kind=kOutput, calls=%fused_computation.10 | convolution fusion | flops 10883432448 | bytes 20054016 | tf_op jit(solution)/shard_map/dot_general | solution.py:779
  523.7 226.7 %shard_map.306 = (f32[24,24,1536]{2,1,0:T(8,128)}, f32[64,1536]{1,0:T(8,128)}, bf16[4,128,1024]{2,1,0:T(8,128)(2,1)}, bf16[4,32,4096]{2,1,0:T(8,128)(2,1)}, bf16...) custom-call(bf16[4,2,2,2,192,768]{5,4,3,2,1,0:T(8,128)(2,1)} %bitcas, ...), custom_call_target="tpu_custom_call" | custom-call | tf_op jit(solution)/shard_map/pallas_call | solution.py:705
  768.2 3.2 bitcast_convert_fusion
  (270 shorter events, 124.5 us)
Async XLA Ops:
  286.6 61.8 %collective-permute-start.6 = (bf16[144,1024]{0,1:T(8,128)(2,1)}, bf16[144,1024]{0,1:T(8,128)(2,1)}, u32[]{:S(2)}, u32[]{:S(2)}) collective-permute-start(bf16[144,1024]{0,1:T(8,128)(2,1)} %bitcast.13), channel_id=1, source_target_pairs={{0,1},{1,0},{2,3},{3,2},{4,5},{5,4},{6,7},{7,6},{8,9},{9,8},{10,11... | collective-permute-start | bytes 884744 | tf_op jit(solution)/shard_map/ppermute | solution.py:750
  289.4 79.0 %collective-permute-start.2 = (bf16[144,1024]{1,0:T(8,128)(2,1)}, bf16[144,1024]{1,0:T(8,128)(2,1)}, u32[]{:S(2)}, u32[]{:S(2)}) collective-permute-start(bf16[144,1024]{1,0:T(8,128)(2,1)} %multiply_convert_fusion.4), channel_id=1, source_target_pairs={{0,1},{1,0},{2,3},{3,2},{4,5},{5,4},{6,7},{7,6},{8,9},{9,8},{10,11... | collective-permute-start | bytes 884744 | tf_op jit(solution)/shard_map/ppermute | solution.py:750
  326.7 24.0 %all-to-all-start = ((bf16[4,36,1536]{2,1,0:T(8,128)(2,1)}), bf16[4,36,1536]{2,1,0:T(8,128)(2,1)}, u32[]{:S(2)}, u32[]{:S(2)}) async-start(bf16[4,36,1536]{2,1,0:T(8,128)(2,1)} %reshape.471), calls=%async_computation | async-start | bytes 983040 | tf_op jit(solution)/shard_map/all_to_all | solution.py:990
  330.9 44.5 %collective-permute-start = (bf16[144,4096]{1,0:T(8,128)(2,1)}, bf16[144,4096]{1,0:T(8,128)(2,1)}, u32[]{:S(2)}, u32[]{:S(2)}) collective-permute-start(bf16[144,4096]{1,0:T(8,128)(2,1)} %get-tuple-element.181), channel_id=1, source_target_pairs={{0,1},{1,0},{2,3},{3,2},{4,5},{5,4},{6,7},{7,6},{8,9},{9,8},{10,11... | collective-permute-start | bytes 3538952 | tf_op jit(solution)/shard_map/ppermute | solution.py:750
  333.9 23.3 %collective-permute-start.5 = (bf16[144,1536]{1,0:T(8,128)(2,1)}, bf16[144,1536]{1,0:T(8,128)(2,1)}, u32[]{:S(2)}, u32[]{:S(2)}) collective-permute-start(bf16[144,1536]{1,0:T(8,128)(2,1)} %get-tuple-element.144), channel_id=1, source_target_pairs={{0,1},{1,0},{2,3},{3,2},{4,5},{5,4},{6,7},{7,6},{8,9},{9,8},{10,11... | collective-permute-start | bytes 1327112 | tf_op jit(solution)/shard_map/ppermute | solution.py:750
  334.8 13.2 %collective-permute-start.7 = (bf16[144,512]{1,0:T(8,128)(2,1)S(1)}, bf16[144,512]{1,0:T(8,128)(2,1)}, u32[]{:S(2)}, u32[]{:S(2)}) collective-permute-start(bf16[144,512]{1,0:T(8,128)(2,1)S(1)} %get-tuple-element.160), channel_id=1, source_target_pairs={{0,1},{1,0},{2,3},{3,2},{4,5},{5,4},{6,7},{7,6},{8,9},{9,8},{10,11... | collective-permute-start | bytes 442376 | tf_op jit(solution)/shard_map/ppermute | solution.py:750
  348.0 9.0 %collective-permute-start.4 = (bf16[144,1024]{1,0:T(8,128)(2,1)S(1)}, bf16[144,1024]{1,0:T(8,128)(2,1)}, u32[]{:S(2)}, u32[]{:S(2)}) collective-permute-start(bf16[144,1024]{1,0:T(8,128)(2,1)S(1)} %copy-done.23), channel_id=1, source_target_pairs={{0,1},{1,0},{2,3},{3,2},{4,5},{5,4},{6,7},{7,6},{8,9},{9,8},{10,11... | collective-permute-start | bytes 884744 | tf_op jit(solution)/shard_map/ppermute | solution.py:750
  348.3 12.7 %collective-permute-start.8 = (bf16[144,1536]{1,0:T(8,128)(2,1)}, bf16[144,1536]{1,0:T(8,128)(2,1)}, u32[]{:S(2)}, u32[]{:S(2)}) collective-permute-start(bf16[144,1536]{1,0:T(8,128)(2,1)} %get-tuple-element.63), channel_id=1, source_target_pairs={{0,1},{1,0},{2,3},{3,2},{4,5},{5,4},{6,7},{7,6},{8,9},{9,8},{10,11... | collective-permute-start | bytes 1327112 | tf_op jit(solution)/shard_map/ppermute | solution.py:750
  353.0 29.8 %all-to-all-start.1 = ((bf16[4,36,1536]{2,1,0:T(8,128)(2,1)}), bf16[4,36,1536]{2,1,0:T(8,128)(2,1)S(1)}, u32[]{:S(2)}, u32[]{:S(2)}) async-start(bf16[4,36,1536]{2,1,0:T(8,128)(2,1)} %copy.83), calls=%async_computation.1 | async-start | bytes 983040 | tf_op jit(solution)/shard_map/all_to_all | solution.py:994
  357.1 18.3 %collective-permute-start.1 = (bf16[144,512]{1,0:T(8,128)(2,1)S(1)}, bf16[144,512]{1,0:T(8,128)(2,1)S(1)}, u32[]{:S(2)}, u32[]{:S(2)}) collective-permute-start(bf16[144,512]{1,0:T(8,128)(2,1)S(1)} %get-tuple-element.164), channel_id=1, source_target_pairs={{0,1},{1,0},{2,3},{3,2},{4,5},{5,4},{6,7},{7,6},{8,9},{9,8},{10,11... | collective-permute-start | bytes 442376 | tf_op jit(solution)/shard_map/ppermute | solution.py:750
  357.2 3.6 collective-permute-start.9
  360.9 7.6 collective-permute-start.3
  361.0 40.1 %collective-permute-start.10 = (bf16[144,6144]{1,0:T(8,128)(2,1)}, bf16[144,6144]{1,0:T(8,128)(2,1)}, u32[]{:S(2)}, u32[]{:S(2)}) collective-permute-start(bf16[144,6144]{1,0:T(8,128)(2,1)} %reshape.479), channel_id=1, source_target_pairs={{0,1},{1,0},{2,3},{3,2},{4,5},{5,4},{6,7},{7,6},{8,9},{9,8},{10,11... | collective-permute-start | bytes 5308424 | tf_op jit(solution)/shard_map/ppermute | solution.py:750
  368.4 130.5 %collective-permute-start.12 = (bf16[576,1536]{1,0:T(8,128)(2,1)}, bf16[576,1536]{1,0:T(8,128)(2,1)}, u32[]{:S(2)}, u32[]{:S(2)}) collective-permute-start(bf16[576,1536]{1,0:T(8,128)(2,1)} %get-tuple-element.73), channel_id=1, source_target_pairs={{0,1},{1,0},{2,3},{3,2},{4,5},{5,4},{6,7},{7,6},{8,9},{9,8},{10,11... | collective-permute-start | bytes 5308424 | tf_op jit(solution)/shard_map/ppermute | solution.py:750
  390.3 10.2 %collective-permute-start.11 = (bf16[144,768]{1,0:T(8,128)(2,1)}, bf16[144,768]{1,0:T(8,128)(2,1)}, u32[]{:S(2)}, u32[]{:S(2)}) collective-permute-start(bf16[144,768]{1,0:T(8,128)(2,1)} %get-tuple-element.158), channel_id=1, source_target_pairs={{0,1},{1,0},{2,3},{3,2},{4,5},{5,4},{6,7},{7,6},{8,9},{9,8},{10,11... | collective-permute-start | bytes 663560 | tf_op jit(solution)/shard_map/ppermute | solution.py:750
  390.7 49.7 %collective-permute-start.13 = (bf16[4,2,2,128,512]{4,3,2,1,0:T(8,128)(2,1)}, bf16[4,2,2,128,512]{4,3,2,1,0:T(8,128)(2,1)}, u32[]{:S(2)}, u32[]{:S(2)}) collective-permute-start(bf16[4,2,2,128,512]{4,3,2,1,0:T(8,128)(2,1)} %dynamic-slice_bitcast_fusion.1), channel_id=1, source_target_pairs={{0,8},{8,0},{16,24},{24,16},{1,9},{9,1},{17,25},{25,17},{2,10},{10... | collective-permute-start | bytes 6291464 | tf_op jit(solution)/shard_map/ppermute | solution.py:750
  392.8 49.5 %collective-permute-start.14 = (bf16[4,2,2,32,2048]{4,3,2,1,0:T(8,128)(2,1)}, bf16[4,2,2,32,2048]{4,3,2,1,0:T(8,128)(2,1)}, u32[]{:S(2)}, u32[]{:S(2)}) collective-permute-start(bf16[4,2,2,32,2048]{4,3,2,1,0:T(8,128)(2,1)} %dynamic-slice_bitcast_fusion), channel_id=1, source_target_pairs={{0,16},{8,24},{16,0},{24,8},{1,17},{9,25},{17,1},{25,9},{2,18},{10... | collective-permute-start | bytes 6291464 | tf_op jit(solution)/shard_map/ppermute | solution.py:750
  400.6 80.2 %collective-permute-start.16 = (bf16[4,2,2,32,1536]{4,3,2,1,0:T(8,128)(2,1)}, bf16[4,2,2,32,1536]{4,3,2,1,0:T(8,128)(2,1)S(1)}, u32[]{:S(2)}, u32[]{:S(2)}) collective-permute-start(bf16[4,2,2,32,1536]{4,3,2,1,0:T(8,128)(2,1)} %dynamic-slice_bitcast_fusion.2), channel_id=1, source_target_pairs={{0,8},{8,0},{16,24},{24,16},{1,9},{9,1},{17,25},{25,17},{2,10},{10... | collective-permute-start | bytes 4718600 | tf_op jit(solution)/shard_map/ppermute | solution.py:750
  401.1 79.0 %collective-permute-start.17 = (bf16[4,2,2,80,512]{4,3,2,1,0:T(8,128)(2,1)}, bf16[4,2,2,80,512]{4,3,2,1,0:T(8,128)(2,1)S(1)}, u32[]{:S(2)}, u32[]{:S(2)}) collective-permute-start(bf16[4,2,2,80,512]{4,3,2,1,0:T(8,128)(2,1)} %dynamic-slice_bitcast_fusion.3), channel_id=1, source_target_pairs={{0,16},{8,24},{16,0},{24,8},{1,17},{9,25},{17,1},{25,9},{2,18},{10... | collective-permute-start | bytes 3932168 | tf_op jit(solution)/shard_map/ppermute | solution.py:750
  440.4 58.1 %collective-permute-start.18 = (bf16[2,2,2,192,384]{4,3,2,1,0:T(8,128)(2,1)}, bf16[2,2,2,192,384]{4,3,2,1,0:T(8,128)(2,1)}, u32[]{:S(2)}, u32[]{:S(2)}) collective-permute-start(bf16[2,2,2,192,384]{4,3,2,1,0:T(8,128)(2,1)} %get-tuple-element.83), channel_id=1, source_target_pairs={{0,8},{8,0},{16,24},{24,16},{1,9},{9,1},{17,25},{25,17},{2,10},{10... | collective-permute-start | bytes 3538952 | tf_op jit(solution)/shard_map/ppermute | solution.py:750
  446.8 22.9 %collective-permute-start.15 = (bf16[576,3072]{1,0:T(8,128)(2,1)}, bf16[576,3072]{1,0:T(8,128)(2,1)}, u32[]{:S(2)}, u32[]{:S(2)}) collective-permute-start(bf16[576,3072]{1,0:T(8,128)(2,1)} %get-tuple-element.138), channel_id=1, source_target_pairs={{0,1},{1,0},{2,3},{3,2},{4,5},{5,4},{6,7},{7,6},{8,9},{9,8},{10,11... | collective-permute-start | bytes 10616840 | tf_op jit(solution)/shard_map/ppermute | solution.py:750
  469.8 29.1 %collective-permute-start.19 = (bf16[2,2,2,192,384]{4,3,2,1,0:T(8,128)(2,1)}, bf16[2,2,2,192,384]{4,3,2,1,0:T(8,128)(2,1)}, u32[]{:S(2)}, u32[]{:S(2)}) collective-permute-start(bf16[2,2,2,192,384]{4,3,2,1,0:T(8,128)(2,1)} %get-tuple-element.84), channel_id=1, source_target_pairs={{0,16},{8,24},{16,0},{24,8},{1,17},{9,25},{17,1},{25,9},{2,18},{10... | collective-permute-start | bytes 3538952 | tf_op jit(solution)/shard_map/ppermute | solution.py:750
  480.2 43.1 %collective-permute-start.20 = (bf16[2,2,2,192,384]{4,3,2,1,0:T(8,128)(2,1)}, bf16[2,2,2,192,384]{4,3,2,1,0:T(8,128)(2,1)}, u32[]{:S(2)}, u32[]{:S(2)}) collective-permute-start(bf16[2,2,2,192,384]{4,3,2,1,0:T(8,128)(2,1)} %get-tuple-element.87), channel_id=1, source_target_pairs={{0,8},{8,0},{16,24},{24,16},{1,9},{9,1},{17,25},{25,17},{2,10},{10... | collective-permute-start | bytes 3538952 | tf_op jit(solution)/shard_map/ppermute | solution.py:750
  480.8 43.0 %collective-permute-start.21 = (bf16[2,2,2,192,384]{4,3,2,1,0:T(8,128)(2,1)}, bf16[2,2,2,192,384]{4,3,2,1,0:T(8,128)(2,1)}, u32[]{:S(2)}, u32[]{:S(2)}) collective-permute-start(bf16[2,2,2,192,384]{4,3,2,1,0:T(8,128)(2,1)} %get-tuple-element.89), channel_id=1, source_target_pairs={{0,16},{8,24},{16,0},{24,8},{1,17},{9,25},{17,1},{25,9},{2,18},{10... | collective-permute-start | bytes 3538952 | tf_op jit(solution)/shard_map/ppermute | solution.py:750
  (56 other events, 247.0 us)
